TPU v7x, 512 devices: a whole 4x8x8 slice. The times are simulated.
512 devices in a mesh: row: 16 (over x_hi, z), col: 32 (over x_lo, y, core).
Axes of the slice: x: 4 (x_hi: 2, x_lo: 2; x = x_hi * 2 + x_lo), y: 8, z: 8, core: 2. Of those that a mesh axis runs over, the one named last changes fastest.
Arguments:
- tokens: bfloat16 [512, 12288], P('col', 'row'), may hold values from -6 to 6
- expand: bfloat16 [12288, 24576], P('row', 'col'), may hold values from -0.0546875 to 0.0546875
- project: bfloat16 [24576, 12288], P('col', 'row'), may hold values from -0.0390625 to 0.0390625
- out_grad: bfloat16 [512, 12288], P('col', 'row'), may hold values from -6 to 6
Outputs:
- layer_out: bfloat16 [512, 12288], P('col', 'row')
- token_grad: bfloat16 [512, 12288], P('col', 'row')
- expand_grad: bfloat16 [12288, 24576], P('row', 'col')
- project_grad: bfloat16 [24576, 12288], P('col', 'row')
All inputs are finite; a program needn't handle non-finite values.
Results may differ from a plain program's by a relative error of at most 0.0049.
Values may be sent and summed in bfloat16 or wider, within the bound.
No kernel may reach another device: no remote copies, remote signals or barrier semaphores. Data moves between devices by JAX's collectives and lax.ppermute only.
A program may use at most 64 MiB of HBM per device.

v0:
```python
import math

import jax
import jax.numpy as jnp
from jax import lax
from jax.sharding import PartitionSpec as P

SLOPE_C = math.sqrt(2.0 / math.pi)
CUBIC = 0.044715


def gelu_tanh(value):
    inner = SLOPE_C * (value + CUBIC * value * value * value)
    return 0.5 * value * (1.0 + jnp.tanh(inner))


def gelu_slope(value):
    inner = SLOPE_C * (value + CUBIC * value * value * value)
    tanh_value = jnp.tanh(inner)
    return 0.5 * (1.0 + tanh_value) + 0.5 * value * (1.0 - tanh_value * tanh_value) * SLOPE_C * (
        1.0 + 3.0 * CUBIC * value * value
    )


def row_total(term):
    return lax.psum(term, "row")


def column_rows(panel, weight, contract):
    own_rows = panel.shape[0] // lax.axis_size("col")

    def term(start, count):
        return lax.dot_general(
            panel, weight, (contract, ((), ())), preferred_element_type=jnp.float32
        )

    return lax.psum_scatter(
        term(jnp.int32(0), lax.axis_size("col") * own_rows), "col", scatter_dimension=0, tiled=True
    )


def shards(tokens, expand, project, out_grad):
    tok_panel, cot_panel = (
        lax.all_gather(tokens, "col", axis=0, tiled=True),
        lax.all_gather(out_grad, "col", axis=0, tiled=True),
    )
    factor = 1.0 / math.sqrt(tok_panel.shape[0])
    pre_part = jnp.dot(tok_panel, expand, preferred_element_type=jnp.float32)
    back_part = lax.dot_general(
        cot_panel, project, (((1,), (1,)), ((), ())), preferred_element_type=jnp.float32
    )
    pre_act = row_total(pre_part)
    act_panel = gelu_tanh(pre_act).astype(jnp.bfloat16)
    back_total = row_total(back_part)
    grad_panel = (back_total * gelu_slope(pre_act)).astype(jnp.bfloat16)
    layer_out = column_rows(act_panel, project, ((1,), (0,))).astype(jnp.bfloat16)
    project_grad = (
        lax.dot_general(
            act_panel, cot_panel, (((0,), (0,)), ((), ())), preferred_element_type=jnp.float32
        )
        * factor
    ).astype(jnp.bfloat16)
    expand_grad = (
        lax.dot_general(
            tok_panel, grad_panel, (((0,), (0,)), ((), ())), preferred_element_type=jnp.float32
        )
        * factor
    ).astype(jnp.bfloat16)
    token_grad = column_rows(grad_panel, expand, ((1,), (1,))).astype(jnp.bfloat16)
    return (layer_out, token_grad, expand_grad, project_grad)


def solution(mesh):
    placed = (P("col", "row"), P("row", "col"), P("col", "row"), P("col", "row"))
    return jax.shard_map(
        shards,
        mesh=mesh,
        in_specs=placed,
        out_specs=(P("col", "row"), P("col", "row"), P("row", "col"), P("col", "row")),
        check_vma=False,
    )
```

profile of v0, /device:TPU:64, one launch (start us, length us, event | category | flops | bytes accessed | tf_op | source)
XLA Modules:
  0.0 503.5 jit_solution(7952533412155082272)
XLA Ops:
  7.2 0.0 copy-start
  7.2 0.0 all-reduce.3.cloned.1.call-start
  7.2 37.3 %all_gather.6 = bf16[512,768]{1,0:T(8,128)(2,1)S(1)} all-gather(bf16[16,768]{1,0:T(8,128)(2,1)} %param.4), channel_id=1, replica_groups=mesh['row'=16,'col'=32] {'col'}, dimensions={0}, use_global_device_ids=true | all-gather | bytes 811008 | tf_op jit(solution)/shard_map/all_gather | solution.py:44
  44.5 0.0 copy-start.2
  44.5 33.1 %all_gather.7 = bf16[512,768]{1,0:T(8,128)(2,1)S(1)} all-gather(bf16[16,768]{1,0:T(8,128)(2,1)} %param.7), channel_id=1, replica_groups=mesh['row'=16,'col'=32] {'col'}, dimensions={0}, use_global_device_ids=true | all-gather | bytes 811008 | tf_op jit(solution)/shard_map/all_gather | solution.py:45
  77.5 0.0 copy-done
  77.5 0.0 copy-start.4
  77.5 2.0 fusion.10
  79.5 0.0 copy-done.2
  79.5 0.0 copy-done.4
  79.5 1.9 fusion.9
  81.5 0.0 all-reduce.3.cloned.1.call-update
  81.5 0.0 reduce-scatter.3.cloned.1.call-start
  81.5 172.9 %all-reduce.3.cloned.1.call-done = (f32[512,768]{1,0:T(8,128)}, f32[512,768]{1,0:T(8,128)}) async-done(((f32[512,768]{1,0:T(8,128)}, f32[512,768]{1,0:T(8,128)}), (f32[512,768]{1,0:T(8,128)}, f32[512,768]{1,0:T(8,128)})) %all-reduce.3.cloned.1.call-update) | async-done | bytes 3145744 | tf_op jit(solution)/shard_map/psum | solution.py:26
  254.4 3.6 fusion.8
  258.0 0.0 copy-start.1
  258.0 0.0 reduce-scatter.3.cloned.1.call-update
  258.1 0.0 reduce-scatter.5.cloned.1.call-start
  258.1 1.3 copy-done.1
  259.4 0.0 copy-start.5
  259.4 2.5 fusion.6
  261.9 0.0 copy-start.3
  262.0 0.9 copy-done.3
  262.8 0.0 copy-done.5
  262.8 2.0 fusion.11
  264.8 0.0 reduce-scatter.5.cloned.1.call-update
  264.8 3.2 fusion.7
  268.0 2.4 copy.8
  270.4 2.0 multiply_convert_fusion
  272.4 104.0 %reduce-scatter.3.cloned.1.call-done = f32[16,768]{1,0:T(8,128)} async-done(((f32[512,768]{1,0:T(8,128)}), f32[16,768]{1,0:T(8,128)}) %reduce-scatter.3.cloned.1.call-update) | async-done | bytes 49168 | tf_op jit(solution)/shard_map/reduce_scatter | solution.py:37
  376.4 1.4 convert_element_type.22
  377.8 117.8 %reduce-scatter.5.cloned.1.call-done = f32[16,768]{1,0:T(8,128)} async-done(((f32[512,768]{1,0:T(8,128)}), f32[16,768]{1,0:T(8,128)}) %reduce-scatter.5.cloned.1.call-update) | async-done | bytes 49168 | tf_op jit(solution)/shard_map/reduce_scatter | solution.py:37
  495.6 1.4 convert_element_type.24
Async XLA Ops:
  7.2 70.4 %copy-start = (bf16[768,768]{1,0:T(8,128)(2,1)S(1)}, bf16[768,768]{1,0:T(8,128)(2,1)}, u32[]{:S(2)}) copy-start(bf16[768,768]{1,0:T(8,128)(2,1)} %param.6) | copy-start | bytes 3538948
  7.2 247.2 %all-reduce.3.cloned.1.call-start = ((), (), s32[]{:S(2)}) async-start(), calls=%async_computation.4 | async-start | bytes 6291456 | tf_op jit(solution)/shard_map/psum | solution.py:26
  44.5 35.0 %copy-start.2 = (bf16[512,768]{1,0:T(8,128)(2,1)}, bf16[512,768]{1,0:T(8,128)(2,1)S(1)}, u32[]{:S(2)}) copy-start(bf16[512,768]{1,0:T(8,128)(2,1)S(1)} %all_gather.6) | copy-start | bytes 2359300
  77.5 2.0 copy-start.4
  81.5 294.9 %reduce-scatter.3.cloned.1.call-start = ((), (), s32[]{:S(2)}) async-start(), calls=%async_computation.2 | async-start | bytes 1622016 | tf_op jit(solution)/shard_map/reduce_scatter | solution.py:37
  258.0 1.4 copy-start.1
  258.1 237.5 %reduce-scatter.5.cloned.1.call-start = ((), (), s32[]{:S(2)}) async-start(), calls=%async_computation.3 | async-start | bytes 1622016 | tf_op jit(solution)/shard_map/reduce_scatter | solution.py:37
  259.4 3.4 copy-start.5
  261.9 0.9 copy-start.3
Sparse Core Ops, SparseCore 0:
  81.6 172.7 all-reduce.2
  258.2 118.1 reduce-scatter.2
  379.4 116.0 reduce-scatter.4
where the time goes:
time: 504 us
  waiting for transfers between devices  395 us (78%)
  blocking collectives  70.3 us (14%)
  matrix products  14.7 us (3%)
  between operations  13.8 us (3%)
  other arithmetic  5.32 us (1%)
    reduce_scatter x2, waiting for transfers between devices, column_rows(): lax.psum_scatter(term(jnp.int32(0), lax.axis_size('col') * own_rows), 'co...  222 us
    psum x1, waiting for transfers between devices, row_total(): return lax.psum(term, 'row')  173 us
    all_gather x1, blocking collectives, shards(): lax.all_gather(tokens, 'col', axis=0, tiled=True)  37.3 us
    all_gather x1, blocking collectives, shards(): lax.all_gather(out_grad, 'col', axis=0, tiled=True)  33.1 us
  transfers between devices with their start and end apart: 3, of which 3 were waited for; matrix products, arithmetic and copies ran while one was open for 3% of the time, Pallas kernels for 0%

commit v1 on v0

v1 whole, which is shorter than its diff:
```python
import math

import jax
import jax.numpy as jnp
from jax import lax
from jax.sharding import PartitionSpec as P

SLOPE_C = math.sqrt(2.0 / math.pi)
CUBIC = 0.044715
CORES = 2


def gelu_and_slope(value):
    inner = SLOPE_C * (value + CUBIC * value * value * value)
    tanh_value = jnp.tanh(inner)
    gelu = 0.5 * value * (1.0 + tanh_value)
    slope = 0.5 * (1.0 + tanh_value) + 0.5 * value * (1.0 - tanh_value * tanh_value) * SLOPE_C * (
        1.0 + 3.0 * CUBIC * value * value
    )
    return gelu, slope


def same_core_groups(cols):
    return [list(range(core, cols, CORES)) for core in range(CORES)]


def swap_cores(block):
    cols = lax.axis_size("col")
    return lax.ppermute(block, "col", [(at, at ^ 1) for at in range(cols)])


def spread(block, members, axis, groups):
    copies = jnp.broadcast_to(block[None], (members, *block.shape))
    return lax.all_to_all(copies, axis, 0, 0, axis_index_groups=groups)


def exchange(parts, axis, groups):
    return jnp.sum(
        lax.all_to_all(parts, axis, 0, 0, axis_index_groups=groups).astype(jnp.float32), axis=0
    )


def matmul(left, right, contract):
    return lax.dot_general(left, right, (contract, ((), ())), preferred_element_type=jnp.float32)


def shards(tokens, expand, project, out_grad):
    rows, cols = lax.axis_size("row"), lax.axis_size("col")
    chips = cols // CORES
    own = tokens.shape[0]
    hidden = expand.shape[1]
    features = tokens.shape[1]
    groups = same_core_groups(cols)
    factor = 1.0 / math.sqrt(own * cols)

    expand_two = jnp.concatenate([expand, swap_cores(expand)], axis=1)
    project_two = jnp.concatenate([project, swap_cores(project)], axis=0)
    panels = spread(jnp.concatenate([tokens, out_grad], axis=0), chips, "col", groups)
    half = chips * own
    tok_panel = panels[:, :own].reshape(half, features)
    cot_panel = panels[:, own:].reshape(half, features)
    tok_other, cot_other = swap_cores(tok_panel), swap_cores(cot_panel)

    pre_part = matmul(tok_panel, expand_two, ((1,), (0,))).astype(jnp.bfloat16)
    back_part = matmul(cot_panel, project_two, ((1,), (1,))).astype(jnp.bfloat16)
    share = half // rows
    sums = exchange(
        jnp.concatenate(
            [
                pre_part.reshape(rows, share, CORES * hidden),
                back_part.reshape(rows, share, CORES * hidden),
            ],
            axis=1,
        ),
        "row",
        None,
    )
    gelu, slope = gelu_and_slope(sums[:share])
    act = gelu.astype(jnp.bfloat16)
    grad = (sums[share:] * slope).astype(jnp.bfloat16)
    hiddens = spread(jnp.concatenate([act, grad], axis=0), rows, "row", None)
    act_panel = hiddens[:, :share].reshape(half, CORES * hidden)
    grad_panel = hiddens[:, share:].reshape(half, CORES * hidden)

    out_part = matmul(act_panel, project_two, ((1,), (0,))).astype(jnp.bfloat16)
    tok_part = matmul(grad_panel, expand_two, ((1,), (1,))).astype(jnp.bfloat16)
    outs = exchange(
        jnp.concatenate(
            [out_part.reshape(chips, own, features), tok_part.reshape(chips, own, features)], axis=1
        ),
        "col",
        groups,
    ).astype(jnp.bfloat16)

    act_other = swap_cores(act_panel[:, hidden:])
    grad_other = swap_cores(grad_panel[:, hidden:])
    project_grad = matmul(
        jnp.concatenate([act_panel[:, :hidden], act_other], axis=0),
        jnp.concatenate([cot_panel, cot_other], axis=0),
        ((0,), (0,)),
    )
    expand_grad = matmul(
        jnp.concatenate([tok_panel, tok_other], axis=0),
        jnp.concatenate([grad_panel[:, :hidden], grad_other], axis=0),
        ((0,), (0,)),
    )
    return (
        outs[:own],
        outs[own:],
        (expand_grad * factor).astype(jnp.bfloat16),
        (project_grad * factor).astype(jnp.bfloat16),
    )


def solution(mesh):
    placed = (P("col", "row"), P("row", "col"), P("col", "row"), P("col", "row"))
    return jax.shard_map(
        shards,
        mesh=mesh,
        in_specs=placed,
        out_specs=(P("col", "row"), P("col", "row"), P("row", "col"), P("col", "row")),
        check_vma=False,
    )
```

time: 504 us -> 162 us (0.32)
  waiting for transfers between devices: 395 us -> 21 us
  starting transfers between devices: 0.12 us -> 28.1 us
  blocking collectives: 70.3 us -> 91.9 us
  between operations: 13.8 us -> 0.91 us
    reduce_scatter x2 -> x0, waiting for transfers between devices: 222 us -> none  [column_rows(): lax.psum_scatter(term(jnp.int32(0), lax.axis_size('col') * own_rows), 'co...]
    psum x1 -> x0, waiting for transfers between devices: 173 us -> none  [row_total(): return lax.psum(term, 'row')]
    all_to_all x0 -> x2, blocking collectives: none -> 91.9 us  [the longest x1 49.1 us: exchange(): lax.all_to_all(parts, axis, 0, 0, axis_index_groups=groups)]
    all_gather x2 -> x0, blocking collectives: 70.3 us -> none  [the longest x1 37.3 us: shards(): lax.all_gather(tokens, 'col', axis=0, tiled=True)]
    all_to_all x0 -> x2, waiting for transfers between devices: none -> 19.8 us  [the longest x1 12.9 us: spread(): return lax.all_to_all(copies, axis, 0, 0, axis_index_groups=groups)]
    all_to_all x0 -> x2, starting transfers between devices: none -> 15.1 us  [the longest x1 8.13 us: spread(): return lax.all_to_all(copies, axis, 0, 0, axis_index_groups=groups)]
    ppermute x0 -> x6, starting transfers between devices: none -> 13 us  [swap_cores(): return lax.ppermute(block, 'col', [(at, at ^ 1) for at in range(cols)])]
    convert_element_type x3 -> x1, other arithmetic: 5.32 us -> 0.08 us  [shards(): act = gelu.astype(jnp.bfloat16)]
  transfers between devices with their start and end apart: 3 -> 8, of which waited for: 3 -> 3; matrix products, arithmetic and copies ran while one was open for 3% -> 4% of each run, Pallas kernels for 0% -> 0%
where the time goes in v1:
time: 162 us; the launch traced here: 161 us
  blocking collectives  91.9 us (57%)
  starting transfers between devices  28.1 us (17%)
  waiting for transfers between devices  21 us (13%)
  matrix products  12.1 us (7%)
  local copies, waits for them, and re-layouts  4.75 us (3%)
  other arithmetic  2.45 us (2%)
    all_to_all x1, blocking collectives, exchange(): lax.all_to_all(parts, axis, 0, 0, axis_index_groups=groups)  49.1 us
    all_to_all x1, blocking collectives, spread(): return lax.all_to_all(copies, axis, 0, 0, axis_index_groups=groups)  42.8 us
    ppermute x6, starting transfers between devices, swap_cores(): return lax.ppermute(block, 'col', [(at, at ^ 1) for at in range(cols)])  13 us
    all_to_all x1, waiting for transfers between devices, spread(): return lax.all_to_all(copies, axis, 0, 0, axis_index_groups=groups)  12.9 us
    dot_general x6, matrix products, matmul(): lax.dot_general(left, right, (contract, ((), ())), preferred_element_type...  12.1 us
    all_to_all x1, starting transfers between devices, spread(): return lax.all_to_all(copies, axis, 0, 0, axis_index_groups=groups)  8.13 us
    all_to_all x1, starting transfers between devices, exchange(): lax.all_to_all(parts, axis, 0, 0, axis_index_groups=groups)  7 us
    all_to_all x1, waiting for transfers between devices, exchange(): lax.all_to_all(parts, axis, 0, 0, axis_index_groups=groups)  6.93 us
  transfers between devices with their start and end apart: 8, of which 3 were waited for; matrix products, arithmetic and copies ran while one was open for 4% of the time, Pallas kernels for 0%

profile of v1, /device:TPU:64, one launch (start us, length us, event | category | flops | bytes accessed | tf_op | source)
XLA Modules:
  0.0 161.2 jit_solution(4512305259268259269)
XLA Ops:
  0.6 0.0 copy-start
  0.6 0.0 copy-start.1
  0.7 0.9 pad_maximum_fusion.3
  1.6 1.0 broadcast_in_dim.4
  2.5 8.1 %all-to-all-start = ((bf16[16,32,768]{2,1,0:T(8,128)(2,1)}), bf16[16,32,768]{2,1,0:T(8,128)(2,1)S(1)}, u32[]{:S(2)}, u32[]{:S(2)}) async-start(bf16[16,32,768]{2,1,0:T(8,128)(2,1)} %broadcast_in_dim.4), calls=%async_computation | async-start | bytes 1572864 | tf_op jit(solution)/shard_map/all_to_all | solution.py:34
  10.7 0.0 copy-done
  10.7 1.9 %collective-permute-start.1 = (bf16[768,768]{1,0:T(8,128)(2,1)S(1)}, bf16[768,768]{1,0:T(8,128)(2,1)S(1)}, u32[]{:S(2)}, u32[]{:S(2)}) collective-permute-start(bf16[768,768]{1,0:T(8,128)(2,1)S(1)} %copy-done), channel_id=1, source_target_pairs={{0,1},{1,0},{2,3},{3,2},{4,5},{5,4},{6,7},{7,6},{8,9},{9,8},{10,11... | collective-permute-start | bytes 3538952 | tf_op jit(solution)/shard_map/ppermute | solution.py:29
  12.6 0.0 copy-done.1
  12.6 2.4 %collective-permute-start = (bf16[768,768]{1,0:T(8,128)(2,1)S(1)}, bf16[768,768]{1,0:T(8,128)(2,1)S(1)}, u32[]{:S(2)}, u32[]{:S(2)}) collective-permute-start(bf16[768,768]{1,0:T(8,128)(2,1)S(1)} %copy-done.1), channel_id=1, source_target_pairs={{0,1},{1,0},{2,3},{3,2},{4,5},{5,4},{6,7},{7,6},{8,9},{9,8},{10,11... | collective-permute-start | bytes 3538952 | tf_op jit(solution)/shard_map/ppermute | solution.py:29
  15.0 0.1 constant_dynamic-update-slice_fusion.3
  15.1 1.1 constant_dynamic-update-slice_fusion.1
  16.2 0.0 collective-permute-done.1
  16.2 0.1 constant_dynamic-update-slice_fusion.2
  16.3 0.0 copy-start.2
  16.3 1.2 collective-permute-done
  17.5 0.3 copy-done.2
  17.8 1.2 constant_dynamic-update-slice_fusion
  18.9 12.9 %all-to-all-done = bf16[16,32,768]{2,1,0:T(8,128)(2,1)S(1)} async-done(((bf16[16,32,768]{2,1,0:T(8,128)(2,1)}), bf16[16,32,768]{2,1,0:T(8,128)(2,1)S(1)}, u32[]{:S(2)}, u32[]{:S(2)}) %all-to-all-start) | async-done | bytes 786464 | tf_op jit(solution)/shard_map/all_to_all | solution.py:34
  31.8 0.1 fusion.24
  31.9 0.0 copy-start.4
  31.9 2.6 %convolution_convert_fusion = bf16[256,1536]{1,0:T(8,128)(2,1)S(1)} fusion(bf16[256,768]{1,0:T(8,128)(2,1)S(1)} %bitcast.22, bf16[1536,768]{1,0:T(8,128)(2,1)} %copy-done.2), kind=kOutput, calls=%fused_computation.1 | convolution fusion | flops 604372992 | bytes 3538944 | tf_op jit(solution)/shard_map/dot_general | solution.py:44
  34.5 0.0 copy-done.4
  34.5 2.4 %convolution_convert_fusion.1 = bf16[256,1536]{1,0:T(8,128)(2,1)S(1)} fusion(bf16[256,768]{1,0:T(8,128)(2,1)S(1)} %bitcast.25, bf16[768,1536]{1,0:T(8,128)(2,1)} %constant_dynamic-update-slice_fusion), kind=kOutput, calls=%fused_computation.2 | convolution fusion | flops 604372992 | bytes 3538944 | tf_op jit(solution)/shard_map/dot_general | solution.py:44
  36.9 0.1 pad_maximum_fusion
  37.1 49.1 %all_to_all.20 = bf16[16,32,1536]{2,1,0:T(8,128)(2,1)S(1)} all-to-all(bf16[16,32,1536]{2,1,0:T(8,128)(2,1)S(1)} %pad_maximum_fusion), channel_id=1, replica_groups=mesh['row'=16,'col'=32] {'row'}, dimensions={0} | all-to-all | bytes 3145728 | tf_op jit(solution)/shard_map/all_to_all | solution.py:39
  86.2 0.2 convert_reduce_fusion
  86.4 0.1 multiply_convert_fusion.2
  86.5 0.1 broadcast_in_dim.5
  86.7 42.8 %all_to_all.21 = bf16[16,32,1536]{2,1,0:T(8,128)(2,1)S(1)} all-to-all(bf16[16,32,1536]{2,1,0:T(8,128)(2,1)S(1)} %broadcast_in_dim.5), channel_id=1, replica_groups=mesh['row'=16,'col'=32] {'row'}, dimensions={0} | all-to-all | bytes 3145728 | tf_op jit(solution)/shard_map/all_to_all | solution.py:34
  129.4 0.1 fusion.21
  129.6 0.0 copy-start.3
  129.6 2.6 %convolution_convert_fusion.2 = bf16[256,768]{1,0:T(8,128)(2,1)S(1)} fusion(bf16[256,1536]{1,0:T(8,128)(2,1)S(1)} %bitcast.18, bf16[768,1536]{1,0:T(8,128)(2,1)} %constant_dynamic-update-slice_fusion), kind=kOutput, calls=%fused_computation.6 | convolution fusion | flops 604176384 | bytes 3538944 | tf_op jit(solution)/shard_map/dot_general | solution.py:44
  132.2 0.0 copy-done.3
  132.2 0.8 convolution_convert_fusion.3
  133.0 0.0 copy-start.5
  133.0 1.0 pad_maximum_fusion.1
  134.0 7.0 %all-to-all-start.3 = ((bf16[16,32,768]{2,1,0:T(8,128)(2,1)}), bf16[16,32,768]{2,1,0:T(8,128)(2,1)S(1)}, u32[]{:S(2)}, u32[]{:S(2)}) async-start(bf16[16,32,768]{2,1,0:T(8,128)(2,1)} %pad_maximum_fusion.1), calls=%async_computation.3 | async-start | bytes 1572864 | tf_op jit(solution)/shard_map/all_to_all | solution.py:39
  141.0 0.0 copy-done.5
  141.0 1.9 %collective-permute-start.2 = (bf16[256,768]{1,0:T(8,128)(2,1)S(1)}, bf16[256,768]{1,0:T(8,128)(2,1)S(1)}, u32[]{:S(2)}, u32[]{:S(2)}) collective-permute-start(bf16[256,768]{1,0:T(8,128)(2,1)S(1)} %bitcast.26), channel_id=1, source_target_pairs={{0,1},{1,0},{2,3},{3,2},{4,5},{5,4},{6,7},{7,6},{8,9},{9,8},{10,11... | collective-permute-start | bytes 1179656 | tf_op jit(solution)/shard_map/ppermute | solution.py:29
  142.9 2.4 %collective-permute-start.5 = (bf16[256,768]{1,0:T(8,128)(2,1)S(1)}, bf16[256,768]{1,0:T(8,128)(2,1)S(1)}, u32[]{:S(2)}, u32[]{:S(2)}) collective-permute-start(bf16[256,768]{1,0:T(8,128)(2,1)S(1)} %bitcast.23), channel_id=1, source_target_pairs={{0,1},{1,0},{2,3},{3,2},{4,5},{5,4},{6,7},{7,6},{8,9},{9,8},{10,11... | collective-permute-start | bytes 1179656 | tf_op jit(solution)/shard_map/ppermute | solution.py:29
  145.3 0.1 fusion.23
  145.4 1.9 %collective-permute-start.3 = (bf16[256,768]{1,0:T(8,128)(2,1)S(1)}, bf16[256,768]{1,0:T(8,128)(2,1)S(1)}, u32[]{:S(2)}, u32[]{:S(2)}) collective-permute-start(bf16[256,768]{1,0:T(8,128)(2,1)S(1)} %get-tuple-element.9), channel_id=1, source_target_pairs={{0,1},{1,0},{2,3},{3,2},{4,5},{5,4},{6,7},{7,6},{8,9},{9,8},{10,11... | collective-permute-start | bytes 1179656 | tf_op jit(solution)/shard_map/ppermute | solution.py:29
  147.3 0.1 fusion.22
  147.4 2.4 %collective-permute-start.4 = (bf16[256,768]{1,0:T(8,128)(2,1)S(1)}, bf16[256,768]{1,0:T(8,128)(2,1)S(1)}, u32[]{:S(2)}, u32[]{:S(2)}) collective-permute-start(bf16[256,768]{1,0:T(8,128)(2,1)S(1)} %get-tuple-element.7), channel_id=1, source_target_pairs={{0,1},{1,0},{2,3},{3,2},{4,5},{5,4},{6,7},{7,6},{8,9},{9,8},{10,11... | collective-permute-start | bytes 1179656 | tf_op jit(solution)/shard_map/ppermute | solution.py:29
  149.8 0.0 collective-permute-done.2
  149.8 0.0 collective-permute-done.3
  149.8 1.8 %multiply_convert_fusion.1 = bf16[768,768]{1,0:T(8,128)(2,1)} fusion(bf16[256,768]{1,0:T(8,128)(2,1)S(1)} %collective-permute-done.2, bf16[256,768]{1,0:T(8,128)(2,1)S(1)} %bitcast.27, bf16[256,768]{1,0:T(8,128)(2,1)S(1)} %collective-permute-done.3, bf16[256,768]{1,0:T(8,128)(2,1)S(1)} %get-tuple-element.8), kind=kOutput, calls=%fused_computation.4 | convolution fusion | flops 608305152 | bytes 2752512 | tf_op jit(solution)/shard_map/dot_general | solution.py:44
  151.7 0.0 collective-permute-done.5
  151.7 0.0 collective-permute-done.4
  151.7 1.8 %multiply_convert_fusion = bf16[768,768]{1,0:T(8,128)(2,1)} fusion(bf16[256,768]{1,0:T(8,128)(2,1)S(1)} %collective-permute-done.4, bf16[256,768]{1,0:T(8,128)(2,1)S(1)} %get-tuple-element.6, bf16[256,768]{1,0:T(8,128)(2,1)S(1)} %collective-permute-done.5, bf16[256,768]{1,0:T(8,128)(2,1)S(1)} %bitcast.24), kind=kOutput, calls=%fused_computation.3 | convolution fusion | flops 608305152 | bytes 2752512 | tf_op jit(solution)/shard_map/dot_general | solution.py:44
  153.5 6.9 %all-to-all-done.3 = bf16[16,32,768]{2,1,0:T(8,128)(2,1)S(1)} async-done(((bf16[16,32,768]{2,1,0:T(8,128)(2,1)}), bf16[16,32,768]{2,1,0:T(8,128)(2,1)S(1)}, u32[]{:S(2)}, u32[]{:S(2)}) %all-to-all-start.3) | async-done | bytes 786464 | tf_op jit(solution)/shard_map/all_to_all | solution.py:39
  160.4 0.1 reduce_sum.22
  160.5 0.6 fusion.25
  (1 shorter events, 0.0 us)
Async XLA Ops:
  0.6 10.0 %copy-start = (bf16[768,768]{1,0:T(8,128)(2,1)S(1)}, bf16[768,768]{1,0:T(8,128)(2,1)}, u32[]{:S(2)}) copy-start(bf16[768,768]{1,0:T(8,128)(2,1)} %param.6) | copy-start | bytes 3538948
  0.6 12.0 %copy-start.1 = (bf16[768,768]{1,0:T(8,128)(2,1)S(1)}, bf16[768,768]{1,0:T(8,128)(2,1)}, u32[]{:S(2)}) copy-start(bf16[768,768]{1,0:T(8,128)(2,1)} %param.5) | copy-start | bytes 3538948
  2.5 29.3 %all-to-all-start = ((bf16[16,32,768]{2,1,0:T(8,128)(2,1)}), bf16[16,32,768]{2,1,0:T(8,128)(2,1)S(1)}, u32[]{:S(2)}, u32[]{:S(2)}) async-start(bf16[16,32,768]{2,1,0:T(8,128)(2,1)} %broadcast_in_dim.4), calls=%async_computation | async-start | bytes 1572864 | tf_op jit(solution)/shard_map/all_to_all | solution.py:34
  10.7 5.6 %collective-permute-start.1 = (bf16[768,768]{1,0:T(8,128)(2,1)S(1)}, bf16[768,768]{1,0:T(8,128)(2,1)S(1)}, u32[]{:S(2)}, u32[]{:S(2)}) collective-permute-start(bf16[768,768]{1,0:T(8,128)(2,1)S(1)} %copy-done), channel_id=1, source_target_pairs={{0,1},{1,0},{2,3},{3,2},{4,5},{5,4},{6,7},{7,6},{8,9},{9,8},{10,11... | collective-permute-start | bytes 3538952 | tf_op jit(solution)/shard_map/ppermute | solution.py:29
  12.6 4.9 %collective-permute-start = (bf16[768,768]{1,0:T(8,128)(2,1)S(1)}, bf16[768,768]{1,0:T(8,128)(2,1)S(1)}, u32[]{:S(2)}, u32[]{:S(2)}) collective-permute-start(bf16[768,768]{1,0:T(8,128)(2,1)S(1)} %copy-done.1), channel_id=1, source_target_pairs={{0,1},{1,0},{2,3},{3,2},{4,5},{5,4},{6,7},{7,6},{8,9},{9,8},{10,11... | collective-permute-start | bytes 3538952 | tf_op jit(solution)/shard_map/ppermute | solution.py:29
  16.3 1.4 copy-start.2
  31.9 2.6 %copy-start.4 = (bf16[16,16,768]{2,1,0:T(8,128)(2,1)}, bf16[16,16,768]{2,1,0:T(8,128)(2,1)S(1)}, u32[]{:S(2)}) copy-start(bf16[16,16,768]{2,1,0:T(8,128)(2,1)S(1)} %get-tuple-element.10) | copy-start | bytes 1179652
  129.6 2.6 %copy-start.3 = (bf16[1536,768]{1,0:T(8,128)(2,1)S(1)}, bf16[1536,768]{1,0:T(8,128)(2,1)}, u32[]{:S(2)}) copy-start(bf16[1536,768]{1,0:T(8,128)(2,1)} %copy-done.2) | copy-start | bytes 7077892
  133.0 8.0 %copy-start.5 = (bf16[16,16,768]{2,1,0:T(8,128)(2,1)S(1)}, bf16[16,16,768]{2,1,0:T(8,128)(2,1)}, u32[]{:S(2)}) copy-start(bf16[16,16,768]{2,1,0:T(8,128)(2,1)} %copy-done.4) | copy-start | bytes 1179652
  134.0 26.4 %all-to-all-start.3 = ((bf16[16,32,768]{2,1,0:T(8,128)(2,1)}), bf16[16,32,768]{2,1,0:T(8,128)(2,1)S(1)}, u32[]{:S(2)}, u32[]{:S(2)}) async-start(bf16[16,32,768]{2,1,0:T(8,128)(2,1)} %pad_maximum_fusion.1), calls=%async_computation.3 | async-start | bytes 1572864 | tf_op jit(solution)/shard_map/all_to_all | solution.py:39
  141.0 8.8 %collective-permute-start.2 = (bf16[256,768]{1,0:T(8,128)(2,1)S(1)}, bf16[256,768]{1,0:T(8,128)(2,1)S(1)}, u32[]{:S(2)}, u32[]{:S(2)}) collective-permute-start(bf16[256,768]{1,0:T(8,128)(2,1)S(1)} %bitcast.26), channel_id=1, source_target_pairs={{0,1},{1,0},{2,3},{3,2},{4,5},{5,4},{6,7},{7,6},{8,9},{9,8},{10,11... | collective-permute-start | bytes 1179656 | tf_op jit(solution)/shard_map/ppermute | solution.py:29
  142.9 8.7 %collective-permute-start.5 = (bf16[256,768]{1,0:T(8,128)(2,1)S(1)}, bf16[256,768]{1,0:T(8,128)(2,1)S(1)}, u32[]{:S(2)}, u32[]{:S(2)}) collective-permute-start(bf16[256,768]{1,0:T(8,128)(2,1)S(1)} %bitcast.23), channel_id=1, source_target_pairs={{0,1},{1,0},{2,3},{3,2},{4,5},{5,4},{6,7},{7,6},{8,9},{9,8},{10,11... | collective-permute-start | bytes 1179656 | tf_op jit(solution)/shard_map/ppermute | solution.py:29
  145.4 4.4 %collective-permute-start.3 = (bf16[256,768]{1,0:T(8,128)(2,1)S(1)}, bf16[256,768]{1,0:T(8,128)(2,1)S(1)}, u32[]{:S(2)}, u32[]{:S(2)}) collective-permute-start(bf16[256,768]{1,0:T(8,128)(2,1)S(1)} %get-tuple-element.9), channel_id=1, source_target_pairs={{0,1},{1,0},{2,3},{3,2},{4,5},{5,4},{6,7},{7,6},{8,9},{9,8},{10,11... | collective-permute-start | bytes 1179656 | tf_op jit(solution)/shard_map/ppermute | solution.py:29
  147.4 4.3 %collective-permute-start.4 = (bf16[256,768]{1,0:T(8,128)(2,1)S(1)}, bf16[256,768]{1,0:T(8,128)(2,1)S(1)}, u32[]{:S(2)}, u32[]{:S(2)}) collective-permute-start(bf16[256,768]{1,0:T(8,128)(2,1)S(1)} %get-tuple-element.7), channel_id=1, source_target_pairs={{0,1},{1,0},{2,3},{3,2},{4,5},{5,4},{6,7},{7,6},{8,9},{9,8},{10,11... | collective-permute-start | bytes 1179656 | tf_op jit(solution)/shard_map/ppermute | solution.py:29

commit v2 on v1

v2 whole, which is shorter than its diff:
```python
import math

import jax
import jax.numpy as jnp
from jax import lax
from jax.sharding import PartitionSpec as P

SLOPE_C = math.sqrt(2.0 / math.pi)
CUBIC = 0.044715
CORES = 2
PAIR = 2


def gelu_and_slope(value):
    inner = SLOPE_C * (value + CUBIC * value * value * value)
    tanh_value = jnp.tanh(inner)
    gelu = 0.5 * value * (1.0 + tanh_value)
    slope = 0.5 * (1.0 + tanh_value) + 0.5 * value * (1.0 - tanh_value * tanh_value) * SLOPE_C * (
        1.0 + 3.0 * CUBIC * value * value
    )
    return gelu, slope


def col_groups(rows, cols):
    chips = cols // CORES
    groups = []
    for row in range(rows):
        mine = row // (rows // PAIR)
        for core in range(CORES):
            order = [half * (chips // PAIR) + at for half in (mine, 1 - mine) for at in range(chips // PAIR)]
            groups.append([row * cols + chip * CORES + core for chip in order])
    return groups


def half_row_groups(rows):
    size = rows // PAIR
    return [list(range(half * size, (half + 1) * size)) for half in range(PAIR)]


def swap_cores(block):
    cols = lax.axis_size("col")
    return lax.ppermute(block, "col", [(at, at ^ 1) for at in range(cols)])


def swap_halves(block):
    rows = lax.axis_size("row")
    return lax.ppermute(block, "row", [(at, (at + rows // PAIR) % rows) for at in range(rows)])


def exchange(parts, axis, groups):
    return lax.all_to_all(parts, axis, 0, 0, axis_index_groups=groups)


def added(parts):
    return jnp.sum(parts.astype(jnp.float32), axis=0)


def matmul(left, right, contract):
    return lax.dot_general(left, right, (contract, ((), ())), preferred_element_type=jnp.float32)


def shards(tokens, expand, project, out_grad):
    rows, cols = lax.axis_size("row"), lax.axis_size("col")
    chips, size = cols // CORES, rows // PAIR
    own, features = tokens.shape
    hidden = expand.shape[1]
    count = chips * own
    half = count // PAIR
    share = half // size
    over_col, over_z = col_groups(rows, cols), half_row_groups(rows)
    factor = 1.0 / math.sqrt(own * cols)
    both = ("row", "col")

    def copies(block, members):
        return jnp.broadcast_to(block[None], (members, *block.shape))

    def after(block, earlier):
        return lax.optimization_barrier((block, earlier))[0]

    tok = exchange(copies(tokens, chips), both, over_col)
    cot = exchange(after(copies(out_grad, chips), tok), both, over_col)
    tok, cot = tok.reshape(count, features), cot.reshape(count, features)
    expand_two = jnp.concatenate([expand, swap_cores(expand)], axis=1)
    project_two = jnp.concatenate([project, swap_cores(project)], axis=0)

    def row_parts(panel, weight, contract):
        theirs = swap_halves(matmul(panel[half:], weight, contract).astype(jnp.bfloat16))
        mine = matmul(panel[:half], weight, contract) + theirs.astype(jnp.float32)
        return mine.astype(jnp.bfloat16).reshape(size, share, CORES * hidden)

    pre_parts = row_parts(tok, expand_two, ((1,), (0,)))
    back_parts = row_parts(cot, project_two, ((1,), (1,)))
    pre_parts = exchange(after(pre_parts, cot), "row", over_z)
    gelu, slope = gelu_and_slope(added(pre_parts))
    act = copies(gelu.astype(jnp.bfloat16), size)
    mixed = exchange(jnp.concatenate([back_parts, act], axis=1), "row", over_z)
    grad = (added(mixed[:, :share]) * slope).astype(jnp.bfloat16)
    act_mine = mixed[:, share:].reshape(half, CORES * hidden)
    grad_mine = exchange(copies(grad, size), "row", over_z).reshape(half, CORES * hidden)
    act_panel = jnp.concatenate([act_mine, swap_halves(act_mine)], axis=0)
    grad_panel = jnp.concatenate([grad_mine, swap_halves(grad_mine)], axis=0)

    def col_parts(panel, weight, contract):
        parts = matmul(panel, weight, contract).astype(jnp.bfloat16)
        return parts.reshape(chips, own, features)

    out_parts = col_parts(act_panel, project_two, ((1,), (0,)))
    tok_parts = col_parts(grad_panel, expand_two, ((1,), (1,)))
    out_parts = exchange(after(out_parts, grad_mine), both, over_col)
    tok_parts = exchange(after(tok_parts, out_parts), both, over_col)
    layer_out = added(out_parts).astype(jnp.bfloat16)
    token_grad = added(tok_parts).astype(jnp.bfloat16)

    def all_tokens(panel):
        return jnp.concatenate([panel, swap_cores(panel)], axis=0)

    def hidden_tokens(panel):
        return jnp.concatenate([panel[:, :hidden], swap_cores(panel[:, hidden:])], axis=0)

    project_grad = matmul(hidden_tokens(act_panel), all_tokens(cot), ((0,), (0,)))
    expand_grad = matmul(all_tokens(tok), hidden_tokens(grad_panel), ((0,), (0,)))
    return (
        layer_out,
        token_grad,
        (expand_grad * factor).astype(jnp.bfloat16),
        (project_grad * factor).astype(jnp.bfloat16),
    )


def solution(mesh):
    placed = (P("col", "row"), P("row", "col"), P("col", "row"), P("col", "row"))
    return jax.shard_map(
        shards,
        mesh=mesh,
        in_specs=placed,
        out_specs=(P("col", "row"), P("col", "row"), P("row", "col"), P("col", "row")),
        check_vma=False,
    )
```

time: 162 us -> 165 us (1.019)
  the two profiles are of different devices: /device:TPU:64 before, /device:TPU:1 now
where the time goes in v2:
time: 165 us; the launch traced here: 164 us
  starting transfers between devices  77.4 us (47%)
  waiting for transfers between devices  31.2 us (19%)
  blocking collectives  23 us (14%)
  matrix products  18.3 us (11%)
  local copies, waits for them, and re-layouts  10.2 us (6%)
  other arithmetic  2.73 us (2%)
    all_to_all x6, starting transfers between devices, exchange(): return lax.all_to_all(parts, axis, 0, 0, axis_index_groups=groups)  34.5 us
    ppermute x6, starting transfers between devices, swap_cores(): return lax.ppermute(block, 'col', [(at, at ^ 1) for at in range(cols)])  31.4 us
    all_to_all x1, blocking collectives, exchange(): return lax.all_to_all(parts, axis, 0, 0, axis_index_groups=groups)  23 us
    all_to_all x6, waiting for transfers between devices, exchange(): return lax.all_to_all(parts, axis, 0, 0, axis_index_groups=groups)  18.6 us
    dot_general x8, matrix products, matmul(): lax.dot_general(left, right, (contract, ((), ())), preferred_element_type...  18.3 us
    ppermute x4, waiting for transfers between devices, swap_halves(): lax.ppermute(block, 'row', [(at, (at + rows // PAIR) % rows) for at in ra...  12.5 us
    ppermute x4, starting transfers between devices, swap_halves(): lax.ppermute(block, 'row', [(at, (at + rows // PAIR) % rows) for at in ra...  11.6 us
  transfers between devices with their start and end apart: 16, of which 6 were waited for; matrix products, arithmetic and copies ran while one was open for 18% of the time, Pallas kernels for 0%

profile of v2, /device:TPU:1, one launch (start us, length us, event | category | flops | bytes accessed | tf_op | source)
XLA Modules:
  0.0 163.8 jit_solution(2463367539330015608)
XLA Ops:
  0.6 8.8 %collective-permute-start.2 = (bf16[768,768]{1,0:T(8,128)(2,1)}, bf16[768,768]{1,0:T(8,128)(2,1)}, u32[]{:S(2)}, u32[]{:S(2)}) collective-permute-start(bf16[768,768]{1,0:T(8,128)(2,1)} %param.5), channel_id=1, source_target_pairs={{0,1},{1,0},{2,3},{3,2},{4,5},{5,4},{6,7},{7,6},{8,9},{9,8},{10,11... | collective-permute-start | bytes 3538952 | tf_op jit(solution)/shard_map/ppermute | solution.py:42
  9.4 1.5 broadcast_in_dim.9
  10.9 3.6 %all-to-all-start = ((bf16[16,16,768]{2,1,0:T(8,128)(2,1)}), bf16[16,16,768]{2,1,0:T(8,128)(2,1)S(1)}, u32[]{:S(2)}, u32[]{:S(2)}) async-start(bf16[16,16,768]{2,1,0:T(8,128)(2,1)} %broadcast_in_dim.9), calls=%async_computation | async-start | bytes 786432 | tf_op jit(solution)/shard_map/all_to_all | solution.py:51
  14.5 0.0 copy-start.5
  14.5 0.0 copy-start.6
  14.5 2.1 %collective-permute-start = (bf16[768,768]{1,0:T(8,128)(2,1)}, bf16[768,768]{1,0:T(8,128)(2,1)}, u32[]{:S(2)}, u32[]{:S(2)}) collective-permute-start(bf16[768,768]{1,0:T(8,128)(2,1)} %param.6), channel_id=1, source_target_pairs={{0,1},{1,0},{2,3},{3,2},{4,5},{5,4},{6,7},{7,6},{8,9},{9,8},{10,11... | collective-permute-start | bytes 3538952 | tf_op jit(solution)/shard_map/ppermute | solution.py:42
  16.6 1.3 constant_dynamic-update-slice_fusion.1
  17.9 0.0 copy-done.5
  17.9 1.2 constant_dynamic-update-slice_fusion.3
  19.1 7.5 %all-to-all-done = bf16[16,16,768]{2,1,0:T(8,128)(2,1)S(1)} async-done(((bf16[16,16,768]{2,1,0:T(8,128)(2,1)}), bf16[16,16,768]{2,1,0:T(8,128)(2,1)S(1)}, u32[]{:S(2)}, u32[]{:S(2)}) %all-to-all-start) | async-done | bytes 393248 | tf_op jit(solution)/shard_map/all_to_all | solution.py:51
  26.6 0.0 copy-done.6
  26.6 0.8 broadcast_in_dim.8
  27.4 5.4 %all-to-all-start.1 = ((bf16[16,16,768]{2,1,0:T(8,128)(2,1)}), bf16[16,16,768]{2,1,0:T(8,128)(2,1)S(1)}, u32[]{:S(2)}, u32[]{:S(2)}) async-start(bf16[16,16,768]{2,1,0:T(8,128)(2,1)} %broadcast_in_dim.8), calls=%async_computation.1 | async-start | bytes 786432 | tf_op jit(solution)/shard_map/all_to_all | solution.py:51
  32.9 0.0 collective-permute-done.2
  32.9 2.5 %constant_dynamic-update-slice_fusion.2 = bf16[768,1536]{1,0:T(8,128)(2,1)} fusion(bf16[768,1536]{1,0:T(8,128)(2,1)} %constant_dynamic-update-slice_fusion.3, bf16[768,768]{1,0:T(8,128)(2,1)} %collective-permute-done.2), kind=kLoop, calls=%fused_computation.53 | loop fusion | bytes 2359296 | tf_op jit(solution)/shard_map/concatenate | solution.py:83
  35.4 2.9 %fusion.3 = bf16[128,1536]{1,0:T(8,128)(2,1)} fusion(bf16[128,768]{1,0:T(8,128)(2,1)S(1)} %bitcast.40, bf16[768,1536]{1,0:T(8,128)(2,1)} %constant_dynamic-update-slice_fusion.2), kind=kOutput, calls=%fused_computation.9 | convolution fusion | flops 302186496 | bytes 2949120 | tf_op jit(solution)/shard_map/dot_general | solution.py:59
  38.3 3.8 %collective-permute-start.3 = (bf16[128,1536]{1,0:T(8,128)(2,1)}, bf16[128,1536]{1,0:T(8,128)(2,1)}, u32[]{:S(2)}, u32[]{:S(2)}) collective-permute-start(bf16[128,1536]{1,0:T(8,128)(2,1)} %fusion.3), channel_id=1, source_target_pairs={{0,256},{32,288},{64,320},{96,352},{128,384},{160,416},{192,448},{... | collective-permute-start | bytes 1179656 | tf_op jit(solution)/shard_map/ppermute | solution.py:47
  42.0 0.0 collective-permute-done
  42.0 1.3 constant_dynamic-update-slice_fusion
  43.4 0.7 all-to-all-done.1
  44.1 0.7 fusion.31
  44.8 1.6 %convolution_convert_fusion.1 = bf16[128,1536]{1,0:T(8,128)(2,1)} fusion(bf16[128,768]{1,0:T(8,128)(2,1)S(1)} %bitcast.41, bf16[1536,768]{1,0:T(8,128)(2,1)S(1)} %constant_dynamic-update-slice_fusion), kind=kOutput, calls=%fused_computation.6 | convolution fusion | flops 302186496 | bytes 2949120 | tf_op jit(solution)/shard_map/dot_general | solution.py:59
  46.4 2.7 %collective-permute-start.1 = (bf16[128,1536]{1,0:T(8,128)(2,1)}, bf16[128,1536]{1,0:T(8,128)(2,1)}, u32[]{:S(2)}, u32[]{:S(2)}) collective-permute-start(bf16[128,1536]{1,0:T(8,128)(2,1)} %convolution_convert_fusion.1), channel_id=1, source_target_pairs={{0,256},{32,288},{64,320},{96,352},{128,384},{160,416},{192,448},{... | collective-permute-start | bytes 1179656 | tf_op jit(solution)/shard_map/ppermute | solution.py:47
  49.1 3.8 %collective-permute-done.3 = bf16[128,1536]{1,0:T(8,128)(2,1)} collective-permute-done((bf16[128,1536]{1,0:T(8,128)(2,1)}, bf16[128,1536]{1,0:T(8,128)(2,1)}, u32[]{:S(2)}, u32[]{:S(2)}) %collective-permute-start.3) | collective-permute-done | bytes 393248 | tf_op jit(solution)/shard_map/ppermute | solution.py:47
  52.9 0.0 copy-done
  52.9 2.2 %fusion.1 = bf16[128,1536]{1,0:T(8,128)(2,1)} fusion(bf16[128,768]{1,0:T(8,128)(2,1)S(1)} %bitcast.38, bf16[768,1536]{1,0:T(8,128)(2,1)S(1)} %copy-done, bf16[128,1536]{1,0:T(8,128)(2,1)} %collective-permute-done.3), kind=kOutput, calls=%fused_computation.3 | convolution fusion | flops 302579712 | bytes 3342336 | tf_op jit(solution)/shard_map/dot_general | solution.py:59
  55.1 0.0 copy-done.1
  55.1 10.0 %all-to-all-start.2 = ((bf16[8,16,1536]{2,1,0:T(8,128)(2,1)}), bf16[8,16,1536]{2,1,0:T(8,128)(2,1)S(1)}, u32[]{:S(2)}, u32[]{:S(2)}) async-start(bf16[8,16,1536]{2,1,0:T(8,128)(2,1)} %bitcast.7), calls=%async_computation.2 | async-start | bytes 786432 | tf_op jit(solution)/shard_map/all_to_all | solution.py:51
  65.1 0.0 collective-permute-done.1
  65.1 2.0 %fusion.2 = bf16[128,1536]{1,0:T(8,128)(2,1)S(1)} fusion(bf16[128,768]{1,0:T(8,128)(2,1)} %bitcast.39, bf16[1536,768]{1,0:T(8,128)(2,1)S(1)} %constant_dynamic-update-slice_fusion, bf16[128,1536]{1,0:T(8,128)(2,1)} %collective-permute-done.1), kind=kOutput, calls=%fused_computation.4 | convolution fusion | flops 302579712 | bytes 3342336 | tf_op jit(solution)/shard_map/dot_general | solution.py:59
  67.1 10.4 %all-to-all-done.2 = bf16[8,16,1536]{2,1,0:T(8,128)(2,1)S(1)} async-done(((bf16[8,16,1536]{2,1,0:T(8,128)(2,1)}), bf16[8,16,1536]{2,1,0:T(8,128)(2,1)S(1)}, u32[]{:S(2)}, u32[]{:S(2)}) %all-to-all-start.2) | async-done | bytes 393248 | tf_op jit(solution)/shard_map/all_to_all | solution.py:51
  77.6 0.1 convert_reduce_fusion.1
  77.7 0.1 pad_maximum_fusion.4
  77.8 23.0 %all_to_all.35 = bf16[8,32,1536]{2,1,0:T(8,128)(2,1)S(1)} all-to-all(bf16[8,32,1536]{2,1,0:T(8,128)(2,1)S(1)} %pad_maximum_fusion.4), channel_id=1, replica_groups={{0,32,64,96,128,160,192,224},{256,288,320,352,384,416,448,480},{1,33,65..., dimensions={0} | all-to-all | bytes 1572864 | tf_op jit(solution)/shard_map/all_to_all | solution.py:51
  100.8 0.1 convert_reduce_fusion
  100.8 0.1 fusion.26
  100.9 0.8 broadcast_in_dim.11
  101.7 4.1 %all-to-all-start.4 = ((bf16[8,16,1536]{2,1,0:T(8,128)(2,1)}), bf16[8,16,1536]{2,1,0:T(8,128)(2,1)}, u32[]{:S(2)}, u32[]{:S(2)}) async-start(bf16[8,16,1536]{2,1,0:T(8,128)(2,1)} %broadcast_in_dim.11), calls=%async_computation.4 | async-start | bytes 786432 | tf_op jit(solution)/shard_map/all_to_all | solution.py:51
  105.8 2.1 %collective-permute-start.4 = (bf16[128,1536]{1,0:T(8,128)(2,1)S(1)}, bf16[128,1536]{1,0:T(8,128)(2,1)S(1)}, u32[]{:S(2)}, u32[]{:S(2)}) collective-permute-start(bf16[128,1536]{1,0:T(8,128)(2,1)S(1)} %bitcast.35), channel_id=1, source_target_pairs={{0,256},{32,288},{64,320},{96,352},{128,384},{160,416},{192,448},{... | collective-permute-start | bytes 1179656 | tf_op jit(solution)/shard_map/ppermute | solution.py:47
  107.9 8.5 %collective-permute-done.4 = bf16[128,1536]{1,0:T(8,128)(2,1)S(1)} collective-permute-done((bf16[128,1536]{1,0:T(8,128)(2,1)S(1)}, bf16[128,1536]{1,0:T(8,128)(2,1)S(1)}, u32[]{:S(2)}, u32[]{:S(2)}) %collective-permute-start.4) | collective-permute-done | bytes 393248 | tf_op jit(solution)/shard_map/ppermute | solution.py:47
  116.4 0.0 copy-done.3
  116.4 1.5 convolution_convert_fusion.3
  117.9 0.0 all-to-all-done.4
  117.9 3.6 %all-to-all-start.5 = ((bf16[16,16,768]{2,1,0:T(8,128)(2,1)}), bf16[16,16,768]{2,1,0:T(8,128)(2,1)S(1)}, u32[]{:S(2)}, u32[]{:S(2)}) async-start(bf16[16,16,768]{2,1,0:T(8,128)(2,1)} %bitcast.10), calls=%async_computation.5 | async-start | bytes 786432 | tf_op jit(solution)/shard_map/all_to_all | solution.py:51
  121.5 3.1 %collective-permute-start.5 = (bf16[128,1536]{1,0:T(8,128)(2,1)}, bf16[128,1536]{1,0:T(8,128)(2,1)S(1)}, u32[]{:S(2)}, u32[]{:S(2)}) collective-permute-start(bf16[128,1536]{1,0:T(8,128)(2,1)} %bitcast.11), channel_id=1, source_target_pairs={{0,256},{32,288},{64,320},{96,352},{128,384},{160,416},{192,448},{... | collective-permute-start | bytes 1179656 | tf_op jit(solution)/shard_map/ppermute | solution.py:47
  124.6 8.8 %collective-permute-start.9 = (bf16[256,768]{1,0:T(8,128)(2,1)S(1)}, bf16[256,768]{1,0:T(8,128)(2,1)}, u32[]{:S(2)}, u32[]{:S(2)}) collective-permute-start(bf16[256,768]{1,0:T(8,128)(2,1)S(1)} %bitcast.32), channel_id=1, source_target_pairs={{0,1},{1,0},{2,3},{3,2},{4,5},{5,4},{6,7},{7,6},{8,9},{9,8},{10,11... | collective-permute-start | bytes 1179656 | tf_op jit(solution)/shard_map/ppermute | solution.py:42
  133.4 0.2 collective-permute-done.5
  133.6 3.4 %convolution_convert_fusion.2 = bf16[256,768]{1,0:T(8,128)(2,1)} fusion(bf16[768,1536]{1,0:T(8,128)(2,1)} %constant_dynamic-update-slice_fusion.2, bf16[128,1536]{1,0:T(8,128)(2,1)S(1)} %collective-permute-done.5, bf16[128,1536]{1,0:T(8,128)(2,1)} %bitcast.11), kind=kOutput, calls=%fused_computation.10 | convolution fusion | flops 605749248 | bytes 3538944 | tf_op jit(solution)/shard_map/dot_general | solution.py:59
  137.0 0.0 all-to-all-done.5
  137.0 7.9 %all-to-all-start.6 = ((bf16[16,16,768]{2,1,0:T(8,128)(2,1)}), bf16[16,16,768]{2,1,0:T(8,128)(2,1)S(1)}, u32[]{:S(2)}, u32[]{:S(2)}) async-start(bf16[16,16,768]{2,1,0:T(8,128)(2,1)} %bitcast.12), calls=%async_computation.6 | async-start | bytes 786432 | tf_op jit(solution)/shard_map/all_to_all | solution.py:51
  144.8 0.1 fusion.18
  144.9 7.4 %collective-permute-start.8 = (bf16[256,768]{1,0:T(8,128)(2,1)S(1)}, bf16[256,768]{1,0:T(8,128)(2,1)S(1)}, u32[]{:S(2)}, u32[]{:S(2)}) collective-permute-start(bf16[256,768]{1,0:T(8,128)(2,1)S(1)} %get-tuple-element.13), channel_id=1, source_target_pairs={{0,1},{1,0},{2,3},{3,2},{4,5},{5,4},{6,7},{7,6},{8,9},{9,8},{10,11... | collective-permute-start | bytes 1179656 | tf_op jit(solution)/shard_map/ppermute | solution.py:42
  152.3 1.9 %collective-permute-start.6 = (bf16[256,768]{1,0:T(8,128)(2,1)S(1)}, bf16[256,768]{1,0:T(8,128)(2,1)S(1)}, u32[]{:S(2)}, u32[]{:S(2)}) collective-permute-start(bf16[256,768]{1,0:T(8,128)(2,1)S(1)} %bitcast.30), channel_id=1, source_target_pairs={{0,1},{1,0},{2,3},{3,2},{4,5},{5,4},{6,7},{7,6},{8,9},{9,8},{10,11... | collective-permute-start | bytes 1179656 | tf_op jit(solution)/shard_map/ppermute | solution.py:42
  154.3 1.1 fusion.16
  155.3 2.4 %collective-permute-start.7 = (bf16[256,768]{1,0:T(8,128)(2,1)S(1)}, bf16[256,768]{1,0:T(8,128)(2,1)S(1)}, u32[]{:S(2)}, u32[]{:S(2)}) collective-permute-start(bf16[256,768]{1,0:T(8,128)(2,1)S(1)} %get-tuple-element.15), channel_id=1, source_target_pairs={{0,1},{1,0},{2,3},{3,2},{4,5},{5,4},{6,7},{7,6},{8,9},{9,8},{10,11... | collective-permute-start | bytes 1179656 | tf_op jit(solution)/shard_map/ppermute | solution.py:42
  157.8 0.0 collective-permute-done.9
  157.8 0.0 collective-permute-done.8
  157.8 2.8 %multiply_convert_fusion = bf16[768,768]{1,0:T(8,128)(2,1)} fusion(bf16[256,768]{1,0:T(8,128)(2,1)S(1)} %collective-permute-done.8, bf16[256,768]{1,0:T(8,128)(2,1)S(1)} %get-tuple-element.12, bf16[256,768]{1,0:T(8,128)(2,1)} %collective-permute-done.9, bf16[256,768]{1,0:T(8,128)(2,1)S(1)} %bitcast.33), kind=kOutput, calls=%fused_computation.7 | convolution fusion | flops 608305152 | bytes 2752512 | tf_op jit(solution)/shard_map/dot_general | solution.py:59
  160.6 0.7 reduce_sum.44
  161.3 0.0 collective-permute-done.6
  161.3 0.0 collective-permute-done.7
  161.3 1.8 %multiply_convert_fusion.1 = bf16[768,768]{1,0:T(8,128)(2,1)} fusion(bf16[256,768]{1,0:T(8,128)(2,1)S(1)} %collective-permute-done.6, bf16[256,768]{1,0:T(8,128)(2,1)S(1)} %bitcast.31, bf16[256,768]{1,0:T(8,128)(2,1)S(1)} %collective-permute-done.7, bf16[256,768]{1,0:T(8,128)(2,1)S(1)} %get-tuple-element.14), kind=kOutput, calls=%fused_computation.8 | convolution fusion | flops 608305152 | bytes 2752512 | tf_op jit(solution)/shard_map/dot_general | solution.py:59
  163.1 0.0 all-to-all-done.6
  163.1 0.7 reduce_sum.45
  (11 shorter events, 0.1 us)
Async XLA Ops:
  0.6 32.3 %collective-permute-start.2 = (bf16[768,768]{1,0:T(8,128)(2,1)}, bf16[768,768]{1,0:T(8,128)(2,1)}, u32[]{:S(2)}, u32[]{:S(2)}) collective-permute-start(bf16[768,768]{1,0:T(8,128)(2,1)} %param.5), channel_id=1, source_target_pairs={{0,1},{1,0},{2,3},{3,2},{4,5},{5,4},{6,7},{7,6},{8,9},{9,8},{10,11... | collective-permute-start | bytes 3538952 | tf_op jit(solution)/shard_map/ppermute | solution.py:42
  10.9 15.7 %all-to-all-start = ((bf16[16,16,768]{2,1,0:T(8,128)(2,1)}), bf16[16,16,768]{2,1,0:T(8,128)(2,1)S(1)}, u32[]{:S(2)}, u32[]{:S(2)}) async-start(bf16[16,16,768]{2,1,0:T(8,128)(2,1)} %broadcast_in_dim.9), calls=%async_computation | async-start | bytes 786432 | tf_op jit(solution)/shard_map/all_to_all | solution.py:51
  14.5 3.4 %copy-start.5 = (bf16[768,768]{1,0:T(8,128)(2,1)S(1)}, bf16[768,768]{1,0:T(8,128)(2,1)}, u32[]{:S(2)}) copy-start(bf16[768,768]{1,0:T(8,128)(2,1)} %param.5) | copy-start | bytes 3538948
  14.5 12.1 %copy-start.6 = (bf16[16,768]{1,0:T(8,128)(2,1)S(1)}, bf16[16,768]{1,0:T(8,128)(2,1)}, u32[]{:S(2)}) copy-start(bf16[16,768]{1,0:T(8,128)(2,1)} %param.7) | copy-start | bytes 73732
  14.5 27.5 %collective-permute-start = (bf16[768,768]{1,0:T(8,128)(2,1)}, bf16[768,768]{1,0:T(8,128)(2,1)}, u32[]{:S(2)}, u32[]{:S(2)}) collective-permute-start(bf16[768,768]{1,0:T(8,128)(2,1)} %param.6), channel_id=1, source_target_pairs={{0,1},{1,0},{2,3},{3,2},{4,5},{5,4},{6,7},{7,6},{8,9},{9,8},{10,11... | collective-permute-start | bytes 3538952 | tf_op jit(solution)/shard_map/ppermute | solution.py:42
  27.4 16.6 %all-to-all-start.1 = ((bf16[16,16,768]{2,1,0:T(8,128)(2,1)}), bf16[16,16,768]{2,1,0:T(8,128)(2,1)S(1)}, u32[]{:S(2)}, u32[]{:S(2)}) async-start(bf16[16,16,768]{2,1,0:T(8,128)(2,1)} %broadcast_in_dim.8), calls=%async_computation.1 | async-start | bytes 786432 | tf_op jit(solution)/shard_map/all_to_all | solution.py:51
  38.3 14.7 %collective-permute-start.3 = (bf16[128,1536]{1,0:T(8,128)(2,1)}, bf16[128,1536]{1,0:T(8,128)(2,1)}, u32[]{:S(2)}, u32[]{:S(2)}) collective-permute-start(bf16[128,1536]{1,0:T(8,128)(2,1)} %fusion.3), channel_id=1, source_target_pairs={{0,256},{32,288},{64,320},{96,352},{128,384},{160,416},{192,448},{... | collective-permute-start | bytes 1179656 | tf_op jit(solution)/shard_map/ppermute | solution.py:47
  44.1 11.1 %copy-start.1 = (bf16[16,16,768]{2,1,0:T(8,128)(2,1)}, bf16[16,16,768]{2,1,0:T(8,128)(2,1)S(1)}, u32[]{:S(2)}) copy-start(bf16[16,16,768]{2,1,0:T(8,128)(2,1)S(1)} %all-to-all-done.1) | copy-start | bytes 1179652
  44.1 8.9 %copy-start = (bf16[768,1536]{1,0:T(8,128)(2,1)S(1)}, bf16[768,1536]{1,0:T(8,128)(2,1)}, u32[]{:S(2)}) copy-start(bf16[768,1536]{1,0:T(8,128)(2,1)} %constant_dynamic-update-slice_fusion.2) | copy-start | bytes 7077892
  46.4 18.7 %collective-permute-start.1 = (bf16[128,1536]{1,0:T(8,128)(2,1)}, bf16[128,1536]{1,0:T(8,128)(2,1)}, u32[]{:S(2)}, u32[]{:S(2)}) collective-permute-start(bf16[128,1536]{1,0:T(8,128)(2,1)} %convolution_convert_fusion.1), channel_id=1, source_target_pairs={{0,256},{32,288},{64,320},{96,352},{128,384},{160,416},{192,448},{... | collective-permute-start | bytes 1179656 | tf_op jit(solution)/shard_map/ppermute | solution.py:47
  55.1 22.4 %all-to-all-start.2 = ((bf16[8,16,1536]{2,1,0:T(8,128)(2,1)}), bf16[8,16,1536]{2,1,0:T(8,128)(2,1)S(1)}, u32[]{:S(2)}, u32[]{:S(2)}) async-start(bf16[8,16,1536]{2,1,0:T(8,128)(2,1)} %bitcast.7), calls=%async_computation.2 | async-start | bytes 786432 | tf_op jit(solution)/shard_map/all_to_all | solution.py:51
  101.7 16.2 %all-to-all-start.4 = ((bf16[8,16,1536]{2,1,0:T(8,128)(2,1)}), bf16[8,16,1536]{2,1,0:T(8,128)(2,1)}, u32[]{:S(2)}, u32[]{:S(2)}) async-start(bf16[8,16,1536]{2,1,0:T(8,128)(2,1)} %broadcast_in_dim.11), calls=%async_computation.4 | async-start | bytes 786432 | tf_op jit(solution)/shard_map/all_to_all | solution.py:51
  105.8 10.6 %copy-start.3 = (bf16[8,16,1536]{2,1,0:T(8,128)(2,1)}, bf16[8,16,1536]{2,1,0:T(8,128)(2,1)S(1)}, u32[]{:S(2)}) copy-start(bf16[8,16,1536]{2,1,0:T(8,128)(2,1)S(1)} %slice.60) | copy-start | bytes 1179652
  105.8 18.8 %copy-start.2 = (bf16[16,16,768]{2,1,0:T(8,128)(2,1)S(1)}, bf16[16,16,768]{2,1,0:T(8,128)(2,1)}, u32[]{:S(2)}) copy-start(bf16[16,16,768]{2,1,0:T(8,128)(2,1)} %copy-done.1) | copy-start | bytes 1179652
  105.8 10.6 %collective-permute-start.4 = (bf16[128,1536]{1,0:T(8,128)(2,1)S(1)}, bf16[128,1536]{1,0:T(8,128)(2,1)S(1)}, u32[]{:S(2)}, u32[]{:S(2)}) collective-permute-start(bf16[128,1536]{1,0:T(8,128)(2,1)S(1)} %bitcast.35), channel_id=1, source_target_pairs={{0,256},{32,288},{64,320},{96,352},{128,384},{160,416},{192,448},{... | collective-permute-start | bytes 1179656 | tf_op jit(solution)/shard_map/ppermute | solution.py:47
  117.9 19.1 %all-to-all-start.5 = ((bf16[16,16,768]{2,1,0:T(8,128)(2,1)}), bf16[16,16,768]{2,1,0:T(8,128)(2,1)S(1)}, u32[]{:S(2)}, u32[]{:S(2)}) async-start(bf16[16,16,768]{2,1,0:T(8,128)(2,1)} %bitcast.10), calls=%async_computation.5 | async-start | bytes 786432 | tf_op jit(solution)/shard_map/all_to_all | solution.py:51
  121.5 23.4 %copy-start.4 = (bf16[8,16,1536]{2,1,0:T(8,128)(2,1)S(1)}, bf16[8,16,1536]{2,1,0:T(8,128)(2,1)}, u32[]{:S(2)}) copy-start(bf16[8,16,1536]{2,1,0:T(8,128)(2,1)} %copy-done.3) | copy-start | bytes 1179652
  121.5 12.1 %collective-permute-start.5 = (bf16[128,1536]{1,0:T(8,128)(2,1)}, bf16[128,1536]{1,0:T(8,128)(2,1)S(1)}, u32[]{:S(2)}, u32[]{:S(2)}) collective-permute-start(bf16[128,1536]{1,0:T(8,128)(2,1)} %bitcast.11), channel_id=1, source_target_pairs={{0,256},{32,288},{64,320},{96,352},{128,384},{160,416},{192,448},{... | collective-permute-start | bytes 1179656 | tf_op jit(solution)/shard_map/ppermute | solution.py:47
  124.6 33.2 %collective-permute-start.9 = (bf16[256,768]{1,0:T(8,128)(2,1)S(1)}, bf16[256,768]{1,0:T(8,128)(2,1)}, u32[]{:S(2)}, u32[]{:S(2)}) collective-permute-start(bf16[256,768]{1,0:T(8,128)(2,1)S(1)} %bitcast.32), channel_id=1, source_target_pairs={{0,1},{1,0},{2,3},{3,2},{4,5},{5,4},{6,7},{7,6},{8,9},{9,8},{10,11... | collective-permute-start | bytes 1179656 | tf_op jit(solution)/shard_map/ppermute | solution.py:42
  137.0 26.1 %all-to-all-start.6 = ((bf16[16,16,768]{2,1,0:T(8,128)(2,1)}), bf16[16,16,768]{2,1,0:T(8,128)(2,1)S(1)}, u32[]{:S(2)}, u32[]{:S(2)}) async-start(bf16[16,16,768]{2,1,0:T(8,128)(2,1)} %bitcast.12), calls=%async_computation.6 | async-start | bytes 786432 | tf_op jit(solution)/shard_map/all_to_all | solution.py:51
  144.9 12.9 %collective-permute-start.8 = (bf16[256,768]{1,0:T(8,128)(2,1)S(1)}, bf16[256,768]{1,0:T(8,128)(2,1)S(1)}, u32[]{:S(2)}, u32[]{:S(2)}) collective-permute-start(bf16[256,768]{1,0:T(8,128)(2,1)S(1)} %get-tuple-element.13), channel_id=1, source_target_pairs={{0,1},{1,0},{2,3},{3,2},{4,5},{5,4},{6,7},{7,6},{8,9},{9,8},{10,11... | collective-permute-start | bytes 1179656 | tf_op jit(solution)/shard_map/ppermute | solution.py:42
  152.3 8.9 %collective-permute-start.6 = (bf16[256,768]{1,0:T(8,128)(2,1)S(1)}, bf16[256,768]{1,0:T(8,128)(2,1)S(1)}, u32[]{:S(2)}, u32[]{:S(2)}) collective-permute-start(bf16[256,768]{1,0:T(8,128)(2,1)S(1)} %bitcast.30), channel_id=1, source_target_pairs={{0,1},{1,0},{2,3},{3,2},{4,5},{5,4},{6,7},{7,6},{8,9},{9,8},{10,11... | collective-permute-start | bytes 1179656 | tf_op jit(solution)/shard_map/ppermute | solution.py:42
  155.3 5.9 %collective-permute-start.7 = (bf16[256,768]{1,0:T(8,128)(2,1)S(1)}, bf16[256,768]{1,0:T(8,128)(2,1)S(1)}, u32[]{:S(2)}, u32[]{:S(2)}) collective-permute-start(bf16[256,768]{1,0:T(8,128)(2,1)S(1)} %get-tuple-element.15), channel_id=1, source_target_pairs={{0,1},{1,0},{2,3},{3,2},{4,5},{5,4},{6,7},{7,6},{8,9},{9,8},{10,11... | collective-permute-start | bytes 1179656 | tf_op jit(solution)/shard_map/ppermute | solution.py:42

commit v3 on v1

v3 whole, which is shorter than its diff:
```python
import functools
import math

import jax
import jax.numpy as jnp
from jax import lax
from jax.experimental import pallas as pl
from jax.experimental.pallas import tpu as pltpu
from jax.sharding import PartitionSpec as P

SLOPE_C = math.sqrt(2.0 / math.pi)
CUBIC = 0.044715
CORES = 2
PAIR = 2
HIDE_FRONT = 1
HIDE_ACT = 1
HIDE_BACK = 100
F32, BF16 = jnp.float32, jnp.bfloat16
VMEM_BYTES = 12 << 20
IN_SMEM = pl.BlockSpec(memory_space=pltpu.SMEM)
IN_VMEM = pl.BlockSpec(memory_space=pltpu.VMEM)
ANYWHERE = pl.BlockSpec(memory_space=pl.ANY)


def gelu_and_slope(value):
    inner = SLOPE_C * (value + CUBIC * value * value * value)
    tanh_value = jnp.tanh(inner)
    gelu = 0.5 * value * (1.0 + tanh_value)
    slope = 0.5 * (1.0 + tanh_value) + 0.5 * value * (1.0 - tanh_value * tanh_value) * SLOPE_C * (
        1.0 + 3.0 * CUBIC * value * value
    )
    return gelu, slope


def col_groups(cols):
    return [list(range(core, cols, CORES)) for core in range(CORES)]


def swap_cores(block):
    cols = lax.axis_size("col")
    return lax.ppermute(block, "col", [(at, at ^ 1) for at in range(cols)])


def row_groups(rows):
    step = rows // PAIR
    return [list(range(at * step, (at + 1) * step)) for at in range(PAIR)]


def swap_halves(block):
    rows = lax.axis_size("row")
    return lax.ppermute(block, "row", [(at, (at + rows // PAIR) % rows) for at in range(rows)])


def exchange(parts, axis, groups):
    return lax.all_to_all(parts, axis, 0, 0, axis_index_groups=groups)


def after(block, earlier):
    return lax.optimization_barrier((block, earlier))[0]


def matmul(left, right, contract):
    return lax.dot_general(left, right, (contract, ((), ())), preferred_element_type=F32)


def times(left, right):
    return matmul(left, right, ((1,), (0,)))


def times_turned(left, right):
    return matmul(left, right, ((1,), (1,)))


def flat(block):
    return block.reshape(-1, block.shape[-1])


def array(*shape, dtype=BF16):
    return jax.ShapeDtypeStruct(shape, dtype)


def call(kernel, outs, flops, *args, ins=(), scratch=()):
    held = sum(math.prod(a.shape) * a.dtype.itemsize for a in (*args, *outs))
    one = len(outs) == 1
    return pl.pallas_call(
        kernel,
        out_shape=outs[0] if one else outs,
        in_specs=[
            ANYWHERE if at in ins else IN_SMEM if a.dtype == jnp.int32 else IN_VMEM for at, a in enumerate(args)
        ],
        out_specs=IN_VMEM if one else [IN_VMEM] * len(outs),
        scratch_shapes=scratch,
        compiler_params=pltpu.CompilerParams(vmem_limit_bytes=VMEM_BYTES),
        cost_estimate=pl.CostEstimate(flops=flops, bytes_accessed=held, transcendentals=0),
    )(*args)


def put_terms(out, dot, panel, near, far):
    hidden = out.shape[2] // CORES
    for side, weight in enumerate((near, far)):
        terms = dot(panel, weight[...]).astype(out.dtype)
        out[:, :, side * hidden : (side + 1) * hidden] = terms.reshape(*out.shape[:2], hidden)


def pre_kernel(panels, expand, expand_far, out, held, sem):
    load = pltpu.make_async_copy(panels.at[:, pl.ds(0, out.shape[1])], held, sem)
    load.start()
    load.wait()
    put_terms(out, times, flat(held[...]), expand, expand_far)


def back_kernel(other, which, panels, project, project_far, out, held, sem):
    size, own = out.shape[0], out.shape[1]
    half = 1 - which[0] if other else which[0]
    load = pltpu.make_async_copy(panels.at[pl.ds(half * size, size), pl.ds(own, own)], held, sem)
    load.start()
    load.wait()
    put_terms(out, times_turned, flat(held[...]), project, project_far)


def added(ref, stop):
    total = ref[0, :stop].astype(F32)
    for at in range(1, ref.shape[0]):
        total += ref[at, :stop].astype(F32)
    return total


def act_kernel(sums, act, slope):
    gelu, slope[...] = gelu_and_slope(added(sums, sums.shape[1]))
    act[...] = gelu.astype(BF16)


def merge_kernel(mine, came, act, mixed):
    share = act.shape[0]
    mixed[:, :share] = (mine[...] + came[...].astype(F32)).astype(BF16)
    block = act[...]
    for at in range(mixed.shape[0]):
        mixed[at, share:] = block


def grad_kernel(mixed, slope, act, out):
    share = slope.shape[0]
    act[...] = mixed[:, share:]
    grad = (added(mixed, share) * slope[...]).astype(BF16)
    for at in range(out.shape[0]):
        out[at] = grad


def out_kernel(which, act, act_far, project, project_far, out, keep, send):
    size, own, hidden = act.shape[0], out.shape[1], project.shape[0]
    for half, block in ((which[0], act[...]), (1 - which[0], act_far[...])):
        at = pl.ds(half * size, size)
        left, right = block[:, :, :hidden], block[:, :, hidden:]
        keep[at] = left
        send[at] = right
        terms = times(flat(left), project[...]) + times(flat(right), project_far[...])
        out[at] = terms.astype(BF16).reshape(size, own, out.shape[2])


def tok_kernel(grad, out_parts, expand, expand_far, out):
    own, hidden = out_parts.shape[1], expand.shape[1]
    block = flat(grad[...])
    terms = times_turned(block[:, :hidden], expand[...]) + times_turned(block[:, hidden:], expand_far[...])
    out[:, :own] = out_parts[...]
    out[:, own:] = terms.astype(BF16).reshape(out.shape[0], own, out.shape[2])


def pack_kernel(grad, keep, send):
    hidden = keep.shape[2]
    keep[...] = grad[:, :, :hidden]
    send[...] = grad[:, :, hidden:]


def weight_grads_kernel(factor, panels, panels_far, act, act_got, grad, grad_got, expand_grad, project_grad):
    own = panels.shape[1] // 2

    def sums(left, left_far, right, right_far):
        total = matmul(flat(left), flat(right), ((0,), (0,))) + matmul(flat(left_far), flat(right_far), ((0,), (0,)))
        return (total * factor).astype(BF16)

    project_grad[...] = sums(act[...], act_got[...], panels[:, own:], panels_far[:, own:])
    expand_grad[...] = sums(panels[:, :own], panels_far[:, :own], grad[...], grad_got[...])


def final_kernel(sums, layer_out, token_grad):
    own = layer_out.shape[0]
    total = added(sums, 2 * own).astype(BF16)
    layer_out[...] = total[:own]
    token_grad[...] = total[own:]


def shards(tokens, expand, project, out_grad):
    rows, cols = lax.axis_size("row"), lax.axis_size("col")
    chips = cols // CORES
    own, features = tokens.shape
    hidden = expand.shape[1]
    wide, share, size = CORES * hidden, chips * own // rows, rows // PAIR
    over_col, along_z = col_groups(cols), row_groups(rows)
    factor = 1.0 / math.sqrt(own * cols)
    work = 2 * chips * own * wide * features
    which = (lax.axis_index("row") // size).astype(jnp.int32).reshape(1)

    block = jnp.concatenate([tokens, out_grad], axis=0)
    copies = jnp.broadcast_to(block[None], (chips, *block.shape))
    project_far = swap_cores(after(project, copies))
    expand_far = swap_cores(after(expand, copies))
    panels = exchange(copies, "col", over_col)

    half_sums = array(size, share, wide)
    pre = call(
        pre_kernel,
        [array(rows, share, wide)],
        work,
        panels,
        expand,
        expand_far,
        ins=(0,),
        scratch=[pltpu.VMEM((chips, own, features), BF16), pltpu.SemaphoreType.DMA],
    )

    def back_terms(other, dtype, earlier):
        return call(
            functools.partial(back_kernel, other),
            [array(size, share, wide, dtype=dtype)],
            work // 2 * HIDE_FRONT,
            which,
            after(panels, earlier),
            project,
            project_far,
            ins=(1,),
            scratch=[pltpu.VMEM((size, own, features), BF16), pltpu.SemaphoreType.DMA],
        )

    theirs = back_terms(True, BF16, pre)
    came = swap_halves(theirs)
    mine = back_terms(False, F32, theirs)
    pre = exchange(pre, "row", None)
    act, slope = call(
        act_kernel, [array(share, wide), array(share, wide, dtype=F32)], work * HIDE_ACT, pre
    )
    mixed = call(merge_kernel, [array(size, 2 * share, wide)], 0, mine, came, act)
    mixed = exchange(mixed, "row", along_z)
    act, grad = call(grad_kernel, [half_sums, array(rows, share, wide)], 0, mixed, slope)
    act_far = swap_halves(act)
    grad = exchange(grad, "row", None)
    held = array(chips, own, hidden)
    out_parts, act, act_send = call(
        out_kernel,
        [array(chips, own, features), held, held],
        work * HIDE_BACK,
        which,
        act,
        act_far,
        project,
        project_far,
    )
    parts = call(
        tok_kernel, [array(chips, 2 * own, features)], work, grad, out_parts, expand, expand_far
    )
    sums = exchange(parts, "col", over_col)
    act_got = swap_cores(act_send)
    grad, grad_send = call(pack_kernel, [held, held], 0, after(grad, parts))
    grad_got = swap_cores(grad_send)
    panels_far = swap_cores(after(panels, parts))
    expand_grad, project_grad = call(
        functools.partial(weight_grads_kernel, factor),
        [array(features, hidden), array(hidden, features)],
        2 * work,
        panels,
        panels_far,
        act,
        act_got,
        grad,
        grad_got,
    )
    shard = array(own, features)
    layer_out, token_grad = call(final_kernel, [shard, shard], 0, after(sums, expand_grad))
    return (layer_out, token_grad, expand_grad, project_grad)


def solution(mesh):
    placed = (P("col", "row"), P("row", "col"), P("col", "row"), P("col", "row"))
    return jax.shard_map(
        shards,
        mesh=mesh,
        in_specs=placed,
        out_specs=(P("col", "row"), P("col", "row"), P("row", "col"), P("col", "row")),
        check_vma=False,
    )
```

time: 162 us -> 157 us (0.969)
  blocking collectives: 91.9 us -> 26.7 us
  waiting for transfers between devices: 21 us -> 50.9 us
  starting transfers between devices: 28.1 us -> 50.4 us
  Pallas kernels: 0 us -> 15.2 us
  matrix products: 12.1 us -> 0 us
  local copies, waits for them, and re-layouts: 4.75 us -> 11.2 us
  other arithmetic: 2.45 us -> 0.76 us
    all_to_all x2 -> x1, blocking collectives: 91.9 us -> 26.7 us  [exchange(): return lax.all_to_all(parts, axis, 0, 0, axis_index_groups=groups)]
    all_to_all x2 -> x4, waiting for transfers between devices: 19.8 us -> 44.3 us  [exchange(): return lax.all_to_all(parts, axis, 0, 0, axis_index_groups=groups)]
    all_to_all x2 -> x4, starting transfers between devices: 15.1 us -> 31.6 us  [exchange(): return lax.all_to_all(parts, axis, 0, 0, axis_index_groups=groups)]
    pallas_call x0 -> x11, Pallas kernels: none -> 15.2 us  [call(): pl.pallas_call(kernel, out_shape=outs[0] if one else outs, in_specs=[ANYW...]
    dot_general x6 -> x0, matrix products: 12.1 us -> none  [matmul(): lax.dot_general(left, right, (contract, ((), ())), preferred_element_type...]
    unnamed x14 -> x26, local copies, waits for them, and re-layouts: 1.5 us -> 10.2 us
    ppermute x0 -> x2, starting transfers between devices: none -> 8.17 us  [swap_halves(): lax.ppermute(block, 'row', [(at, (at + rows // PAIR) % rows) for at in ra...]
    ppermute x0 -> x2, waiting for transfers between devices: none -> 4.5 us  [swap_halves(): lax.ppermute(block, 'row', [(at, (at + rows // PAIR) % rows) for at in ra...]
  transfers between devices with their start and end apart: 8 -> 11, of which waited for: 3 -> 8; matrix products, arithmetic and copies ran while one was open for 4% -> 0% of each run, Pallas kernels for 0% -> 7%
where the time goes in v3:
time: 157 us; the launch traced here: 156 us
  waiting for transfers between devices  50.9 us (32%)
  starting transfers between devices  50.4 us (32%)
  blocking collectives  26.7 us (17%)
  Pallas kernels  15.2 us (10%)
  local copies, waits for them, and re-layouts  11.2 us (7%)
    all_to_all x4, waiting for transfers between devices, exchange(): return lax.all_to_all(parts, axis, 0, 0, axis_index_groups=groups)  44.3 us
    all_to_all x4, starting transfers between devices, exchange(): return lax.all_to_all(parts, axis, 0, 0, axis_index_groups=groups)  31.6 us
    all_to_all x1, blocking collectives, exchange(): return lax.all_to_all(parts, axis, 0, 0, axis_index_groups=groups)  26.7 us
    pallas_call x11, Pallas kernels, call(): pl.pallas_call(kernel, out_shape=outs[0] if one else outs, in_specs=[ANYW...  15.2 us
    ppermute x5, starting transfers between devices, swap_cores(): return lax.ppermute(block, 'col', [(at, at ^ 1) for at in range(cols)])  10.6 us
    unnamed x26, local copies, waits for them, and re-layouts  10.2 us
    ppermute x2, starting transfers between devices, swap_halves(): lax.ppermute(block, 'row', [(at, (at + rows // PAIR) % rows) for at in ra...  8.17 us
    ppermute x2, waiting for transfers between devices, swap_halves(): lax.ppermute(block, 'row', [(at, (at + rows // PAIR) % rows) for at in ra...  4.5 us
  transfers between devices with their start and end apart: 11, of which 8 were waited for; matrix products, arithmetic and copies ran while one was open for 0% of the time, Pallas kernels for 7%

profile of v3, /device:TPU:64, one launch (start us, length us, event | category | flops | bytes accessed | tf_op | source)
XLA Modules:
  0.0 155.9 jit_solution(17099500074904397477)
XLA Ops:
  0.6 0.8 pad_maximum_fusion
  1.4 0.0 copy-start.1
  1.4 0.0 copy-start
  1.4 1.0 broadcast_in_dim.2
  2.4 8.3 %all-to-all-start = ((bf16[16,32,768]{2,1,0:T(8,128)(2,1)}), bf16[16,32,768]{2,1,0:T(8,128)(2,1)S(1)}, u32[]{:S(2)}, u32[]{:S(2)}) async-start(bf16[16,32,768]{2,1,0:T(8,128)(2,1)} %broadcast_in_dim.2), calls=%async_computation | async-start | bytes 1572864 | tf_op jit(solution)/shard_map/all_to_all | solution.py:55
  10.6 0.0 copy-done.1
  10.6 1.9 %collective-permute-start = (bf16[768,768]{1,0:T(8,128)(2,1)S(1)}, bf16[768,768]{1,0:T(8,128)(2,1)S(1)}, u32[]{:S(2)}, u32[]{:S(2)}) collective-permute-start(bf16[768,768]{1,0:T(8,128)(2,1)S(1)} %copy-done.1), channel_id=1, source_target_pairs={{0,1},{1,0},{2,3},{3,2},{4,5},{5,4},{6,7},{7,6},{8,9},{9,8},{10,11... | collective-permute-start | bytes 3538952 | tf_op jit(solution)/shard_map/ppermute | solution.py:41
  12.6 0.0 copy-done
  12.6 2.4 %collective-permute-start.1 = (bf16[768,768]{1,0:T(8,128)(2,1)S(1)}, bf16[768,768]{1,0:T(8,128)(2,1)}, u32[]{:S(2)}, u32[]{:S(2)}) collective-permute-start(bf16[768,768]{1,0:T(8,128)(2,1)S(1)} %copy-done), channel_id=1, source_target_pairs={{0,1},{1,0},{2,3},{3,2},{4,5},{5,4},{6,7},{7,6},{8,9},{9,8},{10,11... | collective-permute-start | bytes 3538952 | tf_op jit(solution)/shard_map/ppermute | solution.py:41
  15.0 0.4 collective-permute-done.expand_far
  15.4 0.0 copy-start.3
  15.4 1.0 copy-done.3
  16.4 15.4 %all-to-all-done.panels = bf16[16,32,768]{2,1,0:T(8,128)(2,1)S(1)} async-done(((bf16[16,32,768]{2,1,0:T(8,128)(2,1)}), bf16[16,32,768]{2,1,0:T(8,128)(2,1)S(1)}, u32[]{:S(2)}, u32[]{:S(2)}) %all-to-all-start) | async-done | bytes 786464 | tf_op jit(solution)/shard_map/all_to_all | solution.py:55
  31.8 0.0 copy-start.4
  31.8 1.3 copy-done.4
  33.0 0.8 shard_map.75
  33.9 0.0 copy-start.6
  33.9 0.9 copy-done.6
  34.8 12.1 %all-to-all-start.1 = ((bf16[16,16,1536]{2,1,0:T(8,128)(2,1)}), bf16[16,16,1536]{2,1,0:T(8,128)(2,1)S(1)}, u32[]{:S(2)}, u32[]{:S(2)}) async-start(bf16[16,16,1536]{2,1,0:T(8,128)(2,1)} %copy-done.6), calls=%async_computation.1 | async-start | bytes 1572864 | tf_op jit(solution)/shard_map/all_to_all | solution.py:55
  46.9 0.0 collective-permute-done.1.project_far
  46.9 3.0 %shard_map.76 = bf16[8,16,1536]{2,1,0:T(8,128)(2,1)} custom-call(s32[1]{0:T(128)} %bitcast.which, bf16[16,32,768]{2,1,0:T(8,128)(2,1)S(1)} %all-to-all-done.panels, bf16[768,768]{1,0:T(8,128)(2,1)S(1)} %copy-done, bf16[768,768]{1,0:T(8,128)(2,1)} %collective-permute-done.1.project_far), custom_call_target="tpu_custom_call" | custom-call | flops 301989888 | bytes 3538948 | tf_op jit(solution)/shard_map/pallas_call | solution.py:85
  49.9 4.9 %collective-permute-start.2 = (bf16[8,16,1536]{2,1,0:T(8,128)(2,1)}, bf16[8,16,1536]{2,1,0:T(8,128)(2,1)}, u32[]{:S(2)}, u32[]{:S(2)}) collective-permute-start(bf16[8,16,1536]{2,1,0:T(8,128)(2,1)} %shard_map.76), channel_id=1, source_target_pairs={{0,256},{32,288},{64,320},{96,352},{128,384},{160,416},{192,448},{... | collective-permute-start | bytes 1179656 | tf_op jit(solution)/shard_map/ppermute | solution.py:51
  54.8 2.2 %shard_map.77.mine = f32[8,16,1536]{2,1,0:T(8,128)S(1)} custom-call(s32[1]{0:T(128)} %bitcast.which, bf16[16,32,768]{2,1,0:T(8,128)(2,1)S(1)} %all-to-all-done.panels, bf16[768,768]{1,0:T(8,128)(2,1)S(1)} %copy-done, bf16[768,768]{1,0:T(8,128)(2,1)} %collective-permute-done.1.project_far), custom_call_target="tpu_custom_call" | custom-call | flops 301989888 | bytes 3932164 | tf_op jit(solution)/shard_map/pallas_call | solution.py:85
  57.0 10.5 %all-to-all-done.1.sums = bf16[16,16,1536]{2,1,0:T(8,128)(2,1)S(1)} async-done(((bf16[16,16,1536]{2,1,0:T(8,128)(2,1)}), bf16[16,16,1536]{2,1,0:T(8,128)(2,1)S(1)}, u32[]{:S(2)}, u32[]{:S(2)}) %all-to-all-start.1) | async-done | bytes 786464 | tf_op jit(solution)/shard_map/all_to_all | solution.py:55
  67.4 0.2 shard_map.78
  67.6 1.0 collective-permute-done.2.came
  68.6 1.1 shard_map.79
  69.7 26.7 %all_to_all.25.mixed = bf16[8,32,1536]{2,1,0:T(8,128)(2,1)S(1)} all-to-all(bf16[8,32,1536]{2,1,0:T(8,128)(2,1)S(1)} %shard_map.79), channel_id=1, replica_groups={{0,32,64,96,128,160,192,224},{256,288,320,352,384,416,448,480},{1,33,65..., dimensions={0} | all-to-all | bytes 1572864 | tf_op jit(solution)/shard_map/all_to_all | solution.py:55
  96.5 1.0 shard_map.80
  97.5 0.0 copy-start.7
  97.5 3.3 %collective-permute-start.3 = (bf16[8,16,1536]{2,1,0:T(8,128)(2,1)S(1)}, bf16[8,16,1536]{2,1,0:T(8,128)(2,1)S(1)}, u32[]{:S(2)}, u32[]{:S(2)}) collective-permute-start(bf16[8,16,1536]{2,1,0:T(8,128)(2,1)S(1)} %get-tuple-element.31.act), channel_id=1, source_target_pairs={{0,256},{32,288},{64,320},{96,352},{128,384},{160,416},{192,448},{... | collective-permute-start | bytes 1179656 | tf_op jit(solution)/shard_map/ppermute | solution.py:51
  100.8 4.9 %all-to-all-start.3 = ((bf16[16,16,1536]{2,1,0:T(8,128)(2,1)}), bf16[16,16,1536]{2,1,0:T(8,128)(2,1)S(1)}, u32[]{:S(2)}, u32[]{:S(2)}) async-start(bf16[16,16,1536]{2,1,0:T(8,128)(2,1)} %get-tuple-element.30), calls=%async_computation.3 | async-start | bytes 1572864 | tf_op jit(solution)/shard_map/all_to_all | solution.py:55
  105.7 0.0 copy-done.7
  105.7 3.5 %collective-permute-done.3.act_far = bf16[8,16,1536]{2,1,0:T(8,128)(2,1)S(1)} collective-permute-done((bf16[8,16,1536]{2,1,0:T(8,128)(2,1)S(1)}, bf16[8,16,1536]{2,1,0:T(8,128)(2,1)S(1)}, u32[]{:S(2)}, u32[]{:S(2)}) %collective-permute-start.3) | collective-permute-done | bytes 393248 | tf_op jit(solution)/shard_map/ppermute | solution.py:51
  109.2 0.0 copy-start.9
  109.2 0.8 copy-done.9
  109.9 0.0 copy-start.8
  109.9 1.0 copy-done.8
  110.9 0.0 copy-start.10
  110.9 1.0 copy-done.10
  111.9 2.1 %shard_map.81 = (bf16[16,16,768]{2,1,0:T(8,128)(2,1)S(1)}, bf16[16,16,768]{2,1,0:T(8,128)(2,1)S(1)}, bf16[16,16,768]{2,1,0:T(8,128)(2,1)S(1)}) custom-call(s32[1]{0:T(128)} %bitcast.which, bf16[8,16,1536]{2,1,0:T(8,128)(2,1)S(1)} %copy-done.8, bf16[8,16,1536]{2,1,0:T(8,128)(2,1)S(1)} %copy-done.10, bf16[768,768]{1,0:T(8,128)(2,1)S(1)} %copy-done, ...), custom_call_target="tpu_custom_call" | custom-call | flops 60397977600 | bytes 4325380 | tf_op jit(solution)/shard_map/pallas_call | solution.py:85
  114.0 0.0 copy-start.11
  114.0 0.8 copy-done.11
  114.7 11.5 %all-to-all-done.3.grad = bf16[16,16,1536]{2,1,0:T(8,128)(2,1)S(1)} async-done(((bf16[16,16,1536]{2,1,0:T(8,128)(2,1)}), bf16[16,16,1536]{2,1,0:T(8,128)(2,1)S(1)}, u32[]{:S(2)}, u32[]{:S(2)}) %all-to-all-start.3) | async-done | bytes 786464 | tf_op jit(solution)/shard_map/all_to_all | solution.py:55
  126.2 0.0 copy-start.2
  126.2 1.3 copy-done.2
  127.5 0.0 copy-start.5
  127.5 1.3 copy-done.5
  128.7 1.7 %shard_map.82 = bf16[16,32,768]{2,1,0:T(8,128)(2,1)} custom-call(bf16[16,16,1536]{2,1,0:T(8,128)(2,1)S(1)} %all-to-all-done.3.grad, bf16[16,16,768]{2,1,0:T(8,128)(2,1)S(1)} %get-tuple-element.32.out_parts, bf16[768,768]{1,0:T(8,128)(2,1)S(1)} %copy-done.2, bf16[768,768]{1,0:T(8,128)(2,1)S(1)} %copy-done.5), custom_call_target="tpu_custom_call" | custom-call | flops 603979776 | bytes 4325376 | tf_op jit(solution)/shard_map/pallas_call | solution.py:85
  130.4 6.3 %all-to-all-start.4 = ((bf16[16,32,768]{2,1,0:T(8,128)(2,1)}), bf16[16,32,768]{2,1,0:T(8,128)(2,1)S(1)}, u32[]{:S(2)}, u32[]{:S(2)}) async-start(bf16[16,32,768]{2,1,0:T(8,128)(2,1)} %shard_map.82), calls=%async_computation.4 | async-start | bytes 1572864 | tf_op jit(solution)/shard_map/all_to_all | solution.py:55
  136.8 1.9 %collective-permute-start.4 = (bf16[16,32,768]{2,1,0:T(8,128)(2,1)S(1)}, bf16[16,32,768]{2,1,0:T(8,128)(2,1)S(1)}, u32[]{:S(2)}, u32[]{:S(2)}) collective-permute-start(bf16[16,32,768]{2,1,0:T(8,128)(2,1)S(1)} %all-to-all-done.panels), channel_id=1, source_target_pairs={{0,1},{1,0},{2,3},{3,2},{4,5},{5,4},{6,7},{7,6},{8,9},{9,8},{10,11... | collective-permute-start | bytes 2359304 | tf_op jit(solution)/shard_map/ppermute | solution.py:41
  138.7 2.4 %collective-permute-start.5 = (bf16[16,16,768]{2,1,0:T(8,128)(2,1)S(1)}, bf16[16,16,768]{2,1,0:T(8,128)(2,1)S(1)}, u32[]{:S(2)}, u32[]{:S(2)}) collective-permute-start(bf16[16,16,768]{2,1,0:T(8,128)(2,1)S(1)} %get-tuple-element.35), channel_id=1, source_target_pairs={{0,1},{1,0},{2,3},{3,2},{4,5},{5,4},{6,7},{7,6},{8,9},{9,8},{10,11... | collective-permute-start | bytes 1179656 | tf_op jit(solution)/shard_map/ppermute | solution.py:41
  141.1 0.1 shard_map.83
  141.2 1.9 %collective-permute-start.6 = (bf16[16,16,768]{2,1,0:T(8,128)(2,1)S(1)}, bf16[16,16,768]{2,1,0:T(8,128)(2,1)S(1)}, u32[]{:S(2)}, u32[]{:S(2)}) collective-permute-start(bf16[16,16,768]{2,1,0:T(8,128)(2,1)S(1)} %get-tuple-element.38), channel_id=1, source_target_pairs={{0,1},{1,0},{2,3},{3,2},{4,5},{5,4},{6,7},{7,6},{8,9},{9,8},{10,11... | collective-permute-start | bytes 1179656 | tf_op jit(solution)/shard_map/ppermute | solution.py:41
  143.1 0.0 collective-permute-done.5.act_got
  143.1 1.7 %collective-permute-done.6.grad_got = bf16[16,16,768]{2,1,0:T(8,128)(2,1)S(1)} collective-permute-done((bf16[16,16,768]{2,1,0:T(8,128)(2,1)S(1)}, bf16[16,16,768]{2,1,0:T(8,128)(2,1)S(1)}, u32[]{:S(2)}, u32[]{:S(2)}) %collective-permute-start.6) | collective-permute-done | bytes 393248 | tf_op jit(solution)/shard_map/ppermute | solution.py:41
  144.8 0.0 collective-permute-done.4.panels_far
  144.8 0.0 copy-start.12
  144.8 1.0 copy-done.12
  145.8 2.4 %shard_map.84 = (bf16[768,768]{1,0:T(8,128)(2,1)}, bf16[768,768]{1,0:T(8,128)(2,1)}) custom-call(bf16[16,32,768]{2,1,0:T(8,128)(2,1)S(1)} %all-to-all-done.panels, bf16[16,32,768]{2,1,0:T(8,128)(2,1)S(1)} %collective-permute-done.4.panels_far, bf16[16,16,768]{2,1,0:T(8,128)(2,1)S(1)} %copy-done.12, bf16[16,16,768]{2,1,0:T(8,128)(2,1)S(1)} %collective-permute-done.5.act_got, ...), custom_call_target="tpu_custom_call" | custom-call | flops 1207959552 | bytes 5505024 | tf_op jit(solution)/shard_map/pallas_call | solution.py:85
  148.2 7.0 %all-to-all-done.4.sums = bf16[16,32,768]{2,1,0:T(8,128)(2,1)S(1)} async-done(((bf16[16,32,768]{2,1,0:T(8,128)(2,1)}), bf16[16,32,768]{2,1,0:T(8,128)(2,1)S(1)}, u32[]{:S(2)}, u32[]{:S(2)}) %all-to-all-start.4) | async-done | bytes 786464 | tf_op jit(solution)/shard_map/all_to_all | solution.py:55
  155.2 0.7 shard_map.85
Async XLA Ops:
  1.4 9.2 %copy-start.1 = (bf16[768,768]{1,0:T(8,128)(2,1)S(1)}, bf16[768,768]{1,0:T(8,128)(2,1)}, u32[]{:S(2)}) copy-start(bf16[768,768]{1,0:T(8,128)(2,1)} %expand.3) | copy-start | bytes 3538948
  1.4 11.2 %copy-start = (bf16[768,768]{1,0:T(8,128)(2,1)S(1)}, bf16[768,768]{1,0:T(8,128)(2,1)}, u32[]{:S(2)}) copy-start(bf16[768,768]{1,0:T(8,128)(2,1)} %project.5) | copy-start | bytes 3538948
  2.4 29.4 %all-to-all-start = ((bf16[16,32,768]{2,1,0:T(8,128)(2,1)}), bf16[16,32,768]{2,1,0:T(8,128)(2,1)S(1)}, u32[]{:S(2)}, u32[]{:S(2)}) async-start(bf16[16,32,768]{2,1,0:T(8,128)(2,1)} %broadcast_in_dim.2), calls=%async_computation | async-start | bytes 1572864 | tf_op jit(solution)/shard_map/all_to_all | solution.py:55
  10.6 4.7 %collective-permute-start = (bf16[768,768]{1,0:T(8,128)(2,1)S(1)}, bf16[768,768]{1,0:T(8,128)(2,1)S(1)}, u32[]{:S(2)}, u32[]{:S(2)}) collective-permute-start(bf16[768,768]{1,0:T(8,128)(2,1)S(1)} %copy-done.1), channel_id=1, source_target_pairs={{0,1},{1,0},{2,3},{3,2},{4,5},{5,4},{6,7},{7,6},{8,9},{9,8},{10,11... | collective-permute-start | bytes 3538952 | tf_op jit(solution)/shard_map/ppermute | solution.py:41
  12.6 34.3 %collective-permute-start.1 = (bf16[768,768]{1,0:T(8,128)(2,1)S(1)}, bf16[768,768]{1,0:T(8,128)(2,1)}, u32[]{:S(2)}, u32[]{:S(2)}) collective-permute-start(bf16[768,768]{1,0:T(8,128)(2,1)S(1)} %copy-done), channel_id=1, source_target_pairs={{0,1},{1,0},{2,3},{3,2},{4,5},{5,4},{6,7},{7,6},{8,9},{9,8},{10,11... | collective-permute-start | bytes 3538952 | tf_op jit(solution)/shard_map/ppermute | solution.py:41
  15.4 1.0 copy-start.3
  31.8 1.3 copy-start.4
  33.9 0.9 copy-start.6
  34.8 32.7 %all-to-all-start.1 = ((bf16[16,16,1536]{2,1,0:T(8,128)(2,1)}), bf16[16,16,1536]{2,1,0:T(8,128)(2,1)S(1)}, u32[]{:S(2)}, u32[]{:S(2)}) async-start(bf16[16,16,1536]{2,1,0:T(8,128)(2,1)} %copy-done.6), calls=%async_computation.1 | async-start | bytes 1572864 | tf_op jit(solution)/shard_map/all_to_all | solution.py:55
  49.9 18.8 %collective-permute-start.2 = (bf16[8,16,1536]{2,1,0:T(8,128)(2,1)}, bf16[8,16,1536]{2,1,0:T(8,128)(2,1)}, u32[]{:S(2)}, u32[]{:S(2)}) collective-permute-start(bf16[8,16,1536]{2,1,0:T(8,128)(2,1)} %shard_map.76), channel_id=1, source_target_pairs={{0,256},{32,288},{64,320},{96,352},{128,384},{160,416},{192,448},{... | collective-permute-start | bytes 1179656 | tf_op jit(solution)/shard_map/ppermute | solution.py:51
  97.5 8.2 %copy-start.7 = (bf16[8,16,1536]{2,1,0:T(8,128)(2,1)}, bf16[8,16,1536]{2,1,0:T(8,128)(2,1)S(1)}, u32[]{:S(2)}) copy-start(bf16[8,16,1536]{2,1,0:T(8,128)(2,1)S(1)} %get-tuple-element.31.act) | copy-start | bytes 1179652
  97.5 11.7 %collective-permute-start.3 = (bf16[8,16,1536]{2,1,0:T(8,128)(2,1)S(1)}, bf16[8,16,1536]{2,1,0:T(8,128)(2,1)S(1)}, u32[]{:S(2)}, u32[]{:S(2)}) collective-permute-start(bf16[8,16,1536]{2,1,0:T(8,128)(2,1)S(1)} %get-tuple-element.31.act), channel_id=1, source_target_pairs={{0,256},{32,288},{64,320},{96,352},{128,384},{160,416},{192,448},{... | collective-permute-start | bytes 1179656 | tf_op jit(solution)/shard_map/ppermute | solution.py:51
  100.8 25.4 %all-to-all-start.3 = ((bf16[16,16,1536]{2,1,0:T(8,128)(2,1)}), bf16[16,16,1536]{2,1,0:T(8,128)(2,1)S(1)}, u32[]{:S(2)}, u32[]{:S(2)}) async-start(bf16[16,16,1536]{2,1,0:T(8,128)(2,1)} %get-tuple-element.30), calls=%async_computation.3 | async-start | bytes 1572864 | tf_op jit(solution)/shard_map/all_to_all | solution.py:55
  109.2 0.8 copy-start.9
  109.9 1.0 copy-start.8
  110.9 1.0 copy-start.10
  114.0 0.8 copy-start.11
  126.2 1.3 copy-start.2
  127.5 1.3 copy-start.5
  130.4 24.8 %all-to-all-start.4 = ((bf16[16,32,768]{2,1,0:T(8,128)(2,1)}), bf16[16,32,768]{2,1,0:T(8,128)(2,1)S(1)}, u32[]{:S(2)}, u32[]{:S(2)}) async-start(bf16[16,32,768]{2,1,0:T(8,128)(2,1)} %shard_map.82), calls=%async_computation.4 | async-start | bytes 1572864 | tf_op jit(solution)/shard_map/all_to_all | solution.py:55
  136.8 8.0 %collective-permute-start.4 = (bf16[16,32,768]{2,1,0:T(8,128)(2,1)S(1)}, bf16[16,32,768]{2,1,0:T(8,128)(2,1)S(1)}, u32[]{:S(2)}, u32[]{:S(2)}) collective-permute-start(bf16[16,32,768]{2,1,0:T(8,128)(2,1)S(1)} %all-to-all-done.panels), channel_id=1, source_target_pairs={{0,1},{1,0},{2,3},{3,2},{4,5},{5,4},{6,7},{7,6},{8,9},{9,8},{10,11... | collective-permute-start | bytes 2359304 | tf_op jit(solution)/shard_map/ppermute | solution.py:41
  138.7 4.4 %collective-permute-start.5 = (bf16[16,16,768]{2,1,0:T(8,128)(2,1)S(1)}, bf16[16,16,768]{2,1,0:T(8,128)(2,1)S(1)}, u32[]{:S(2)}, u32[]{:S(2)}) collective-permute-start(bf16[16,16,768]{2,1,0:T(8,128)(2,1)S(1)} %get-tuple-element.35), channel_id=1, source_target_pairs={{0,1},{1,0},{2,3},{3,2},{4,5},{5,4},{6,7},{7,6},{8,9},{9,8},{10,11... | collective-permute-start | bytes 1179656 | tf_op jit(solution)/shard_map/ppermute | solution.py:41
  141.2 3.6 %collective-permute-start.6 = (bf16[16,16,768]{2,1,0:T(8,128)(2,1)S(1)}, bf16[16,16,768]{2,1,0:T(8,128)(2,1)S(1)}, u32[]{:S(2)}, u32[]{:S(2)}) collective-permute-start(bf16[16,16,768]{2,1,0:T(8,128)(2,1)S(1)} %get-tuple-element.38), channel_id=1, source_target_pairs={{0,1},{1,0},{2,3},{3,2},{4,5},{5,4},{6,7},{7,6},{8,9},{9,8},{10,11... | collective-permute-start | bytes 1179656 | tf_op jit(solution)/shard_map/ppermute | solution.py:41
  144.8 1.0 copy-start.12

commit v4 on v3

--- a/solution.py
+++ b/solution.py
@@ -12,8 +12,11 @@
 CUBIC = 0.044715
 CORES = 2
 PAIR = 2
-HIDE_FRONT = 1
+HIDE_FRONT = 5
 HIDE_ACT = 1
+HIDE_PRE = 0
+HIDE_TOK = 0
+HIDE_SWAP = 1
 HIDE_BACK = 100
 F32, BF16 = jnp.float32, jnp.bfloat16
 VMEM_BYTES = 12 << 20
@@ -210,7 +213,7 @@
     pre = call(
         pre_kernel,
         [array(rows, share, wide)],
-        work,
+        work * HIDE_PRE,
         panels,
         expand,
         expand_far,
@@ -255,7 +258,7 @@
         project_far,
     )
     parts = call(
-        tok_kernel, [array(chips, 2 * own, features)], work, grad, out_parts, expand, expand_far
+        tok_kernel, [array(chips, 2 * own, features)], work * HIDE_TOK, grad, out_parts, expand, expand_far
     )
     sums = exchange(parts, "col", over_col)
     act_got = swap_cores(act_send)

time: 157 us -> 154 us (0.981)
  local copies, waits for them, and re-layouts: 11.2 us -> 9.53 us
    unnamed x26 -> x32, local copies, waits for them, and re-layouts: 10.2 us -> 8.57 us
  transfers between devices with their start and end apart: 11 -> 11, of which waited for: 8 -> 8; matrix products, arithmetic and copies ran while one was open for 0% -> 0% of each run, Pallas kernels for 7% -> 8%
where the time goes in v4:
time: 154 us; the launch traced here: 153 us
  waiting for transfers between devices  50.2 us (33%)
  starting transfers between devices  50 us (32%)
  blocking collectives  27.9 us (18%)
  Pallas kernels  13.7 us (9%)
  local copies, waits for them, and re-layouts  9.53 us (6%)
    all_to_all x4, waiting for transfers between devices, exchange(): return lax.all_to_all(parts, axis, 0, 0, axis_index_groups=groups)  43.6 us
    all_to_all x4, starting transfers between devices, exchange(): return lax.all_to_all(parts, axis, 0, 0, axis_index_groups=groups)  32.7 us
    all_to_all x1, blocking collectives, exchange(): return lax.all_to_all(parts, axis, 0, 0, axis_index_groups=groups)  27.9 us
    pallas_call x11, Pallas kernels, call(): pl.pallas_call(kernel, out_shape=outs[0] if one else outs, in_specs=[ANYW...  13.7 us
    ppermute x5, starting transfers between devices, swap_cores(): return lax.ppermute(block, 'col', [(at, at ^ 1) for at in range(cols)])  10.6 us
    unnamed x32, local copies, waits for them, and re-layouts  8.57 us
    ppermute x2, starting transfers between devices, swap_halves(): lax.ppermute(block, 'row', [(at, (at + rows // PAIR) % rows) for at in ra...  6.79 us
    ppermute x2, waiting for transfers between devices, swap_halves(): lax.ppermute(block, 'row', [(at, (at + rows // PAIR) % rows) for at in ra...  4.5 us
  transfers between devices with their start and end apart: 11, of which 8 were waited for; matrix products, arithmetic and copies ran while one was open for 0% of the time, Pallas kernels for 8%

profile of v4, /device:TPU:64, one launch (start us, length us, event | category | flops | bytes accessed | tf_op | source)
XLA Modules:
  0.0 153.1 jit_solution(4429345777593691545)
XLA Ops:
  0.6 0.8 pad_maximum_fusion
  1.4 0.0 copy-start
  1.4 1.0 broadcast_in_dim.2
  2.4 8.1 %all-to-all-start = ((bf16[16,32,768]{2,1,0:T(8,128)(2,1)}), bf16[16,32,768]{2,1,0:T(8,128)(2,1)S(1)}, u32[]{:S(2)}, u32[]{:S(2)}) async-start(bf16[16,32,768]{2,1,0:T(8,128)(2,1)} %broadcast_in_dim.2), calls=%async_computation | async-start | bytes 1572864 | tf_op jit(solution)/shard_map/all_to_all | solution.py:58
  10.5 0.0 copy-done
  10.5 1.9 %collective-permute-start = (bf16[768,768]{1,0:T(8,128)(2,1)S(1)}, bf16[768,768]{1,0:T(8,128)(2,1)S(1)}, u32[]{:S(2)}, u32[]{:S(2)}) collective-permute-start(bf16[768,768]{1,0:T(8,128)(2,1)S(1)} %copy-done), channel_id=1, source_target_pairs={{0,1},{1,0},{2,3},{3,2},{4,5},{5,4},{6,7},{7,6},{8,9},{9,8},{10,11... | collective-permute-start | bytes 3538952 | tf_op jit(solution)/shard_map/ppermute | solution.py:44
  12.4 2.4 %collective-permute-start.1 = (bf16[768,768]{1,0:T(8,128)(2,1)}, bf16[768,768]{1,0:T(8,128)(2,1)}, u32[]{:S(2)}, u32[]{:S(2)}) collective-permute-start(bf16[768,768]{1,0:T(8,128)(2,1)} %project.5), channel_id=1, source_target_pairs={{0,1},{1,0},{2,3},{3,2},{4,5},{5,4},{6,7},{7,6},{8,9},{9,8},{10,11... | collective-permute-start | bytes 3538952 | tf_op jit(solution)/shard_map/ppermute | solution.py:44
  14.9 0.4 collective-permute-done.expand_far
  15.2 16.4 %all-to-all-done.panels = bf16[16,32,768]{2,1,0:T(8,128)(2,1)S(1)} async-done(((bf16[16,32,768]{2,1,0:T(8,128)(2,1)}), bf16[16,32,768]{2,1,0:T(8,128)(2,1)S(1)}, u32[]{:S(2)}, u32[]{:S(2)}) %all-to-all-start) | async-done | bytes 786464 | tf_op jit(solution)/shard_map/all_to_all | solution.py:58
  31.6 0.0 copy-start.1
  31.6 0.8 shard_map.75
  32.5 0.0 copy-start.3
  32.5 0.9 copy-done.3
  33.4 12.1 %all-to-all-start.1 = ((bf16[16,16,1536]{2,1,0:T(8,128)(2,1)}), bf16[16,16,1536]{2,1,0:T(8,128)(2,1)}, u32[]{:S(2)}, u32[]{:S(2)}) async-start(bf16[16,16,1536]{2,1,0:T(8,128)(2,1)} %copy-done.3), calls=%async_computation.1 | async-start | bytes 1572864 | tf_op jit(solution)/shard_map/all_to_all | solution.py:58
  45.5 0.0 collective-permute-done.1.project_far
  45.5 0.0 copy-start.8
  45.5 1.3 copy-done.8
  46.8 2.9 %shard_map.76 = bf16[8,16,1536]{2,1,0:T(8,128)(2,1)} custom-call(s32[1]{0:T(128)} %bitcast.which, bf16[16,32,768]{2,1,0:T(8,128)(2,1)S(1)} %all-to-all-done.panels, bf16[768,768]{1,0:T(8,128)(2,1)S(1)} %copy-done.8, bf16[768,768]{1,0:T(8,128)(2,1)} %collective-permute-done.1.project_far), custom_call_target="tpu_custom_call" | custom-call | flops 1509949440 | bytes 3538948 | tf_op jit(solution)/shard_map/pallas_call | solution.py:88
  49.7 4.9 %collective-permute-start.2 = (bf16[8,16,1536]{2,1,0:T(8,128)(2,1)}, bf16[8,16,1536]{2,1,0:T(8,128)(2,1)S(1)}, u32[]{:S(2)}, u32[]{:S(2)}) collective-permute-start(bf16[8,16,1536]{2,1,0:T(8,128)(2,1)} %shard_map.76), channel_id=1, source_target_pairs={{0,256},{32,288},{64,320},{96,352},{128,384},{160,416},{192,448},{... | collective-permute-start | bytes 1179656 | tf_op jit(solution)/shard_map/ppermute | solution.py:54
  54.6 0.0 copy-done.1
  54.6 2.2 %shard_map.77.mine = f32[8,16,1536]{2,1,0:T(8,128)S(1)} custom-call(s32[1]{0:T(128)} %bitcast.which, bf16[16,32,768]{2,1,0:T(8,128)(2,1)S(1)} %all-to-all-done.panels, bf16[768,768]{1,0:T(8,128)(2,1)S(1)} %copy-done.8, bf16[768,768]{1,0:T(8,128)(2,1)} %collective-permute-done.1.project_far), custom_call_target="tpu_custom_call" | custom-call | flops 1509949440 | bytes 3932164 | tf_op jit(solution)/shard_map/pallas_call | solution.py:88
  56.8 0.0 copy-start.6
  56.8 0.9 copy-done.6
  57.7 8.4 %all-to-all-done.1.sums = bf16[16,16,1536]{2,1,0:T(8,128)(2,1)} async-done(((bf16[16,16,1536]{2,1,0:T(8,128)(2,1)}), bf16[16,16,1536]{2,1,0:T(8,128)(2,1)}, u32[]{:S(2)}, u32[]{:S(2)}) %all-to-all-start.1) | async-done | bytes 786464 | tf_op jit(solution)/shard_map/all_to_all | solution.py:58
  66.1 0.0 copy-start.7
  66.2 1.4 shard_map.78
  67.5 0.2 collective-permute-done.2.came
  67.7 0.0 copy-done.7
  67.7 0.1 shard_map.79
  67.8 27.9 %all_to_all.25.mixed = bf16[8,32,1536]{2,1,0:T(8,128)(2,1)S(1)} all-to-all(bf16[8,32,1536]{2,1,0:T(8,128)(2,1)S(1)} %shard_map.79), channel_id=1, replica_groups={{0,32,64,96,128,160,192,224},{256,288,320,352,384,416,448,480},{1,33,65..., dimensions={0} | all-to-all | bytes 1572864 | tf_op jit(solution)/shard_map/all_to_all | solution.py:58
  95.7 0.1 shard_map.80
  95.8 0.0 copy-start.5
  95.8 0.9 copy-done.5
  96.7 0.0 copy-start.12
  96.7 1.9 %collective-permute-start.3 = (bf16[8,16,1536]{2,1,0:T(8,128)(2,1)S(1)}, bf16[8,16,1536]{2,1,0:T(8,128)(2,1)}, u32[]{:S(2)}, u32[]{:S(2)}) collective-permute-start(bf16[8,16,1536]{2,1,0:T(8,128)(2,1)S(1)} %get-tuple-element.31.act), channel_id=1, source_target_pairs={{0,256},{32,288},{64,320},{96,352},{128,384},{160,416},{192,448},{... | collective-permute-start | bytes 1179656 | tf_op jit(solution)/shard_map/ppermute | solution.py:54
  98.6 6.3 %all-to-all-start.3 = ((bf16[16,16,1536]{2,1,0:T(8,128)(2,1)}), bf16[16,16,1536]{2,1,0:T(8,128)(2,1)S(1)}, u32[]{:S(2)}, u32[]{:S(2)}) async-start(bf16[16,16,1536]{2,1,0:T(8,128)(2,1)} %copy-done.5), calls=%async_computation.3 | async-start | bytes 1572864 | tf_op jit(solution)/shard_map/all_to_all | solution.py:58
  104.9 0.0 copy-done.12
  104.9 4.4 %collective-permute-done.3.act_far = bf16[8,16,1536]{2,1,0:T(8,128)(2,1)} collective-permute-done((bf16[8,16,1536]{2,1,0:T(8,128)(2,1)S(1)}, bf16[8,16,1536]{2,1,0:T(8,128)(2,1)}, u32[]{:S(2)}, u32[]{:S(2)}) %collective-permute-start.3) | collective-permute-done | bytes 393248 | tf_op jit(solution)/shard_map/ppermute | solution.py:54
  109.3 0.0 copy-start.9
  109.3 1.3 copy-done.9
  110.5 0.0 copy-start.13
  110.5 1.0 copy-done.13
  111.5 2.2 %shard_map.81 = (bf16[16,16,768]{2,1,0:T(8,128)(2,1)S(1)}, bf16[16,16,768]{2,1,0:T(8,128)(2,1)S(1)}, bf16[16,16,768]{2,1,0:T(8,128)(2,1)S(1)}) custom-call(s32[1]{0:T(128)} %bitcast.which, bf16[8,16,1536]{2,1,0:T(8,128)(2,1)S(1)} %copy-done.13, bf16[8,16,1536]{2,1,0:T(8,128)(2,1)} %collective-permute-done.3.act_far, bf16[768,768]{1,0:T(8,128)(2,1)S(1)} %copy-done.9, ...), custom_call_target="tpu_custom_call" | custom-call | flops 60397977600 | bytes 4325380 | tf_op jit(solution)/shard_map/pallas_call | solution.py:88
  113.7 0.0 copy-start.10
  113.7 0.8 copy-done.10
  114.5 0.7 copy-done.14
  115.2 10.9 %all-to-all-done.3.grad = bf16[16,16,1536]{2,1,0:T(8,128)(2,1)S(1)} async-done(((bf16[16,16,1536]{2,1,0:T(8,128)(2,1)}), bf16[16,16,1536]{2,1,0:T(8,128)(2,1)S(1)}, u32[]{:S(2)}, u32[]{:S(2)}) %all-to-all-start.3) | async-done | bytes 786464 | tf_op jit(solution)/shard_map/all_to_all | solution.py:58
  126.1 0.8 shard_map.82
  127.0 0.0 copy-start.4
  127.0 0.9 copy-done.4
  127.9 6.1 %all-to-all-start.4 = ((bf16[16,32,768]{2,1,0:T(8,128)(2,1)}), bf16[16,32,768]{2,1,0:T(8,128)(2,1)S(1)}, u32[]{:S(2)}, u32[]{:S(2)}) async-start(bf16[16,32,768]{2,1,0:T(8,128)(2,1)} %copy-done.4), calls=%async_computation.4 | async-start | bytes 1572864 | tf_op jit(solution)/shard_map/all_to_all | solution.py:58
  134.0 0.0 copy-done.2
  134.0 1.9 %collective-permute-start.4 = (bf16[16,32,768]{2,1,0:T(8,128)(2,1)S(1)}, bf16[16,32,768]{2,1,0:T(8,128)(2,1)S(1)}, u32[]{:S(2)}, u32[]{:S(2)}) collective-permute-start(bf16[16,32,768]{2,1,0:T(8,128)(2,1)S(1)} %copy-done.2), channel_id=1, source_target_pairs={{0,1},{1,0},{2,3},{3,2},{4,5},{5,4},{6,7},{7,6},{8,9},{9,8},{10,11... | collective-permute-start | bytes 2359304 | tf_op jit(solution)/shard_map/ppermute | solution.py:44
  135.9 0.0 copy-done.11
  135.9 2.4 %collective-permute-start.5 = (bf16[16,16,768]{2,1,0:T(8,128)(2,1)S(1)}, bf16[16,16,768]{2,1,0:T(8,128)(2,1)S(1)}, u32[]{:S(2)}, u32[]{:S(2)}) collective-permute-start(bf16[16,16,768]{2,1,0:T(8,128)(2,1)S(1)} %copy-done.11), channel_id=1, source_target_pairs={{0,1},{1,0},{2,3},{3,2},{4,5},{5,4},{6,7},{7,6},{8,9},{9,8},{10,11... | collective-permute-start | bytes 1179656 | tf_op jit(solution)/shard_map/ppermute | solution.py:44
  138.3 0.1 shard_map.83
  138.4 1.9 %collective-permute-start.6 = (bf16[16,16,768]{2,1,0:T(8,128)(2,1)S(1)}, bf16[16,16,768]{2,1,0:T(8,128)(2,1)S(1)}, u32[]{:S(2)}, u32[]{:S(2)}) collective-permute-start(bf16[16,16,768]{2,1,0:T(8,128)(2,1)S(1)} %get-tuple-element.38), channel_id=1, source_target_pairs={{0,1},{1,0},{2,3},{3,2},{4,5},{5,4},{6,7},{7,6},{8,9},{9,8},{10,11... | collective-permute-start | bytes 1179656 | tf_op jit(solution)/shard_map/ppermute | solution.py:44
  140.3 0.0 collective-permute-done.5.act_got
  140.3 1.7 %collective-permute-done.6.grad_got = bf16[16,16,768]{2,1,0:T(8,128)(2,1)S(1)} collective-permute-done((bf16[16,16,768]{2,1,0:T(8,128)(2,1)S(1)}, bf16[16,16,768]{2,1,0:T(8,128)(2,1)S(1)}, u32[]{:S(2)}, u32[]{:S(2)}) %collective-permute-start.6) | collective-permute-done | bytes 393248 | tf_op jit(solution)/shard_map/ppermute | solution.py:44
  142.0 0.0 collective-permute-done.4.panels_far
  142.0 0.0 copy-done.15
  142.0 2.4 %shard_map.84 = (bf16[768,768]{1,0:T(8,128)(2,1)}, bf16[768,768]{1,0:T(8,128)(2,1)}) custom-call(bf16[16,32,768]{2,1,0:T(8,128)(2,1)S(1)} %copy-done.2, bf16[16,32,768]{2,1,0:T(8,128)(2,1)S(1)} %collective-permute-done.4.panels_far, bf16[16,16,768]{2,1,0:T(8,128)(2,1)S(1)} %copy-done.15, bf16[16,16,768]{2,1,0:T(8,128)(2,1)S(1)} %collective-permute-done.5.act_got, ...), custom_call_target="tpu_custom_call" | custom-call | flops 1207959552 | bytes 5505024 | tf_op jit(solution)/shard_map/pallas_call | solution.py:88
  144.5 7.9 %all-to-all-done.4.sums = bf16[16,32,768]{2,1,0:T(8,128)(2,1)S(1)} async-done(((bf16[16,32,768]{2,1,0:T(8,128)(2,1)}), bf16[16,32,768]{2,1,0:T(8,128)(2,1)S(1)}, u32[]{:S(2)}, u32[]{:S(2)}) %all-to-all-start.4) | async-done | bytes 786464 | tf_op jit(solution)/shard_map/all_to_all | solution.py:58
  152.4 0.7 shard_map.85
  (4 shorter events, 0.0 us)
Async XLA Ops:
  1.4 9.1 %copy-start = (bf16[768,768]{1,0:T(8,128)(2,1)S(1)}, bf16[768,768]{1,0:T(8,128)(2,1)}, u32[]{:S(2)}) copy-start(bf16[768,768]{1,0:T(8,128)(2,1)} %expand.3) | copy-start | bytes 3538948
  2.4 29.3 %all-to-all-start = ((bf16[16,32,768]{2,1,0:T(8,128)(2,1)}), bf16[16,32,768]{2,1,0:T(8,128)(2,1)S(1)}, u32[]{:S(2)}, u32[]{:S(2)}) async-start(bf16[16,32,768]{2,1,0:T(8,128)(2,1)} %broadcast_in_dim.2), calls=%async_computation | async-start | bytes 1572864 | tf_op jit(solution)/shard_map/all_to_all | solution.py:58
  10.5 4.7 %collective-permute-start = (bf16[768,768]{1,0:T(8,128)(2,1)S(1)}, bf16[768,768]{1,0:T(8,128)(2,1)S(1)}, u32[]{:S(2)}, u32[]{:S(2)}) collective-permute-start(bf16[768,768]{1,0:T(8,128)(2,1)S(1)} %copy-done), channel_id=1, source_target_pairs={{0,1},{1,0},{2,3},{3,2},{4,5},{5,4},{6,7},{7,6},{8,9},{9,8},{10,11... | collective-permute-start | bytes 3538952 | tf_op jit(solution)/shard_map/ppermute | solution.py:44
  12.4 33.1 %collective-permute-start.1 = (bf16[768,768]{1,0:T(8,128)(2,1)}, bf16[768,768]{1,0:T(8,128)(2,1)}, u32[]{:S(2)}, u32[]{:S(2)}) collective-permute-start(bf16[768,768]{1,0:T(8,128)(2,1)} %project.5), channel_id=1, source_target_pairs={{0,1},{1,0},{2,3},{3,2},{4,5},{5,4},{6,7},{7,6},{8,9},{9,8},{10,11... | collective-permute-start | bytes 3538952 | tf_op jit(solution)/shard_map/ppermute | solution.py:44
  31.6 23.0 %copy-start.1 = (bf16[16,32,768]{2,1,0:T(8,128)(2,1)}, bf16[16,32,768]{2,1,0:T(8,128)(2,1)S(1)}, u32[]{:S(2)}) copy-start(bf16[16,32,768]{2,1,0:T(8,128)(2,1)S(1)} %all-to-all-done.panels) | copy-start | bytes 2359300
  32.5 0.9 copy-start.3
  33.4 32.8 %all-to-all-start.1 = ((bf16[16,16,1536]{2,1,0:T(8,128)(2,1)}), bf16[16,16,1536]{2,1,0:T(8,128)(2,1)}, u32[]{:S(2)}, u32[]{:S(2)}) async-start(bf16[16,16,1536]{2,1,0:T(8,128)(2,1)} %copy-done.3), calls=%async_computation.1 | async-start | bytes 1572864 | tf_op jit(solution)/shard_map/all_to_all | solution.py:58
  45.5 1.3 copy-start.8
  49.7 18.0 %collective-permute-start.2 = (bf16[8,16,1536]{2,1,0:T(8,128)(2,1)}, bf16[8,16,1536]{2,1,0:T(8,128)(2,1)S(1)}, u32[]{:S(2)}, u32[]{:S(2)}) collective-permute-start(bf16[8,16,1536]{2,1,0:T(8,128)(2,1)} %shard_map.76), channel_id=1, source_target_pairs={{0,256},{32,288},{64,320},{96,352},{128,384},{160,416},{192,448},{... | collective-permute-start | bytes 1179656 | tf_op jit(solution)/shard_map/ppermute | solution.py:54
  56.8 0.9 copy-start.6
  66.1 1.5 %copy-start.7 = (f32[8,16,1536]{2,1,0:T(8,128)S(1)}, f32[8,16,1536]{2,1,0:T(8,128)}, u32[]{:S(2)}) copy-start(f32[8,16,1536]{2,1,0:T(8,128)} %copy-done.6) | copy-start | bytes 2359300
  95.8 0.9 copy-start.5
  96.7 8.2 %copy-start.12 = (bf16[8,16,1536]{2,1,0:T(8,128)(2,1)}, bf16[8,16,1536]{2,1,0:T(8,128)(2,1)S(1)}, u32[]{:S(2)}) copy-start(bf16[8,16,1536]{2,1,0:T(8,128)(2,1)S(1)} %get-tuple-element.31.act) | copy-start | bytes 1179652
  96.7 12.6 %collective-permute-start.3 = (bf16[8,16,1536]{2,1,0:T(8,128)(2,1)S(1)}, bf16[8,16,1536]{2,1,0:T(8,128)(2,1)}, u32[]{:S(2)}, u32[]{:S(2)}) collective-permute-start(bf16[8,16,1536]{2,1,0:T(8,128)(2,1)S(1)} %get-tuple-element.31.act), channel_id=1, source_target_pairs={{0,256},{32,288},{64,320},{96,352},{128,384},{160,416},{192,448},{... | collective-permute-start | bytes 1179656 | tf_op jit(solution)/shard_map/ppermute | solution.py:54
  98.6 27.5 %all-to-all-start.3 = ((bf16[16,16,1536]{2,1,0:T(8,128)(2,1)}), bf16[16,16,1536]{2,1,0:T(8,128)(2,1)S(1)}, u32[]{:S(2)}, u32[]{:S(2)}) async-start(bf16[16,16,1536]{2,1,0:T(8,128)(2,1)} %copy-done.5), calls=%async_computation.3 | async-start | bytes 1572864 | tf_op jit(solution)/shard_map/all_to_all | solution.py:58
  109.3 1.3 copy-start.9
  110.5 1.0 copy-start.13
  113.7 0.8 copy-start.10
  114.5 0.7 copy-start.14
  127.0 0.9 copy-start.4
  127.9 6.1 %copy-start.2 = (bf16[16,32,768]{2,1,0:T(8,128)(2,1)S(1)}, bf16[16,32,768]{2,1,0:T(8,128)(2,1)}, u32[]{:S(2)}) copy-start(bf16[16,32,768]{2,1,0:T(8,128)(2,1)} %copy-done.1) | copy-start | bytes 2359300
  127.9 8.1 %copy-start.11 = (bf16[16,16,768]{2,1,0:T(8,128)(2,1)S(1)}, bf16[16,16,768]{2,1,0:T(8,128)(2,1)}, u32[]{:S(2)}) copy-start(bf16[16,16,768]{2,1,0:T(8,128)(2,1)} %copy-done.10) | copy-start | bytes 1179652
  127.9 14.2 %copy-start.15 = (bf16[16,16,768]{2,1,0:T(8,128)(2,1)S(1)}, bf16[16,16,768]{2,1,0:T(8,128)(2,1)}, u32[]{:S(2)}) copy-start(bf16[16,16,768]{2,1,0:T(8,128)(2,1)} %copy-done.14) | copy-start | bytes 1179652
  127.9 24.5 %all-to-all-start.4 = ((bf16[16,32,768]{2,1,0:T(8,128)(2,1)}), bf16[16,32,768]{2,1,0:T(8,128)(2,1)S(1)}, u32[]{:S(2)}, u32[]{:S(2)}) async-start(bf16[16,32,768]{2,1,0:T(8,128)(2,1)} %copy-done.4), calls=%async_computation.4 | async-start | bytes 1572864 | tf_op jit(solution)/shard_map/all_to_all | solution.py:58
  134.0 8.0 %collective-permute-start.4 = (bf16[16,32,768]{2,1,0:T(8,128)(2,1)S(1)}, bf16[16,32,768]{2,1,0:T(8,128)(2,1)S(1)}, u32[]{:S(2)}, u32[]{:S(2)}) collective-permute-start(bf16[16,32,768]{2,1,0:T(8,128)(2,1)S(1)} %copy-done.2), channel_id=1, source_target_pairs={{0,1},{1,0},{2,3},{3,2},{4,5},{5,4},{6,7},{7,6},{8,9},{9,8},{10,11... | collective-permute-start | bytes 2359304 | tf_op jit(solution)/shard_map/ppermute | solution.py:44
  135.9 4.4 %collective-permute-start.5 = (bf16[16,16,768]{2,1,0:T(8,128)(2,1)S(1)}, bf16[16,16,768]{2,1,0:T(8,128)(2,1)S(1)}, u32[]{:S(2)}, u32[]{:S(2)}) collective-permute-start(bf16[16,16,768]{2,1,0:T(8,128)(2,1)S(1)} %copy-done.11), channel_id=1, source_target_pairs={{0,1},{1,0},{2,3},{3,2},{4,5},{5,4},{6,7},{7,6},{8,9},{9,8},{10,11... | collective-permute-start | bytes 1179656 | tf_op jit(solution)/shard_map/ppermute | solution.py:44
  138.4 3.6 %collective-permute-start.6 = (bf16[16,16,768]{2,1,0:T(8,128)(2,1)S(1)}, bf16[16,16,768]{2,1,0:T(8,128)(2,1)S(1)}, u32[]{:S(2)}, u32[]{:S(2)}) collective-permute-start(bf16[16,16,768]{2,1,0:T(8,128)(2,1)S(1)} %get-tuple-element.38), channel_id=1, source_target_pairs={{0,1},{1,0},{2,3},{3,2},{4,5},{5,4},{6,7},{7,6},{8,9},{9,8},{10,11... | collective-permute-start | bytes 1179656 | tf_op jit(solution)/shard_map/ppermute | solution.py:44

commit v5 on v3

--- a/solution.py
+++ b/solution.py
@@ -12,9 +12,8 @@
 CUBIC = 0.044715
 CORES = 2
 PAIR = 2
-HIDE_FRONT = 1
-HIDE_ACT = 1
-HIDE_BACK = 100
+UNIT = 600_000_000
+COSTS = dict(pre=(100, 10), theirs=(2.5, 1), mine=(2.5, 1), act=(0, 1), merge=(0, 1), grad=(0, 1), out=(100, 1), layer=(1, 1), tok=(0, 1), pack=(2.5, 1), grads=(2, 1), final=(0, 1))
 F32, BF16 = jnp.float32, jnp.bfloat16
 VMEM_BYTES = 12 << 20
 IN_SMEM = pl.BlockSpec(memory_space=pltpu.SMEM)
@@ -46,9 +45,9 @@
     return [list(range(at * step, (at + 1) * step)) for at in range(PAIR)]
 
 
-def swap_halves(block):
-    rows = lax.axis_size("row")
-    return lax.ppermute(block, "row", [(at, (at + rows // PAIR) % rows) for at in range(rows)])
+def swap_halves(block, axis):
+    count = lax.axis_size(axis)
+    return lax.ppermute(block, axis, [(at, (at + count // PAIR) % count) for at in range(count)])
 
 
 def exchange(parts, axis, groups):
@@ -79,9 +78,10 @@
     return jax.ShapeDtypeStruct(shape, dtype)
 
 
-def call(kernel, outs, flops, *args, ins=(), scratch=()):
+def call(kernel, name, outs, *args, ins=(), scratch=()):
     held = sum(math.prod(a.shape) * a.dtype.itemsize for a in (*args, *outs))
     one = len(outs) == 1
+    products, touched = COSTS[name]
     return pl.pallas_call(
         kernel,
         out_shape=outs[0] if one else outs,
@@ -91,7 +91,9 @@
         out_specs=IN_VMEM if one else [IN_VMEM] * len(outs),
         scratch_shapes=scratch,
         compiler_params=pltpu.CompilerParams(vmem_limit_bytes=VMEM_BYTES),
-        cost_estimate=pl.CostEstimate(flops=flops, bytes_accessed=held, transcendentals=0),
+        cost_estimate=pl.CostEstimate(
+            flops=int(products * UNIT), bytes_accessed=int(touched * held), transcendentals=0
+        ),
     )(*args)
 
 
@@ -146,47 +148,62 @@
         out[at] = grad
 
 
-def out_kernel(which, act, act_far, project, project_far, out, keep, send):
-    size, own, hidden = act.shape[0], out.shape[1], project.shape[0]
+def out_kernel(which, act, act_far, project, project_far, stay, leave, keep, send):
+    size, rows, hidden = act.shape[0], stay.shape[1], project.shape[0]
+    low = which[1] == 0
     for half, block in ((which[0], act[...]), (1 - which[0], act_far[...])):
         at = pl.ds(half * size, size)
         left, right = block[:, :, :hidden], block[:, :, hidden:]
         keep[at] = left
         send[at] = right
         terms = times(flat(left), project[...]) + times(flat(right), project_far[...])
-        out[at] = terms.astype(BF16).reshape(size, own, out.shape[2])
-
-
-def tok_kernel(grad, out_parts, expand, expand_far, out):
-    own, hidden = out_parts.shape[1], expand.shape[1]
+        terms = terms.reshape(size, 2 * rows, -1)
+        first, second = terms[:, :rows], terms[:, rows:]
+        stay[at] = jnp.where(low, first, second)
+        leave[at] = jnp.where(low, second, first).astype(BF16)
+
+
+def layer_kernel(stay, came, out):
+    out[...] = (stay[...] + came[...].astype(F32)).astype(BF16)
+
+
+def tok_kernel(grad, layer, expand, expand_far, out):
+    hidden = expand.shape[1]
+    chips, rows, features = layer.shape
     block = flat(grad[...])
     terms = times_turned(block[:, :hidden], expand[...]) + times_turned(block[:, hidden:], expand_far[...])
-    out[:, :own] = out_parts[...]
-    out[:, own:] = terms.astype(BF16).reshape(out.shape[0], own, out.shape[2])
-
-
-def pack_kernel(grad, keep, send):
+    parts = [layer[...].astype(F32), terms.reshape(chips, 2 * rows, features)]
+    out[...] = jnp.concatenate(parts, axis=1).astype(BF16)
+
+
+def pack_kernel(grad, act_send, keep, send):
     hidden = keep.shape[2]
     keep[...] = grad[:, :, :hidden]
-    send[...] = grad[:, :, hidden:]
-
-
-def weight_grads_kernel(factor, panels, panels_far, act, act_got, grad, grad_got, expand_grad, project_grad):
+    send[0] = act_send[...]
+    send[1] = grad[:, :, hidden:]
+
+
+def weight_grads_kernel(factor, panels, panels_far, act, grad, got, expand_grad, project_grad):
     own = panels.shape[1] // 2
 
     def sums(left, left_far, right, right_far):
         total = matmul(flat(left), flat(right), ((0,), (0,))) + matmul(flat(left_far), flat(right_far), ((0,), (0,)))
         return (total * factor).astype(BF16)
 
-    project_grad[...] = sums(act[...], act_got[...], panels[:, own:], panels_far[:, own:])
-    expand_grad[...] = sums(panels[:, :own], panels_far[:, :own], grad[...], grad_got[...])
+    project_grad[...] = sums(act[...], got[0], panels[:, own:], panels_far[:, own:])
+    expand_grad[...] = sums(panels[:, :own], panels_far[:, :own], grad[...], got[1])
 
 
 def final_kernel(sums, layer_out, token_grad):
-    own = layer_out.shape[0]
-    total = added(sums, 2 * own).astype(BF16)
-    layer_out[...] = total[:own]
-    token_grad[...] = total[own:]
+    members, rows = sums.shape[0], layer_out.shape[0] // 2
+    totals = []
+    for first in (0, members // 2):
+        total = sums[first].astype(F32)
+        for at in range(first + 1, first + members // 2):
+            total += sums[at].astype(F32)
+        totals.append(total)
+    layer_out[...] = jnp.concatenate([total[:rows] for total in totals], axis=0).astype(BF16)
+    token_grad[...] = (totals[0][rows:] + totals[1][rows:]).astype(BF16)
 
 
 def shards(tokens, expand, project, out_grad):
@@ -197,8 +214,7 @@
     wide, share, size = CORES * hidden, chips * own // rows, rows // PAIR
     over_col, along_z = col_groups(cols), row_groups(rows)
     factor = 1.0 / math.sqrt(own * cols)
-    work = 2 * chips * own * wide * features
-    which = (lax.axis_index("row") // size).astype(jnp.int32).reshape(1)
+    which = jnp.stack([lax.axis_index("row") // size, lax.axis_index("col") // (cols // PAIR)]).astype(jnp.int32)
 
     block = jnp.concatenate([tokens, out_grad], axis=0)
     copies = jnp.broadcast_to(block[None], (chips, *block.shape))
@@ -209,8 +225,8 @@
     half_sums = array(size, share, wide)
     pre = call(
         pre_kernel,
+        "pre",
         [array(rows, share, wide)],
-        work,
         panels,
         expand,
         expand_far,
@@ -221,8 +237,8 @@
     def back_terms(other, dtype, earlier):
         return call(
             functools.partial(back_kernel, other),
+            "theirs" if other else "mine",
             [array(size, share, wide, dtype=dtype)],
-            work // 2 * HIDE_FRONT,
             which,
             after(panels, earlier),
             project,
@@ -232,49 +248,49 @@
         )
 
     theirs = back_terms(True, BF16, pre)
-    came = swap_halves(theirs)
+    came = swap_halves(theirs, "row")
     mine = back_terms(False, F32, theirs)
     pre = exchange(pre, "row", None)
     act, slope = call(
-        act_kernel, [array(share, wide), array(share, wide, dtype=F32)], work * HIDE_ACT, pre
-    )
-    mixed = call(merge_kernel, [array(size, 2 * share, wide)], 0, mine, came, act)
+        act_kernel, "act", [array(share, wide), array(share, wide, dtype=F32)], pre
+    )
+    mixed = call(merge_kernel, "merge", [array(size, 2 * share, wide)], mine, came, act)
     mixed = exchange(mixed, "row", along_z)
-    act, grad = call(grad_kernel, [half_sums, array(rows, share, wide)], 0, mixed, slope)
-    act_far = swap_halves(act)
+    act, grad = call(grad_kernel, "grad", [half_sums, array(rows, share, wide)], mixed, slope)
+    act_far = swap_halves(act, "row")
     grad = exchange(grad, "row", None)
     held = array(chips, own, hidden)
-    out_parts, act, act_send = call(
+    stay, leave, act, act_send = call(
         out_kernel,
-        [array(chips, own, features), held, held],
-        work * HIDE_BACK,
+        "out",
+        [array(chips, own // 2, features, dtype=F32), array(chips, own // 2, features), held, held],
         which,
         act,
         act_far,
         project,
         project_far,
     )
+    layer_came = swap_halves(leave, "col")
+    layer = call(layer_kernel, "layer", [array(chips, own // 2, features)], stay, layer_came)
     parts = call(
-        tok_kernel, [array(chips, 2 * own, features)], work, grad, out_parts, expand, expand_far
+        tok_kernel, "tok", [array(chips, own + own // 2, features)], grad, layer, expand, expand_far
     )
     sums = exchange(parts, "col", over_col)
-    act_got = swap_cores(act_send)
-    grad, grad_send = call(pack_kernel, [held, held], 0, after(grad, parts))
-    grad_got = swap_cores(grad_send)
+    grad, send = call(pack_kernel, "pack", [held, array(2, chips, own, hidden)], after(grad, parts), act_send)
+    got = swap_cores(send)
     panels_far = swap_cores(after(panels, parts))
     expand_grad, project_grad = call(
         functools.partial(weight_grads_kernel, factor),
+        "grads",
         [array(features, hidden), array(hidden, features)],
-        2 * work,
         panels,
         panels_far,
         act,
-        act_got,
         grad,
-        grad_got,
+        got,
     )
     shard = array(own, features)
-    layer_out, token_grad = call(final_kernel, [shard, shard], 0, after(sums, expand_grad))
+    layer_out, token_grad = call(final_kernel, "final", [shard, shard], after(sums, expand_grad))
     return (layer_out, token_grad, expand_grad, project_grad)
 
 

time: 157 us -> 151 us (0.962)
  the two profiles are of different devices: /device:TPU:64 before, /device:TPU:74 now
where the time goes in v5:
time: 151 us; the launch traced here: 150 us
  starting transfers between devices  55.4 us (37%)
  waiting for transfers between devices  43.9 us (29%)
  blocking collectives  26.4 us (17%)
  Pallas kernels  13.4 us (9%)
  local copies, waits for them, and re-layouts  8.81 us (6%)
    all_to_all x4, starting transfers between devices, exchange(): return lax.all_to_all(parts, axis, 0, 0, axis_index_groups=groups)  36.3 us
    all_to_all x4, waiting for transfers between devices, exchange(): return lax.all_to_all(parts, axis, 0, 0, axis_index_groups=groups)  30.5 us
    all_to_all x1, blocking collectives, exchange(): return lax.all_to_all(parts, axis, 0, 0, axis_index_groups=groups)  26.4 us
    pallas_call x12, Pallas kernels, call(): pl.pallas_call(kernel, out_shape=outs[0] if one else outs, in_specs=[ANYW...  13.4 us
    ppermute x3, waiting for transfers between devices, swap_halves(): lax.ppermute(block, axis, [(at, (at + count // PAIR) % count) for at in r...  11.1 us
    ppermute x3, starting transfers between devices, swap_halves(): lax.ppermute(block, axis, [(at, (at + count // PAIR) % count) for at in r...  10.3 us
    ppermute x4, starting transfers between devices, swap_cores(): return lax.ppermute(block, 'col', [(at, at ^ 1) for at in range(cols)])  8.79 us
    unnamed x28, local copies, waits for them, and re-layouts  7.85 us
  transfers between devices with their start and end apart: 11, of which 9 were waited for; matrix products, arithmetic and copies ran while one was open for 0% of the time, Pallas kernels for 7%

profile of v5, /device:TPU:74, one launch (start us, length us, event | category | flops | bytes accessed | tf_op | source)
XLA Modules:
  0.0 149.6 jit_solution(14665564988633533888)
XLA Ops:
  0.6 0.8 pad_maximum_fusion
  1.4 0.0 copy-start
  1.4 1.0 broadcast_in_dim.2
  2.4 8.5 %all-to-all-start = ((bf16[16,32,768]{2,1,0:T(8,128)(2,1)}), bf16[16,32,768]{2,1,0:T(8,128)(2,1)S(1)}, u32[]{:S(2)}, u32[]{:S(2)}) async-start(bf16[16,32,768]{2,1,0:T(8,128)(2,1)} %broadcast_in_dim.2), calls=%async_computation | async-start | bytes 1572864 | tf_op jit(solution)/shard_map/all_to_all | solution.py:54
  10.8 0.0 copy-done
  10.8 1.9 %collective-permute-start = (bf16[768,768]{1,0:T(8,128)(2,1)S(1)}, bf16[768,768]{1,0:T(8,128)(2,1)S(1)}, u32[]{:S(2)}, u32[]{:S(2)}) collective-permute-start(bf16[768,768]{1,0:T(8,128)(2,1)S(1)} %copy-done), channel_id=1, source_target_pairs={{0,1},{1,0},{2,3},{3,2},{4,5},{5,4},{6,7},{7,6},{8,9},{9,8},{10,11... | collective-permute-start | bytes 3538952 | tf_op jit(solution)/shard_map/ppermute | solution.py:40
  12.8 2.4 %collective-permute-start.1 = (bf16[768,768]{1,0:T(8,128)(2,1)}, bf16[768,768]{1,0:T(8,128)(2,1)}, u32[]{:S(2)}, u32[]{:S(2)}) collective-permute-start(bf16[768,768]{1,0:T(8,128)(2,1)} %project.5), channel_id=1, source_target_pairs={{0,1},{1,0},{2,3},{3,2},{4,5},{5,4},{6,7},{7,6},{8,9},{9,8},{10,11... | collective-permute-start | bytes 3538952 | tf_op jit(solution)/shard_map/ppermute | solution.py:40
  15.2 0.4 collective-permute-done.expand_far
  15.6 15.9 %all-to-all-done.panels = bf16[16,32,768]{2,1,0:T(8,128)(2,1)S(1)} async-done(((bf16[16,32,768]{2,1,0:T(8,128)(2,1)}), bf16[16,32,768]{2,1,0:T(8,128)(2,1)S(1)}, u32[]{:S(2)}, u32[]{:S(2)}) %all-to-all-start) | async-done | bytes 786464 | tf_op jit(solution)/shard_map/all_to_all | solution.py:54
  31.4 0.0 copy-start.1
  31.4 0.8 shard_map.75
  32.3 0.0 copy-done.1
  32.3 0.0 copy-start.4
  32.3 0.9 copy-done.4
  33.2 11.5 %all-to-all-start.1 = ((bf16[16,16,1536]{2,1,0:T(8,128)(2,1)}), bf16[16,16,1536]{2,1,0:T(8,128)(2,1)S(1)}, u32[]{:S(2)}, u32[]{:S(2)}) async-start(bf16[16,16,1536]{2,1,0:T(8,128)(2,1)} %copy-done.4), calls=%async_computation.1 | async-start | bytes 1572864 | tf_op jit(solution)/shard_map/all_to_all | solution.py:54
  44.7 0.1 pad_add_fusion.which
  44.8 0.0 collective-permute-done.1.project_far
  44.8 0.0 copy-start.2
  44.8 1.1 copy-done.2
  45.9 0.0 copy-start.8
  45.9 1.3 copy-done.8
  47.2 3.0 %shard_map.76 = bf16[8,16,1536]{2,1,0:T(8,128)(2,1)} custom-call(s32[2]{0:T(128)S(1)} %pad_add_fusion.which, bf16[16,32,768]{2,1,0:T(8,128)(2,1)S(1)} %copy-done.2, bf16[768,768]{1,0:T(8,128)(2,1)S(1)} %copy-done.8, bf16[768,768]{1,0:T(8,128)(2,1)} %collective-permute-done.1.project_far), custom_call_target="tpu_custom_call" | custom-call | flops 1500000000 | bytes 3538952 | tf_op jit(solution)/shard_map/pallas_call | solution.py:85
  50.2 4.9 %collective-permute-start.2 = (bf16[8,16,1536]{2,1,0:T(8,128)(2,1)}, bf16[8,16,1536]{2,1,0:T(8,128)(2,1)S(1)}, u32[]{:S(2)}, u32[]{:S(2)}) collective-permute-start(bf16[8,16,1536]{2,1,0:T(8,128)(2,1)} %shard_map.76), channel_id=1, source_target_pairs={{0,256},{32,288},{64,320},{96,352},{128,384},{160,416},{192,448},{... | collective-permute-start | bytes 1179656 | tf_op jit(solution)/shard_map/ppermute | solution.py:50
  55.1 2.2 %shard_map.77.mine = f32[8,16,1536]{2,1,0:T(8,128)S(1)} custom-call(s32[2]{0:T(128)S(1)} %pad_add_fusion.which, bf16[16,32,768]{2,1,0:T(8,128)(2,1)S(1)} %copy-done.2, bf16[768,768]{1,0:T(8,128)(2,1)S(1)} %copy-done.8, bf16[768,768]{1,0:T(8,128)(2,1)} %collective-permute-done.1.project_far), custom_call_target="tpu_custom_call" | custom-call | flops 1500000000 | bytes 3932168 | tf_op jit(solution)/shard_map/pallas_call | solution.py:85
  57.3 0.0 copy-start.6
  57.3 0.9 copy-done.6
  58.2 6.7 %all-to-all-done.1.sums = bf16[16,16,1536]{2,1,0:T(8,128)(2,1)S(1)} async-done(((bf16[16,16,1536]{2,1,0:T(8,128)(2,1)}), bf16[16,16,1536]{2,1,0:T(8,128)(2,1)S(1)}, u32[]{:S(2)}, u32[]{:S(2)}) %all-to-all-start.1) | async-done | bytes 786464 | tf_op jit(solution)/shard_map/all_to_all | solution.py:54
  64.9 0.0 copy-start.7
  64.9 0.2 shard_map.78
  65.1 1.9 %collective-permute-done.2.came = bf16[8,16,1536]{2,1,0:T(8,128)(2,1)S(1)} collective-permute-done((bf16[8,16,1536]{2,1,0:T(8,128)(2,1)}, bf16[8,16,1536]{2,1,0:T(8,128)(2,1)S(1)}, u32[]{:S(2)}, u32[]{:S(2)}) %collective-permute-start.2) | collective-permute-done | bytes 393248 | tf_op jit(solution)/shard_map/ppermute | solution.py:50
  67.0 0.0 copy-done.7
  67.0 0.1 shard_map.79
  67.1 26.4 %all_to_all.25.mixed = bf16[8,32,1536]{2,1,0:T(8,128)(2,1)S(1)} all-to-all(bf16[8,32,1536]{2,1,0:T(8,128)(2,1)S(1)} %shard_map.79), channel_id=1, replica_groups={{0,32,64,96,128,160,192,224},{256,288,320,352,384,416,448,480},{1,33,65..., dimensions={0} | all-to-all | bytes 1572864 | tf_op jit(solution)/shard_map/all_to_all | solution.py:54
  93.4 0.1 shard_map.80
  93.5 0.0 copy-start.5
  93.5 0.9 copy-done.5
  94.4 2.6 %collective-permute-start.3 = (bf16[8,16,1536]{2,1,0:T(8,128)(2,1)S(1)}, bf16[8,16,1536]{2,1,0:T(8,128)(2,1)}, u32[]{:S(2)}, u32[]{:S(2)}) collective-permute-start(bf16[8,16,1536]{2,1,0:T(8,128)(2,1)S(1)} %get-tuple-element.32.act), channel_id=1, source_target_pairs={{0,256},{32,288},{64,320},{96,352},{128,384},{160,416},{192,448},{... | collective-permute-start | bytes 1179656 | tf_op jit(solution)/shard_map/ppermute | solution.py:50
  97.0 5.6 %all-to-all-start.3 = ((bf16[16,16,1536]{2,1,0:T(8,128)(2,1)}), bf16[16,16,1536]{2,1,0:T(8,128)(2,1)S(1)}, u32[]{:S(2)}, u32[]{:S(2)}) async-start(bf16[16,16,1536]{2,1,0:T(8,128)(2,1)} %copy-done.5), calls=%async_computation.3 | async-start | bytes 1572864 | tf_op jit(solution)/shard_map/all_to_all | solution.py:54
  102.6 3.6 %collective-permute-done.3.act_far = bf16[8,16,1536]{2,1,0:T(8,128)(2,1)} collective-permute-done((bf16[8,16,1536]{2,1,0:T(8,128)(2,1)S(1)}, bf16[8,16,1536]{2,1,0:T(8,128)(2,1)}, u32[]{:S(2)}, u32[]{:S(2)}) %collective-permute-start.3) | collective-permute-done | bytes 393248 | tf_op jit(solution)/shard_map/ppermute | solution.py:50
  106.2 0.0 copy-start.9
  106.2 1.3 copy-done.9
  107.5 2.2 %shard_map.81 = (f32[16,8,768]{2,1,0:T(8,128)S(1)}, bf16[16,8,768]{2,1,0:T(8,128)(2,1)S(1)}, bf16[16,16,768]{2,1,0:T(8,128)(2,1)S(1)}, bf16[16,16,768]{2,1,0:T(8,128)(2,1)S(1)}) custom-call(s32[2]{0:T(128)S(1)} %pad_add_fusion.which, bf16[8,16,1536]{2,1,0:T(8,128)(2,1)S(1)} %get-tuple-element.32.act, bf16[8,16,1536]{2,1,0:T(8,128)(2,1)} %collective-permute-done.3.act_far, ...), custom_call_target="tpu_custom_call" | custom-call | flops 60000002048 | bytes 4521992 | tf_op jit(solution)/shard_map/pallas_call | solution.py:85
  109.7 0.0 copy-start.10
  109.7 0.8 copy-done.10
  110.5 0.0 copy-start.12
  110.5 0.7 copy-done.12
  111.2 2.9 %collective-permute-start.4 = (bf16[16,8,768]{2,1,0:T(8,128)(2,1)S(1)}, bf16[16,8,768]{2,1,0:T(8,128)(2,1)S(1)}, u32[]{:S(2)}, u32[]{:S(2)}) collective-permute-start(bf16[16,8,768]{2,1,0:T(8,128)(2,1)S(1)} %get-tuple-element.34), channel_id=1, source_target_pairs={{0,16},{1,17},{2,18},{3,19},{4,20},{5,21},{6,22},{7,23},{8,24},{9,... | collective-permute-start | bytes 589832 | tf_op jit(solution)/shard_map/ppermute | solution.py:50
  114.1 5.7 %collective-permute-done.4.came = bf16[16,8,768]{2,1,0:T(8,128)(2,1)S(1)} collective-permute-done((bf16[16,8,768]{2,1,0:T(8,128)(2,1)S(1)}, bf16[16,8,768]{2,1,0:T(8,128)(2,1)S(1)}, u32[]{:S(2)}, u32[]{:S(2)}) %collective-permute-start.4) | collective-permute-done | bytes 196640 | tf_op jit(solution)/shard_map/ppermute | solution.py:50
  119.8 3.0 %all-to-all-done.3.grad = bf16[16,16,1536]{2,1,0:T(8,128)(2,1)S(1)} async-done(((bf16[16,16,1536]{2,1,0:T(8,128)(2,1)}), bf16[16,16,1536]{2,1,0:T(8,128)(2,1)S(1)}, u32[]{:S(2)}, u32[]{:S(2)}) %all-to-all-start.3) | async-done | bytes 786464 | tf_op jit(solution)/shard_map/all_to_all | solution.py:54
  122.8 1.6 %shard_map.83 = bf16[16,24,768]{2,1,0:T(8,128)(2,1)} custom-call(bf16[16,16,1536]{2,1,0:T(8,128)(2,1)S(1)} %all-to-all-done.3.grad, bf16[16,8,768]{2,1,0:T(8,128)(2,1)S(1)} %shard_map.82.layer, bf16[768,768]{1,0:T(8,128)(2,1)S(1)} %copy-done, bf16[768,768]{1,0:T(8,128)(2,1)S(1)} %collective-permute-done.expand_far), custom_call_target="tpu_custom_call" | custom-call | bytes 3932160 | tf_op jit(solution)/shard_map/pallas_call | solution.py:85
  124.4 0.0 copy-start.3
  124.4 10.7 %all-to-all-start.4 = ((bf16[16,24,768]{2,1,0:T(8,128)(2,1)}), bf16[16,24,768]{2,1,0:T(8,128)(2,1)S(1)}, u32[]{:S(2)}, u32[]{:S(2)}) async-start(bf16[16,24,768]{2,1,0:T(8,128)(2,1)} %shard_map.83), calls=%async_computation.4 | async-start | bytes 1179648 | tf_op jit(solution)/shard_map/all_to_all | solution.py:54
  135.1 0.0 copy-done.3
  135.1 1.9 %collective-permute-start.5 = (bf16[16,32,768]{2,1,0:T(8,128)(2,1)S(1)}, bf16[16,32,768]{2,1,0:T(8,128)(2,1)S(1)}, u32[]{:S(2)}, u32[]{:S(2)}) collective-permute-start(bf16[16,32,768]{2,1,0:T(8,128)(2,1)S(1)} %copy-done.3), channel_id=1, source_target_pairs={{0,1},{1,0},{2,3},{3,2},{4,5},{5,4},{6,7},{7,6},{8,9},{9,8},{10,11... | collective-permute-start | bytes 2359304 | tf_op jit(solution)/shard_map/ppermute | solution.py:40
  137.0 0.0 copy-done.13
  137.0 0.0 copy-start.11
  137.0 0.1 shard_map.84
  137.1 2.5 %collective-permute-start.6 = (bf16[2,16,16,768]{3,2,1,0:T(8,128)(2,1)S(1)}, bf16[2,16,16,768]{3,2,1,0:T(8,128)(2,1)S(1)}, u32[]{:S(2)}, u32[]{:S(2)}) collective-permute-start(bf16[2,16,16,768]{3,2,1,0:T(8,128)(2,1)S(1)} %get-tuple-element.40), channel_id=1, source_target_pairs={{0,1},{1,0},{2,3},{3,2},{4,5},{5,4},{6,7},{7,6},{8,9},{9,8},{10,11... | collective-permute-start | bytes 2359304 | tf_op jit(solution)/shard_map/ppermute | solution.py:40
  139.7 0.0 collective-permute-done.5.panels_far
  139.7 1.9 %collective-permute-done.6.got = bf16[2,16,16,768]{3,2,1,0:T(8,128)(2,1)S(1)} collective-permute-done((bf16[2,16,16,768]{3,2,1,0:T(8,128)(2,1)S(1)}, bf16[2,16,16,768]{3,2,1,0:T(8,128)(2,1)S(1)}, u32[]{:S(2)}, u32[]{:S(2)}) %collective-permute-start.6) | collective-permute-done | bytes 786464 | tf_op jit(solution)/shard_map/ppermute | solution.py:40
  141.6 0.0 copy-done.11
  141.6 2.4 %shard_map.85 = (bf16[768,768]{1,0:T(8,128)(2,1)}, bf16[768,768]{1,0:T(8,128)(2,1)}) custom-call(bf16[16,32,768]{2,1,0:T(8,128)(2,1)S(1)} %copy-done.3, bf16[16,32,768]{2,1,0:T(8,128)(2,1)S(1)} %collective-permute-done.5.panels_far, bf16[16,16,768]{2,1,0:T(8,128)(2,1)S(1)} %copy-done.11, bf16[16,16,768]{2,1,0:T(8,128)(2,1)S(1)} %get-tuple-element.39.grad, ...), custom_call_target="tpu_custom_call" | custom-call | flops 1200000000 | bytes 5505024 | tf_op jit(solution)/shard_map/pallas_call | solution.py:85
  144.0 4.9 %all-to-all-done.4.sums = bf16[16,24,768]{2,1,0:T(8,128)(2,1)S(1)} async-done(((bf16[16,24,768]{2,1,0:T(8,128)(2,1)}), bf16[16,24,768]{2,1,0:T(8,128)(2,1)S(1)}, u32[]{:S(2)}, u32[]{:S(2)}) %all-to-all-start.4) | async-done | bytes 589856 | tf_op jit(solution)/shard_map/all_to_all | solution.py:54
  148.9 0.7 shard_map.86
  (2 shorter events, 0.0 us)
Async XLA Ops:
  1.4 9.4 %copy-start = (bf16[768,768]{1,0:T(8,128)(2,1)S(1)}, bf16[768,768]{1,0:T(8,128)(2,1)}, u32[]{:S(2)}) copy-start(bf16[768,768]{1,0:T(8,128)(2,1)} %expand.3) | copy-start | bytes 3538948
  2.4 29.1 %all-to-all-start = ((bf16[16,32,768]{2,1,0:T(8,128)(2,1)}), bf16[16,32,768]{2,1,0:T(8,128)(2,1)S(1)}, u32[]{:S(2)}, u32[]{:S(2)}) async-start(bf16[16,32,768]{2,1,0:T(8,128)(2,1)} %broadcast_in_dim.2), calls=%async_computation | async-start | bytes 1572864 | tf_op jit(solution)/shard_map/all_to_all | solution.py:54
  10.8 4.7 %collective-permute-start = (bf16[768,768]{1,0:T(8,128)(2,1)S(1)}, bf16[768,768]{1,0:T(8,128)(2,1)S(1)}, u32[]{:S(2)}, u32[]{:S(2)}) collective-permute-start(bf16[768,768]{1,0:T(8,128)(2,1)S(1)} %copy-done), channel_id=1, source_target_pairs={{0,1},{1,0},{2,3},{3,2},{4,5},{5,4},{6,7},{7,6},{8,9},{9,8},{10,11... | collective-permute-start | bytes 3538952 | tf_op jit(solution)/shard_map/ppermute | solution.py:40
  12.8 32.0 %collective-permute-start.1 = (bf16[768,768]{1,0:T(8,128)(2,1)}, bf16[768,768]{1,0:T(8,128)(2,1)}, u32[]{:S(2)}, u32[]{:S(2)}) collective-permute-start(bf16[768,768]{1,0:T(8,128)(2,1)} %project.5), channel_id=1, source_target_pairs={{0,1},{1,0},{2,3},{3,2},{4,5},{5,4},{6,7},{7,6},{8,9},{9,8},{10,11... | collective-permute-start | bytes 3538952 | tf_op jit(solution)/shard_map/ppermute | solution.py:40
  31.4 0.9 copy-start.1
  32.3 0.9 copy-start.4
  33.2 31.7 %all-to-all-start.1 = ((bf16[16,16,1536]{2,1,0:T(8,128)(2,1)}), bf16[16,16,1536]{2,1,0:T(8,128)(2,1)S(1)}, u32[]{:S(2)}, u32[]{:S(2)}) async-start(bf16[16,16,1536]{2,1,0:T(8,128)(2,1)} %copy-done.4), calls=%async_computation.1 | async-start | bytes 1572864 | tf_op jit(solution)/shard_map/all_to_all | solution.py:54
  44.8 1.1 copy-start.2
  45.9 1.3 copy-start.8
  50.2 16.8 %collective-permute-start.2 = (bf16[8,16,1536]{2,1,0:T(8,128)(2,1)}, bf16[8,16,1536]{2,1,0:T(8,128)(2,1)S(1)}, u32[]{:S(2)}, u32[]{:S(2)}) collective-permute-start(bf16[8,16,1536]{2,1,0:T(8,128)(2,1)} %shard_map.76), channel_id=1, source_target_pairs={{0,256},{32,288},{64,320},{96,352},{128,384},{160,416},{192,448},{... | collective-permute-start | bytes 1179656 | tf_op jit(solution)/shard_map/ppermute | solution.py:50
  57.3 0.9 copy-start.6
  64.9 2.1 %copy-start.7 = (f32[8,16,1536]{2,1,0:T(8,128)S(1)}, f32[8,16,1536]{2,1,0:T(8,128)}, u32[]{:S(2)}) copy-start(f32[8,16,1536]{2,1,0:T(8,128)} %copy-done.6) | copy-start | bytes 2359300
  93.5 0.9 copy-start.5
  94.4 11.8 %collective-permute-start.3 = (bf16[8,16,1536]{2,1,0:T(8,128)(2,1)S(1)}, bf16[8,16,1536]{2,1,0:T(8,128)(2,1)}, u32[]{:S(2)}, u32[]{:S(2)}) collective-permute-start(bf16[8,16,1536]{2,1,0:T(8,128)(2,1)S(1)} %get-tuple-element.32.act), channel_id=1, source_target_pairs={{0,256},{32,288},{64,320},{96,352},{128,384},{160,416},{192,448},{... | collective-permute-start | bytes 1179656 | tf_op jit(solution)/shard_map/ppermute | solution.py:50
  97.0 25.8 %all-to-all-start.3 = ((bf16[16,16,1536]{2,1,0:T(8,128)(2,1)}), bf16[16,16,1536]{2,1,0:T(8,128)(2,1)S(1)}, u32[]{:S(2)}, u32[]{:S(2)}) async-start(bf16[16,16,1536]{2,1,0:T(8,128)(2,1)} %copy-done.5), calls=%async_computation.3 | async-start | bytes 1572864 | tf_op jit(solution)/shard_map/all_to_all | solution.py:54
  106.2 1.3 copy-start.9
  109.7 0.8 copy-start.10
  110.5 0.7 copy-start.12
  111.2 8.5 %collective-permute-start.4 = (bf16[16,8,768]{2,1,0:T(8,128)(2,1)S(1)}, bf16[16,8,768]{2,1,0:T(8,128)(2,1)S(1)}, u32[]{:S(2)}, u32[]{:S(2)}) collective-permute-start(bf16[16,8,768]{2,1,0:T(8,128)(2,1)S(1)} %get-tuple-element.34), channel_id=1, source_target_pairs={{0,16},{1,17},{2,18},{3,19},{4,20},{5,21},{6,22},{7,23},{8,24},{9,... | collective-permute-start | bytes 589832 | tf_op jit(solution)/shard_map/ppermute | solution.py:50
  124.4 10.7 %copy-start.3 = (bf16[16,32,768]{2,1,0:T(8,128)(2,1)S(1)}, bf16[16,32,768]{2,1,0:T(8,128)(2,1)}, u32[]{:S(2)}) copy-start(bf16[16,32,768]{2,1,0:T(8,128)(2,1)} %copy-done.1) | copy-start | bytes 2359300
  124.4 12.6 %copy-start.13 = (bf16[16,16,768]{2,1,0:T(8,128)(2,1)S(1)}, bf16[16,16,768]{2,1,0:T(8,128)(2,1)}, u32[]{:S(2)}) copy-start(bf16[16,16,768]{2,1,0:T(8,128)(2,1)} %copy-done.12) | copy-start | bytes 1179652
  124.4 24.5 %all-to-all-start.4 = ((bf16[16,24,768]{2,1,0:T(8,128)(2,1)}), bf16[16,24,768]{2,1,0:T(8,128)(2,1)S(1)}, u32[]{:S(2)}, u32[]{:S(2)}) async-start(bf16[16,24,768]{2,1,0:T(8,128)(2,1)} %shard_map.83), calls=%async_computation.4 | async-start | bytes 1179648 | tf_op jit(solution)/shard_map/all_to_all | solution.py:54
  135.1 4.6 %collective-permute-start.5 = (bf16[16,32,768]{2,1,0:T(8,128)(2,1)S(1)}, bf16[16,32,768]{2,1,0:T(8,128)(2,1)S(1)}, u32[]{:S(2)}, u32[]{:S(2)}) collective-permute-start(bf16[16,32,768]{2,1,0:T(8,128)(2,1)S(1)} %copy-done.3), channel_id=1, source_target_pairs={{0,1},{1,0},{2,3},{3,2},{4,5},{5,4},{6,7},{7,6},{8,9},{9,8},{10,11... | collective-permute-start | bytes 2359304 | tf_op jit(solution)/shard_map/ppermute | solution.py:40
  137.0 4.5 %copy-start.11 = (bf16[16,16,768]{2,1,0:T(8,128)(2,1)S(1)}, bf16[16,16,768]{2,1,0:T(8,128)(2,1)}, u32[]{:S(2)}) copy-start(bf16[16,16,768]{2,1,0:T(8,128)(2,1)} %copy-done.10) | copy-start | bytes 1179652
  137.1 4.4 %collective-permute-start.6 = (bf16[2,16,16,768]{3,2,1,0:T(8,128)(2,1)S(1)}, bf16[2,16,16,768]{3,2,1,0:T(8,128)(2,1)S(1)}, u32[]{:S(2)}, u32[]{:S(2)}) collective-permute-start(bf16[2,16,16,768]{3,2,1,0:T(8,128)(2,1)S(1)} %get-tuple-element.40), channel_id=1, source_target_pairs={{0,1},{1,0},{2,3},{3,2},{4,5},{5,4},{6,7},{7,6},{8,9},{9,8},{10,11... | collective-permute-start | bytes 2359304 | tf_op jit(solution)/shard_map/ppermute | solution.py:40

commit v6 on v5

--- a/solution.py
+++ b/solution.py
@@ -16,7 +16,7 @@
 COSTS = dict(pre=(100, 10), theirs=(2.5, 1), mine=(2.5, 1), act=(0, 1), merge=(0, 1), grad=(0, 1), out=(100, 1), layer=(1, 1), tok=(0, 1), pack=(2.5, 1), grads=(2, 1), final=(0, 1))
 F32, BF16 = jnp.float32, jnp.bfloat16
 VMEM_BYTES = 12 << 20
-IN_SMEM = pl.BlockSpec(memory_space=pltpu.SMEM)
+MOST_VMEM_BYTES = 60 << 20
 IN_VMEM = pl.BlockSpec(memory_space=pltpu.VMEM)
 ANYWHERE = pl.BlockSpec(memory_space=pl.ANY)
 
@@ -50,6 +50,12 @@
     return lax.ppermute(block, axis, [(at, (at + count // PAIR) % count) for at in range(count)])
 
 
+def place():
+    row, col = lax.axis_index("row"), lax.axis_index("col")
+    rows, cols = lax.axis_size("row"), lax.axis_size("col")
+    return lax.div(row, rows // PAIR), lax.div(col, cols // PAIR), lax.rem(col, CORES)
+
+
 def exchange(parts, axis, groups):
     return lax.all_to_all(parts, axis, 0, 0, axis_index_groups=groups)
 
@@ -78,46 +84,50 @@
     return jax.ShapeDtypeStruct(shape, dtype)
 
 
-def call(kernel, name, outs, *args, ins=(), scratch=()):
+def call(kernel, name, outs, *args, ins=(), scratch=(), limit=VMEM_BYTES):
     held = sum(math.prod(a.shape) * a.dtype.itemsize for a in (*args, *outs))
     one = len(outs) == 1
     products, touched = COSTS[name]
     return pl.pallas_call(
         kernel,
         out_shape=outs[0] if one else outs,
-        in_specs=[
-            ANYWHERE if at in ins else IN_SMEM if a.dtype == jnp.int32 else IN_VMEM for at, a in enumerate(args)
-        ],
+        in_specs=[ANYWHERE if at in ins else IN_VMEM for at in range(len(args))],
         out_specs=IN_VMEM if one else [IN_VMEM] * len(outs),
         scratch_shapes=scratch,
-        compiler_params=pltpu.CompilerParams(vmem_limit_bytes=VMEM_BYTES),
+        compiler_params=pltpu.CompilerParams(vmem_limit_bytes=limit),
         cost_estimate=pl.CostEstimate(
             flops=int(products * UNIT), bytes_accessed=int(touched * held), transcendentals=0
         ),
     )(*args)
 
 
-def put_terms(out, dot, panel, near, far):
-    hidden = out.shape[2] // CORES
-    for side, weight in enumerate((near, far)):
-        terms = dot(panel, weight[...]).astype(out.dtype)
-        out[:, :, side * hidden : (side + 1) * hidden] = terms.reshape(*out.shape[:2], hidden)
-
-
 def pre_kernel(panels, expand, expand_far, out, held, sem):
-    load = pltpu.make_async_copy(panels.at[:, pl.ds(0, out.shape[1])], held, sem)
+    size, rows, hidden = out.shape[0] // PAIR, out.shape[1], out.shape[2]
+    _, _, core = place()
+    load = pltpu.make_async_copy(panels.at[:, pl.ds(0, held.shape[1])], held, sem)
     load.start()
     load.wait()
-    put_terms(out, times, flat(held[...]), expand, expand_far)
-
-
-def back_kernel(other, which, panels, project, project_far, out, held, sem):
-    size, own = out.shape[0], out.shape[1]
-    half = 1 - which[0] if other else which[0]
-    load = pltpu.make_async_copy(panels.at[pl.ds(half * size, size), pl.ds(own, own)], held, sem)
+    for side, weight in ((core, expand), (1 - core, expand_far)):
+        terms = times(flat(held[...]), weight[...]).astype(BF16)
+        out[pl.ds(side * size, size)] = terms.reshape(size, rows, hidden)
+
+
+def back_kernel(other, panels, project, project_far, out, held, weight, sem, weight_sem):
+    own = held.shape[1]
+    x_hi, _, core = place()
+    near = (1 - x_hi if other else x_hi) == core
+    load = pltpu.make_async_copy(panels.at[:, pl.ds(own, own)], held, sem)
     load.start()
+
+    def bring(ref):
+        copy = pltpu.make_async_copy(ref, weight, weight_sem)
+        copy.start()
+        copy.wait()
+
+    pl.when(near)(lambda: bring(project))
+    pl.when(jnp.logical_not(near))(lambda: bring(project_far))
     load.wait()
-    put_terms(out, times_turned, flat(held[...]), project, project_far)
+    out[...] = times_turned(flat(held[...]), weight[...]).astype(out.dtype).reshape(out.shape)
 
 
 def added(ref, stop):
@@ -148,39 +158,43 @@
         out[at] = grad
 
 
-def out_kernel(which, act, act_far, project, project_far, stay, leave, keep, send):
-    size, rows, hidden = act.shape[0], stay.shape[1], project.shape[0]
-    low = which[1] == 0
-    for half, block in ((which[0], act[...]), (1 - which[0], act_far[...])):
-        at = pl.ds(half * size, size)
-        left, right = block[:, :, :hidden], block[:, :, hidden:]
-        keep[at] = left
-        send[at] = right
-        terms = times(flat(left), project[...]) + times(flat(right), project_far[...])
-        terms = terms.reshape(size, 2 * rows, -1)
-        first, second = terms[:, :rows], terms[:, rows:]
-        stay[at] = jnp.where(low, first, second)
-        leave[at] = jnp.where(low, second, first).astype(BF16)
+def out_kernel(act, act_far, project, project_far, stay, leave, keep, send):
+    chips, rows, features = stay.shape
+    x_hi, x_lo, core = place()
+    same, low = x_hi == core, x_lo == 0
+    near, far = jnp.where(same, act[...], act_far[...]), jnp.where(same, act_far[...], act[...])
+    keep[...] = near.reshape(keep.shape)
+    send[...] = far.reshape(send.shape)
+    terms = times(flat(near), project[...]) + times(flat(far), project_far[...])
+    terms = terms.reshape(chips, 2 * rows, features)
+    first, second = terms[:, :rows], terms[:, rows:]
+    stay[...] = jnp.where(low, first, second)
+    leave[...] = jnp.where(low, second, first).astype(BF16)
 
 
 def layer_kernel(stay, came, out):
     out[...] = (stay[...] + came[...].astype(F32)).astype(BF16)
 
 
+def two_cores(grad):
+    size = grad.shape[0] // PAIR
+    _, _, core = place()
+    return [flat(grad[pl.ds(side * size, size)]) for side in (core, 1 - core)]
+
+
 def tok_kernel(grad, layer, expand, expand_far, out):
-    hidden = expand.shape[1]
     chips, rows, features = layer.shape
-    block = flat(grad[...])
-    terms = times_turned(block[:, :hidden], expand[...]) + times_turned(block[:, hidden:], expand_far[...])
+    near, far = two_cores(grad)
+    terms = times_turned(near, expand[...]) + times_turned(far, expand_far[...])
     parts = [layer[...].astype(F32), terms.reshape(chips, 2 * rows, features)]
     out[...] = jnp.concatenate(parts, axis=1).astype(BF16)
 
 
 def pack_kernel(grad, act_send, keep, send):
-    hidden = keep.shape[2]
-    keep[...] = grad[:, :, :hidden]
+    near, far = two_cores(grad)
+    keep[...] = near.reshape(keep.shape)
     send[0] = act_send[...]
-    send[1] = grad[:, :, hidden:]
+    send[1] = far.reshape(keep.shape)
 
 
 def weight_grads_kernel(factor, panels, panels_far, act, grad, got, expand_grad, project_grad):
@@ -211,10 +225,10 @@
     chips = cols // CORES
     own, features = tokens.shape
     hidden = expand.shape[1]
-    wide, share, size = CORES * hidden, chips * own // rows, rows // PAIR
+    size = rows // PAIR
+    share = chips * own // size
     over_col, along_z = col_groups(cols), row_groups(rows)
     factor = 1.0 / math.sqrt(own * cols)
-    which = jnp.stack([lax.axis_index("row") // size, lax.axis_index("col") // (cols // PAIR)]).astype(jnp.int32)
 
     block = jnp.concatenate([tokens, out_grad], axis=0)
     copies = jnp.broadcast_to(block[None], (chips, *block.shape))
@@ -222,11 +236,11 @@
     expand_far = swap_cores(after(expand, copies))
     panels = exchange(copies, "col", over_col)
 
-    half_sums = array(size, share, wide)
+    half_sums = array(size, share, hidden)
     pre = call(
         pre_kernel,
         "pre",
-        [array(rows, share, wide)],
+        [array(rows, share, hidden)],
         panels,
         expand,
         expand_far,
@@ -238,25 +252,28 @@
         return call(
             functools.partial(back_kernel, other),
             "theirs" if other else "mine",
-            [array(size, share, wide, dtype=dtype)],
-            which,
+            [array(size, share, hidden, dtype=dtype)],
             after(panels, earlier),
             project,
             project_far,
-            ins=(1,),
-            scratch=[pltpu.VMEM((size, own, features), BF16), pltpu.SemaphoreType.DMA],
+            ins=(0, 1, 2),
+            scratch=[
+                pltpu.VMEM((chips, own, features), BF16),
+                pltpu.VMEM(project.shape, BF16),
+                pltpu.SemaphoreType.DMA,
+                pltpu.SemaphoreType.DMA,
+            ],
+            limit=MOST_VMEM_BYTES,
         )
 
     theirs = back_terms(True, BF16, pre)
     came = swap_halves(theirs, "row")
     mine = back_terms(False, F32, theirs)
     pre = exchange(pre, "row", None)
-    act, slope = call(
-        act_kernel, "act", [array(share, wide), array(share, wide, dtype=F32)], pre
-    )
-    mixed = call(merge_kernel, "merge", [array(size, 2 * share, wide)], mine, came, act)
+    act, slope = call(act_kernel, "act", [array(share, hidden), array(share, hidden, dtype=F32)], pre)
+    mixed = call(merge_kernel, "merge", [array(size, 2 * share, hidden)], mine, came, act)
     mixed = exchange(mixed, "row", along_z)
-    act, grad = call(grad_kernel, "grad", [half_sums, array(rows, share, wide)], mixed, slope)
+    act, grad = call(grad_kernel, "grad", [half_sums, array(rows, share, hidden)], mixed, slope)
     act_far = swap_halves(act, "row")
     grad = exchange(grad, "row", None)
     held = array(chips, own, hidden)
@@ -264,7 +281,6 @@
         out_kernel,
         "out",
         [array(chips, own // 2, features, dtype=F32), array(chips, own // 2, features), held, held],
-        which,
         act,
         act_far,
         project,
@@ -276,7 +292,9 @@
         tok_kernel, "tok", [array(chips, own + own // 2, features)], grad, layer, expand, expand_far
     )
     sums = exchange(parts, "col", over_col)
-    grad, send = call(pack_kernel, "pack", [held, array(2, chips, own, hidden)], after(grad, parts), act_send)
+    grad, send = call(
+        pack_kernel, "pack", [held, array(2, chips, own, hidden)], after(grad, parts), act_send
+    )
     got = swap_cores(send)
     panels_far = swap_cores(after(panels, parts))
     expand_grad, project_grad = call(

time: 151 us -> 147 us (0.974)
  the two profiles are of different devices: /device:TPU:74 before, /device:TPU:64 now
where the time goes in v6:
time: 147 us; the launch traced here: 146 us
  starting transfers between devices  51 us (35%)
  waiting for transfers between devices  47.6 us (32%)
  blocking collectives  26.5 us (18%)
  Pallas kernels  13.7 us (9%)
  local copies, waits for them, and re-layouts  5.79 us (4%)
    all_to_all x4, waiting for transfers between devices, exchange(): return lax.all_to_all(parts, axis, 0, 0, axis_index_groups=groups)  35 us
    all_to_all x4, starting transfers between devices, exchange(): return lax.all_to_all(parts, axis, 0, 0, axis_index_groups=groups)  31.7 us
    all_to_all x1, blocking collectives, exchange(): return lax.all_to_all(parts, axis, 0, 0, axis_index_groups=groups)  26.5 us
    pallas_call x12, Pallas kernels, call(): pl.pallas_call(kernel, out_shape=outs[0] if one else outs, in_specs=[ANYW...  13.7 us
    ppermute x3, starting transfers between devices, swap_halves(): lax.ppermute(block, axis, [(at, (at + count // PAIR) % count) for at in r...  10.5 us
    ppermute x3, waiting for transfers between devices, swap_halves(): lax.ppermute(block, axis, [(at, (at + count // PAIR) % count) for at in r...  10.3 us
    ppermute x4, starting transfers between devices, swap_cores(): return lax.ppermute(block, 'col', [(at, at ^ 1) for at in range(cols)])  8.79 us
    unnamed x22, local copies, waits for them, and re-layouts  4.83 us
  transfers between devices with their start and end apart: 11, of which 9 were waited for; matrix products, arithmetic and copies ran while one was open for 0% of the time, Pallas kernels for 8%

profile of v6, /device:TPU:64, one launch (start us, length us, event | category | flops | bytes accessed | tf_op | source)
XLA Modules:
  0.0 146.2 jit_solution(11379729734280529036)
XLA Ops:
  0.6 0.8 pad_maximum_fusion
  1.4 0.0 copy-start
  1.4 1.0 broadcast_in_dim.2
  2.4 8.1 %all-to-all-start = ((bf16[16,32,768]{2,1,0:T(8,128)(2,1)}), bf16[16,32,768]{2,1,0:T(8,128)(2,1)S(1)}, u32[]{:S(2)}, u32[]{:S(2)}) async-start(bf16[16,32,768]{2,1,0:T(8,128)(2,1)} %broadcast_in_dim.2), calls=%async_computation | async-start | bytes 1572864 | tf_op jit(solution)/shard_map/all_to_all | solution.py:60
  10.5 0.0 copy-done
  10.5 1.9 %collective-permute-start = (bf16[768,768]{1,0:T(8,128)(2,1)S(1)}, bf16[768,768]{1,0:T(8,128)(2,1)S(1)}, u32[]{:S(2)}, u32[]{:S(2)}) collective-permute-start(bf16[768,768]{1,0:T(8,128)(2,1)S(1)} %copy-done), channel_id=1, source_target_pairs={{0,1},{1,0},{2,3},{3,2},{4,5},{5,4},{6,7},{7,6},{8,9},{9,8},{10,11... | collective-permute-start | bytes 3538952 | tf_op jit(solution)/shard_map/ppermute | solution.py:40
  12.4 2.4 %collective-permute-start.1 = (bf16[768,768]{1,0:T(8,128)(2,1)}, bf16[768,768]{1,0:T(8,128)(2,1)}, u32[]{:S(2)}, u32[]{:S(2)}) collective-permute-start(bf16[768,768]{1,0:T(8,128)(2,1)} %project.5), channel_id=1, source_target_pairs={{0,1},{1,0},{2,3},{3,2},{4,5},{5,4},{6,7},{7,6},{8,9},{9,8},{10,11... | collective-permute-start | bytes 3538952 | tf_op jit(solution)/shard_map/ppermute | solution.py:40
  14.9 0.4 collective-permute-done.expand_far
  15.2 16.4 %all-to-all-done.panels = bf16[16,32,768]{2,1,0:T(8,128)(2,1)S(1)} async-done(((bf16[16,32,768]{2,1,0:T(8,128)(2,1)}), bf16[16,32,768]{2,1,0:T(8,128)(2,1)S(1)}, u32[]{:S(2)}, u32[]{:S(2)}) %all-to-all-start) | async-done | bytes 786464 | tf_op jit(solution)/shard_map/all_to_all | solution.py:60
  31.6 0.0 copy-start.1
  31.6 0.8 shard_map.75
  32.5 0.0 copy-done.1
  32.5 0.0 copy-start.4
  32.5 0.9 copy-done.4
  33.4 12.1 %all-to-all-start.1 = ((bf16[16,32,768]{2,1,0:T(8,128)(2,1)}), bf16[16,32,768]{2,1,0:T(8,128)(2,1)S(1)}, u32[]{:S(2)}, u32[]{:S(2)}) async-start(bf16[16,32,768]{2,1,0:T(8,128)(2,1)} %copy-done.4), calls=%async_computation.1 | async-start | bytes 1572864 | tf_op jit(solution)/shard_map/all_to_all | solution.py:60
  45.5 0.0 collective-permute-done.1.project_far
  45.6 2.7 %shard_map.76 = bf16[8,32,768]{2,1,0:T(8,128)(2,1)} custom-call(bf16[16,32,768]{2,1,0:T(8,128)(2,1)} %copy-done.1, bf16[768,768]{1,0:T(8,128)(2,1)} %project.5, bf16[768,768]{1,0:T(8,128)(2,1)} %collective-permute-done.1.project_far), custom_call_target="tpu_custom_call" | custom-call | flops 1500000000 | bytes 3538944 | tf_op jit(solution)/shard_map/pallas_call | solution.py:91
  48.2 4.9 %collective-permute-start.2 = (bf16[8,32,768]{2,1,0:T(8,128)(2,1)}, bf16[8,32,768]{2,1,0:T(8,128)(2,1)S(1)}, u32[]{:S(2)}, u32[]{:S(2)}) collective-permute-start(bf16[8,32,768]{2,1,0:T(8,128)(2,1)} %shard_map.76), channel_id=1, source_target_pairs={{0,256},{32,288},{64,320},{96,352},{128,384},{160,416},{192,448},{... | collective-permute-start | bytes 1179656 | tf_op jit(solution)/shard_map/ppermute | solution.py:50
  53.1 2.8 %shard_map.77.mine = f32[8,32,768]{2,1,0:T(8,128)} custom-call(bf16[16,32,768]{2,1,0:T(8,128)(2,1)} %copy-done.1, bf16[768,768]{1,0:T(8,128)(2,1)} %project.5, bf16[768,768]{1,0:T(8,128)(2,1)} %collective-permute-done.1.project_far), custom_call_target="tpu_custom_call" | custom-call | flops 1500000000 | bytes 3932160 | tf_op jit(solution)/shard_map/pallas_call | solution.py:91
  55.9 10.2 %all-to-all-done.1.sums = bf16[16,32,768]{2,1,0:T(8,128)(2,1)S(1)} async-done(((bf16[16,32,768]{2,1,0:T(8,128)(2,1)}), bf16[16,32,768]{2,1,0:T(8,128)(2,1)S(1)}, u32[]{:S(2)}, u32[]{:S(2)}) %all-to-all-start.1) | async-done | bytes 786464 | tf_op jit(solution)/shard_map/all_to_all | solution.py:60
  66.1 0.0 copy-start.5
  66.1 0.2 shard_map.78
  66.3 0.7 collective-permute-done.2.came
  67.0 0.2 copy-done.5
  67.2 0.1 shard_map.79
  67.3 26.5 %all_to_all.25.mixed = bf16[8,64,768]{2,1,0:T(8,128)(2,1)S(1)} all-to-all(bf16[8,64,768]{2,1,0:T(8,128)(2,1)S(1)} %shard_map.79), channel_id=1, replica_groups={{0,32,64,96,128,160,192,224},{256,288,320,352,384,416,448,480},{1,33,65..., dimensions={0} | all-to-all | bytes 1572864 | tf_op jit(solution)/shard_map/all_to_all | solution.py:60
  93.8 0.1 shard_map.80
  93.9 0.0 copy-start.3
  93.9 0.9 copy-done.3
  94.8 3.7 %collective-permute-start.3 = (bf16[8,32,768]{2,1,0:T(8,128)(2,1)S(1)}, bf16[8,32,768]{2,1,0:T(8,128)(2,1)}, u32[]{:S(2)}, u32[]{:S(2)}) collective-permute-start(bf16[8,32,768]{2,1,0:T(8,128)(2,1)S(1)} %get-tuple-element.32.act), channel_id=1, source_target_pairs={{0,256},{32,288},{64,320},{96,352},{128,384},{160,416},{192,448},{... | collective-permute-start | bytes 1179656 | tf_op jit(solution)/shard_map/ppermute | solution.py:50
  98.5 4.9 %all-to-all-start.3 = ((bf16[16,32,768]{2,1,0:T(8,128)(2,1)}), bf16[16,32,768]{2,1,0:T(8,128)(2,1)S(1)}, u32[]{:S(2)}, u32[]{:S(2)}) async-start(bf16[16,32,768]{2,1,0:T(8,128)(2,1)} %copy-done.3), calls=%async_computation.3 | async-start | bytes 1572864 | tf_op jit(solution)/shard_map/all_to_all | solution.py:60
  103.4 3.2 %collective-permute-done.3.act_far = bf16[8,32,768]{2,1,0:T(8,128)(2,1)} collective-permute-done((bf16[8,32,768]{2,1,0:T(8,128)(2,1)S(1)}, bf16[8,32,768]{2,1,0:T(8,128)(2,1)}, u32[]{:S(2)}, u32[]{:S(2)}) %collective-permute-start.3) | collective-permute-done | bytes 393248 | tf_op jit(solution)/shard_map/ppermute | solution.py:50
  106.6 0.0 copy-start.6
  106.6 1.3 copy-done.6
  107.9 2.2 %shard_map.81 = (f32[16,8,768]{2,1,0:T(8,128)S(1)}, bf16[16,8,768]{2,1,0:T(8,128)(2,1)S(1)}, bf16[16,16,768]{2,1,0:T(8,128)(2,1)S(1)}, bf16[16,16,768]{2,1,0:T(8,128)(2,1)S(1)}) custom-call(bf16[8,32,768]{2,1,0:T(8,128)(2,1)S(1)} %get-tuple-element.32.act, bf16[8,32,768]{2,1,0:T(8,128)(2,1)} %collective-permute-done.3.act_far, ...), custom_call_target="tpu_custom_call" | custom-call | flops 60000002048 | bytes 4521984 | tf_op jit(solution)/shard_map/pallas_call | solution.py:91
  110.0 0.0 copy-start.7
  110.0 0.7 copy-done.7
  110.8 0.0 copy-start.9
  110.8 0.7 copy-done.9
  111.5 1.9 %collective-permute-start.4 = (bf16[16,8,768]{2,1,0:T(8,128)(2,1)S(1)}, bf16[16,8,768]{2,1,0:T(8,128)(2,1)S(1)}, u32[]{:S(2)}, u32[]{:S(2)}) collective-permute-start(bf16[16,8,768]{2,1,0:T(8,128)(2,1)S(1)} %get-tuple-element.34), channel_id=1, source_target_pairs={{0,16},{1,17},{2,18},{3,19},{4,20},{5,21},{6,22},{7,23},{8,24},{9,... | collective-permute-start | bytes 589832 | tf_op jit(solution)/shard_map/ppermute | solution.py:50
  113.5 6.4 %collective-permute-done.4.came = bf16[16,8,768]{2,1,0:T(8,128)(2,1)S(1)} collective-permute-done((bf16[16,8,768]{2,1,0:T(8,128)(2,1)S(1)}, bf16[16,8,768]{2,1,0:T(8,128)(2,1)S(1)}, u32[]{:S(2)}, u32[]{:S(2)}) %collective-permute-start.4) | collective-permute-done | bytes 196640 | tf_op jit(solution)/shard_map/ppermute | solution.py:50
  119.9 3.5 %all-to-all-done.3.grad = bf16[16,32,768]{2,1,0:T(8,128)(2,1)S(1)} async-done(((bf16[16,32,768]{2,1,0:T(8,128)(2,1)}), bf16[16,32,768]{2,1,0:T(8,128)(2,1)S(1)}, u32[]{:S(2)}, u32[]{:S(2)}) %all-to-all-start.3) | async-done | bytes 786464 | tf_op jit(solution)/shard_map/all_to_all | solution.py:60
  123.5 1.6 %shard_map.83 = bf16[16,24,768]{2,1,0:T(8,128)(2,1)} custom-call(bf16[16,32,768]{2,1,0:T(8,128)(2,1)S(1)} %all-to-all-done.3.grad, bf16[16,8,768]{2,1,0:T(8,128)(2,1)S(1)} %shard_map.82.layer, bf16[768,768]{1,0:T(8,128)(2,1)S(1)} %copy-done, bf16[768,768]{1,0:T(8,128)(2,1)S(1)} %collective-permute-done.expand_far), custom_call_target="tpu_custom_call" | custom-call | bytes 3932160 | tf_op jit(solution)/shard_map/pallas_call | solution.py:91
  125.1 0.0 copy-start.2
  125.1 0.0 copy-start.10
  125.1 6.6 %all-to-all-start.4 = ((bf16[16,24,768]{2,1,0:T(8,128)(2,1)}), bf16[16,24,768]{2,1,0:T(8,128)(2,1)S(1)}, u32[]{:S(2)}, u32[]{:S(2)}) async-start(bf16[16,24,768]{2,1,0:T(8,128)(2,1)} %shard_map.83), calls=%async_computation.4 | async-start | bytes 1179648 | tf_op jit(solution)/shard_map/all_to_all | solution.py:60
  131.7 0.0 copy-done.2
  131.7 1.9 %collective-permute-start.5 = (bf16[16,32,768]{2,1,0:T(8,128)(2,1)S(1)}, bf16[16,32,768]{2,1,0:T(8,128)(2,1)S(1)}, u32[]{:S(2)}, u32[]{:S(2)}) collective-permute-start(bf16[16,32,768]{2,1,0:T(8,128)(2,1)S(1)} %copy-done.2), channel_id=1, source_target_pairs={{0,1},{1,0},{2,3},{3,2},{4,5},{5,4},{6,7},{7,6},{8,9},{9,8},{10,11... | collective-permute-start | bytes 2359304 | tf_op jit(solution)/shard_map/ppermute | solution.py:40
  133.6 0.0 copy-done.10
  133.6 0.0 copy-start.8
  133.6 0.1 shard_map.84
  133.7 2.5 %collective-permute-start.6 = (bf16[2,16,16,768]{3,2,1,0:T(8,128)(2,1)S(1)}, bf16[2,16,16,768]{3,2,1,0:T(8,128)(2,1)S(1)}, u32[]{:S(2)}, u32[]{:S(2)}) collective-permute-start(bf16[2,16,16,768]{3,2,1,0:T(8,128)(2,1)S(1)} %get-tuple-element.40), channel_id=1, source_target_pairs={{0,1},{1,0},{2,3},{3,2},{4,5},{5,4},{6,7},{7,6},{8,9},{9,8},{10,11... | collective-permute-start | bytes 2359304 | tf_op jit(solution)/shard_map/ppermute | solution.py:40
  136.3 0.0 collective-permute-done.5.panels_far
  136.3 1.9 %collective-permute-done.6.got = bf16[2,16,16,768]{3,2,1,0:T(8,128)(2,1)S(1)} collective-permute-done((bf16[2,16,16,768]{3,2,1,0:T(8,128)(2,1)S(1)}, bf16[2,16,16,768]{3,2,1,0:T(8,128)(2,1)S(1)}, u32[]{:S(2)}, u32[]{:S(2)}) %collective-permute-start.6) | collective-permute-done | bytes 786464 | tf_op jit(solution)/shard_map/ppermute | solution.py:40
  138.2 0.0 copy-done.8
  138.2 2.4 %shard_map.85 = (bf16[768,768]{1,0:T(8,128)(2,1)}, bf16[768,768]{1,0:T(8,128)(2,1)}) custom-call(bf16[16,32,768]{2,1,0:T(8,128)(2,1)S(1)} %copy-done.2, bf16[16,32,768]{2,1,0:T(8,128)(2,1)S(1)} %collective-permute-done.5.panels_far, bf16[16,16,768]{2,1,0:T(8,128)(2,1)S(1)} %copy-done.8, bf16[16,16,768]{2,1,0:T(8,128)(2,1)S(1)} %get-tuple-element.39.grad, ...), custom_call_target="tpu_custom_call" | custom-call | flops 1200000000 | bytes 5505024 | tf_op jit(solution)/shard_map/pallas_call | solution.py:91
  140.6 4.9 %all-to-all-done.4.sums = bf16[16,24,768]{2,1,0:T(8,128)(2,1)S(1)} async-done(((bf16[16,24,768]{2,1,0:T(8,128)(2,1)}), bf16[16,24,768]{2,1,0:T(8,128)(2,1)S(1)}, u32[]{:S(2)}, u32[]{:S(2)}) %all-to-all-start.4) | async-done | bytes 589856 | tf_op jit(solution)/shard_map/all_to_all | solution.py:60
  145.5 0.7 shard_map.86
  (1 shorter events, 0.0 us)
Async XLA Ops:
  1.4 9.1 %copy-start = (bf16[768,768]{1,0:T(8,128)(2,1)S(1)}, bf16[768,768]{1,0:T(8,128)(2,1)}, u32[]{:S(2)}) copy-start(bf16[768,768]{1,0:T(8,128)(2,1)} %expand.3) | copy-start | bytes 3538948
  2.4 29.3 %all-to-all-start = ((bf16[16,32,768]{2,1,0:T(8,128)(2,1)}), bf16[16,32,768]{2,1,0:T(8,128)(2,1)S(1)}, u32[]{:S(2)}, u32[]{:S(2)}) async-start(bf16[16,32,768]{2,1,0:T(8,128)(2,1)} %broadcast_in_dim.2), calls=%async_computation | async-start | bytes 1572864 | tf_op jit(solution)/shard_map/all_to_all | solution.py:60
  10.5 4.7 %collective-permute-start = (bf16[768,768]{1,0:T(8,128)(2,1)S(1)}, bf16[768,768]{1,0:T(8,128)(2,1)S(1)}, u32[]{:S(2)}, u32[]{:S(2)}) collective-permute-start(bf16[768,768]{1,0:T(8,128)(2,1)S(1)} %copy-done), channel_id=1, source_target_pairs={{0,1},{1,0},{2,3},{3,2},{4,5},{5,4},{6,7},{7,6},{8,9},{9,8},{10,11... | collective-permute-start | bytes 3538952 | tf_op jit(solution)/shard_map/ppermute | solution.py:40
  12.4 33.1 %collective-permute-start.1 = (bf16[768,768]{1,0:T(8,128)(2,1)}, bf16[768,768]{1,0:T(8,128)(2,1)}, u32[]{:S(2)}, u32[]{:S(2)}) collective-permute-start(bf16[768,768]{1,0:T(8,128)(2,1)} %project.5), channel_id=1, source_target_pairs={{0,1},{1,0},{2,3},{3,2},{4,5},{5,4},{6,7},{7,6},{8,9},{9,8},{10,11... | collective-permute-start | bytes 3538952 | tf_op jit(solution)/shard_map/ppermute | solution.py:40
  31.6 0.9 copy-start.1
  32.5 0.9 copy-start.4
  33.4 32.7 %all-to-all-start.1 = ((bf16[16,32,768]{2,1,0:T(8,128)(2,1)}), bf16[16,32,768]{2,1,0:T(8,128)(2,1)S(1)}, u32[]{:S(2)}, u32[]{:S(2)}) async-start(bf16[16,32,768]{2,1,0:T(8,128)(2,1)} %copy-done.4), calls=%async_computation.1 | async-start | bytes 1572864 | tf_op jit(solution)/shard_map/all_to_all | solution.py:60
  48.2 18.7 %collective-permute-start.2 = (bf16[8,32,768]{2,1,0:T(8,128)(2,1)}, bf16[8,32,768]{2,1,0:T(8,128)(2,1)S(1)}, u32[]{:S(2)}, u32[]{:S(2)}) collective-permute-start(bf16[8,32,768]{2,1,0:T(8,128)(2,1)} %shard_map.76), channel_id=1, source_target_pairs={{0,256},{32,288},{64,320},{96,352},{128,384},{160,416},{192,448},{... | collective-permute-start | bytes 1179656 | tf_op jit(solution)/shard_map/ppermute | solution.py:50
  66.1 1.1 copy-start.5
  93.9 0.9 copy-start.3
  94.8 11.8 %collective-permute-start.3 = (bf16[8,32,768]{2,1,0:T(8,128)(2,1)S(1)}, bf16[8,32,768]{2,1,0:T(8,128)(2,1)}, u32[]{:S(2)}, u32[]{:S(2)}) collective-permute-start(bf16[8,32,768]{2,1,0:T(8,128)(2,1)S(1)} %get-tuple-element.32.act), channel_id=1, source_target_pairs={{0,256},{32,288},{64,320},{96,352},{128,384},{160,416},{192,448},{... | collective-permute-start | bytes 1179656 | tf_op jit(solution)/shard_map/ppermute | solution.py:50
  98.5 25.0 %all-to-all-start.3 = ((bf16[16,32,768]{2,1,0:T(8,128)(2,1)}), bf16[16,32,768]{2,1,0:T(8,128)(2,1)S(1)}, u32[]{:S(2)}, u32[]{:S(2)}) async-start(bf16[16,32,768]{2,1,0:T(8,128)(2,1)} %copy-done.3), calls=%async_computation.3 | async-start | bytes 1572864 | tf_op jit(solution)/shard_map/all_to_all | solution.py:60
  106.6 1.3 copy-start.6
  110.0 0.8 copy-start.7
  110.8 0.7 copy-start.9
  111.5 8.3 %collective-permute-start.4 = (bf16[16,8,768]{2,1,0:T(8,128)(2,1)S(1)}, bf16[16,8,768]{2,1,0:T(8,128)(2,1)S(1)}, u32[]{:S(2)}, u32[]{:S(2)}) collective-permute-start(bf16[16,8,768]{2,1,0:T(8,128)(2,1)S(1)} %get-tuple-element.34), channel_id=1, source_target_pairs={{0,16},{1,17},{2,18},{3,19},{4,20},{5,21},{6,22},{7,23},{8,24},{9,... | collective-permute-start | bytes 589832 | tf_op jit(solution)/shard_map/ppermute | solution.py:50
  125.1 6.6 %copy-start.2 = (bf16[16,32,768]{2,1,0:T(8,128)(2,1)S(1)}, bf16[16,32,768]{2,1,0:T(8,128)(2,1)}, u32[]{:S(2)}) copy-start(bf16[16,32,768]{2,1,0:T(8,128)(2,1)} %copy-done.1) | copy-start | bytes 2359300
  125.1 8.5 %copy-start.10 = (bf16[16,16,768]{2,1,0:T(8,128)(2,1)S(1)}, bf16[16,16,768]{2,1,0:T(8,128)(2,1)}, u32[]{:S(2)}) copy-start(bf16[16,16,768]{2,1,0:T(8,128)(2,1)} %copy-done.9) | copy-start | bytes 1179652
  125.1 20.4 %all-to-all-start.4 = ((bf16[16,24,768]{2,1,0:T(8,128)(2,1)}), bf16[16,24,768]{2,1,0:T(8,128)(2,1)S(1)}, u32[]{:S(2)}, u32[]{:S(2)}) async-start(bf16[16,24,768]{2,1,0:T(8,128)(2,1)} %shard_map.83), calls=%async_computation.4 | async-start | bytes 1179648 | tf_op jit(solution)/shard_map/all_to_all | solution.py:60
  131.7 4.6 %collective-permute-start.5 = (bf16[16,32,768]{2,1,0:T(8,128)(2,1)S(1)}, bf16[16,32,768]{2,1,0:T(8,128)(2,1)S(1)}, u32[]{:S(2)}, u32[]{:S(2)}) collective-permute-start(bf16[16,32,768]{2,1,0:T(8,128)(2,1)S(1)} %copy-done.2), channel_id=1, source_target_pairs={{0,1},{1,0},{2,3},{3,2},{4,5},{5,4},{6,7},{7,6},{8,9},{9,8},{10,11... | collective-permute-start | bytes 2359304 | tf_op jit(solution)/shard_map/ppermute | solution.py:40
  133.6 4.5 %copy-start.8 = (bf16[16,16,768]{2,1,0:T(8,128)(2,1)S(1)}, bf16[16,16,768]{2,1,0:T(8,128)(2,1)}, u32[]{:S(2)}) copy-start(bf16[16,16,768]{2,1,0:T(8,128)(2,1)} %copy-done.7) | copy-start | bytes 1179652
  133.7 4.4 %collective-permute-start.6 = (bf16[2,16,16,768]{3,2,1,0:T(8,128)(2,1)S(1)}, bf16[2,16,16,768]{3,2,1,0:T(8,128)(2,1)S(1)}, u32[]{:S(2)}, u32[]{:S(2)}) collective-permute-start(bf16[2,16,16,768]{3,2,1,0:T(8,128)(2,1)S(1)} %get-tuple-element.40), channel_id=1, source_target_pairs={{0,1},{1,0},{2,3},{3,2},{4,5},{5,4},{6,7},{7,6},{8,9},{9,8},{10,11... | collective-permute-start | bytes 2359304 | tf_op jit(solution)/shard_map/ppermute | solution.py:40

commit v7 on v6

--- a/solution.py
+++ b/solution.py
@@ -12,6 +12,7 @@
 CUBIC = 0.044715
 CORES = 2
 PAIR = 2
+PIECES = 2
 UNIT = 600_000_000
 COSTS = dict(pre=(100, 10), theirs=(2.5, 1), mine=(2.5, 1), act=(0, 1), merge=(0, 1), grad=(0, 1), out=(100, 1), layer=(1, 1), tok=(0, 1), pack=(2.5, 1), grads=(2, 1), final=(0, 1))
 F32, BF16 = jnp.float32, jnp.bfloat16
@@ -112,22 +113,27 @@
         out[pl.ds(side * size, size)] = terms.reshape(size, rows, hidden)
 
 
-def back_kernel(other, panels, project, project_far, out, held, weight, sem, weight_sem):
+def back_kernel(other, panels, project, project_far, out, held, weight, sem, weight_sems):
     own = held.shape[1]
     x_hi, _, core = place()
     near = (1 - x_hi if other else x_hi) == core
     load = pltpu.make_async_copy(panels.at[:, pl.ds(own, own)], held, sem)
     load.start()
 
+    units = weight.shape[0] // PIECES
+    rows = [pl.ds(at * units, units) for at in range(PIECES)]
+
     def bring(ref):
-        copy = pltpu.make_async_copy(ref, weight, weight_sem)
-        copy.start()
-        copy.wait()
+        for at in range(PIECES):
+            pltpu.make_async_copy(ref.at[rows[at]], weight.at[rows[at]], weight_sems.at[at]).start()
 
     pl.when(near)(lambda: bring(project))
     pl.when(jnp.logical_not(near))(lambda: bring(project_far))
     load.wait()
-    out[...] = times_turned(flat(held[...]), weight[...]).astype(out.dtype).reshape(out.shape)
+    for at in range(PIECES):
+        pltpu.make_async_copy(project.at[rows[at]], weight.at[rows[at]], weight_sems.at[at]).wait()
+        terms = times_turned(flat(held[...]), weight[at * units : (at + 1) * units]).astype(out.dtype)
+        out[:, :, at * units : (at + 1) * units] = terms.reshape(*out.shape[:2], units)
 
 
 def added(ref, stop):
@@ -261,7 +267,7 @@
                 pltpu.VMEM((chips, own, features), BF16),
                 pltpu.VMEM(project.shape, BF16),
                 pltpu.SemaphoreType.DMA,
-                pltpu.SemaphoreType.DMA,
+                pltpu.SemaphoreType.DMA((PIECES,)),
             ],
             limit=MOST_VMEM_BYTES,
         )

time: 147 us -> 147 us (level)
  the two profiles are of different devices: /device:TPU:64 before, /device:TPU:10 now
where the time goes in v7:
time: 147 us; the launch traced here: 146 us
  starting transfers between devices  53.2 us (36%)
  waiting for transfers between devices  43.9 us (30%)
  blocking collectives  27.4 us (19%)
  Pallas kernels  13.9 us (9%)
  local copies, waits for them, and re-layouts  6.39 us (4%)
    all_to_all x4, starting transfers between devices, exchange(): return lax.all_to_all(parts, axis, 0, 0, axis_index_groups=groups)  33.3 us
    all_to_all x4, waiting for transfers between devices, exchange(): return lax.all_to_all(parts, axis, 0, 0, axis_index_groups=groups)  30.4 us
    all_to_all x1, blocking collectives, exchange(): return lax.all_to_all(parts, axis, 0, 0, axis_index_groups=groups)  27.4 us
    pallas_call x12, Pallas kernels, call(): pl.pallas_call(kernel, out_shape=outs[0] if one else outs, in_specs=[ANYW...  13.9 us
    ppermute x3, waiting for transfers between devices, swap_halves(): lax.ppermute(block, axis, [(at, (at + count // PAIR) % count) for at in r...  11.2 us
    ppermute x3, starting transfers between devices, swap_halves(): lax.ppermute(block, axis, [(at, (at + count // PAIR) % count) for at in r...  11.1 us
    ppermute x4, starting transfers between devices, swap_cores(): return lax.ppermute(block, 'col', [(at, at ^ 1) for at in range(cols)])  8.79 us
    unnamed x22, local copies, waits for them, and re-layouts  5.43 us
  transfers between devices with their start and end apart: 11, of which 9 were waited for; matrix products, arithmetic and copies ran while one was open for 0% of the time, Pallas kernels for 8%

profile of v7, /device:TPU:10, one launch (start us, length us, event | category | flops | bytes accessed | tf_op | source)
XLA Modules:
  0.0 146.3 jit_solution(8929038663728358852)
XLA Ops:
  0.6 0.8 pad_maximum_fusion
  1.4 0.0 copy-start
  1.4 1.0 broadcast_in_dim.2
  2.4 9.3 %all-to-all-start = ((bf16[16,32,768]{2,1,0:T(8,128)(2,1)}), bf16[16,32,768]{2,1,0:T(8,128)(2,1)S(1)}, u32[]{:S(2)}, u32[]{:S(2)}) async-start(bf16[16,32,768]{2,1,0:T(8,128)(2,1)} %broadcast_in_dim.2), calls=%async_computation | async-start | bytes 1572864 | tf_op jit(solution)/shard_map/all_to_all | solution.py:61
  11.6 0.0 copy-done
  11.6 1.9 %collective-permute-start = (bf16[768,768]{1,0:T(8,128)(2,1)S(1)}, bf16[768,768]{1,0:T(8,128)(2,1)S(1)}, u32[]{:S(2)}, u32[]{:S(2)}) collective-permute-start(bf16[768,768]{1,0:T(8,128)(2,1)S(1)} %copy-done), channel_id=1, source_target_pairs={{0,1},{1,0},{2,3},{3,2},{4,5},{5,4},{6,7},{7,6},{8,9},{9,8},{10,11... | collective-permute-start | bytes 3538952 | tf_op jit(solution)/shard_map/ppermute | solution.py:41
  13.5 2.4 %collective-permute-start.1 = (bf16[768,768]{1,0:T(8,128)(2,1)}, bf16[768,768]{1,0:T(8,128)(2,1)}, u32[]{:S(2)}, u32[]{:S(2)}) collective-permute-start(bf16[768,768]{1,0:T(8,128)(2,1)} %project.5), channel_id=1, source_target_pairs={{0,1},{1,0},{2,3},{3,2},{4,5},{5,4},{6,7},{7,6},{8,9},{9,8},{10,11... | collective-permute-start | bytes 3538952 | tf_op jit(solution)/shard_map/ppermute | solution.py:41
  16.0 0.4 collective-permute-done.expand_far
  16.4 15.1 %all-to-all-done.panels = bf16[16,32,768]{2,1,0:T(8,128)(2,1)S(1)} async-done(((bf16[16,32,768]{2,1,0:T(8,128)(2,1)}), bf16[16,32,768]{2,1,0:T(8,128)(2,1)S(1)}, u32[]{:S(2)}, u32[]{:S(2)}) %all-to-all-start) | async-done | bytes 786464 | tf_op jit(solution)/shard_map/all_to_all | solution.py:61
  31.4 0.0 copy-start.1
  31.4 0.8 shard_map.75
  32.3 0.0 copy-done.1
  32.3 0.0 copy-start.4
  32.3 0.9 copy-done.4
  33.2 12.0 %all-to-all-start.1 = ((bf16[16,32,768]{2,1,0:T(8,128)(2,1)}), bf16[16,32,768]{2,1,0:T(8,128)(2,1)S(1)}, u32[]{:S(2)}, u32[]{:S(2)}) async-start(bf16[16,32,768]{2,1,0:T(8,128)(2,1)} %copy-done.4), calls=%async_computation.1 | async-start | bytes 1572864 | tf_op jit(solution)/shard_map/all_to_all | solution.py:61
  45.2 0.0 collective-permute-done.1.project_far
  45.2 2.8 %shard_map.76 = bf16[8,32,768]{2,1,0:T(8,128)(2,1)} custom-call(bf16[16,32,768]{2,1,0:T(8,128)(2,1)} %copy-done.1, bf16[768,768]{1,0:T(8,128)(2,1)} %project.5, bf16[768,768]{1,0:T(8,128)(2,1)} %collective-permute-done.1.project_far), custom_call_target="tpu_custom_call" | custom-call | flops 1500000000 | bytes 3538944 | tf_op jit(solution)/shard_map/pallas_call | solution.py:92
  48.0 5.3 %collective-permute-start.2 = (bf16[8,32,768]{2,1,0:T(8,128)(2,1)}, bf16[8,32,768]{2,1,0:T(8,128)(2,1)S(1)}, u32[]{:S(2)}, u32[]{:S(2)}) collective-permute-start(bf16[8,32,768]{2,1,0:T(8,128)(2,1)} %shard_map.76), channel_id=1, source_target_pairs={{0,256},{32,288},{64,320},{96,352},{128,384},{160,416},{192,448},{... | collective-permute-start | bytes 1179656 | tf_op jit(solution)/shard_map/ppermute | solution.py:51
  53.3 2.9 %shard_map.77.mine = f32[8,32,768]{2,1,0:T(8,128)} custom-call(bf16[16,32,768]{2,1,0:T(8,128)(2,1)} %copy-done.1, bf16[768,768]{1,0:T(8,128)(2,1)} %project.5, bf16[768,768]{1,0:T(8,128)(2,1)} %collective-permute-done.1.project_far), custom_call_target="tpu_custom_call" | custom-call | flops 1500000000 | bytes 3932160 | tf_op jit(solution)/shard_map/pallas_call | solution.py:92
  56.2 9.9 %all-to-all-done.1.sums = bf16[16,32,768]{2,1,0:T(8,128)(2,1)S(1)} async-done(((bf16[16,32,768]{2,1,0:T(8,128)(2,1)}), bf16[16,32,768]{2,1,0:T(8,128)(2,1)S(1)}, u32[]{:S(2)}, u32[]{:S(2)}) %all-to-all-start.1) | async-done | bytes 786464 | tf_op jit(solution)/shard_map/all_to_all | solution.py:61
  66.1 0.0 copy-start.5
  66.1 0.2 shard_map.78
  66.3 0.1 collective-permute-done.2.came
  66.4 0.8 copy-done.5
  67.2 0.1 shard_map.79
  67.3 27.4 %all_to_all.25.mixed = bf16[8,64,768]{2,1,0:T(8,128)(2,1)S(1)} all-to-all(bf16[8,64,768]{2,1,0:T(8,128)(2,1)S(1)} %shard_map.79), channel_id=1, replica_groups={{0,32,64,96,128,160,192,224},{256,288,320,352,384,416,448,480},{1,33,65..., dimensions={0} | all-to-all | bytes 1572864 | tf_op jit(solution)/shard_map/all_to_all | solution.py:61
  94.7 0.1 shard_map.80
  94.8 0.0 copy-start.3
  94.8 0.9 copy-done.3
  95.7 2.7 %collective-permute-start.3 = (bf16[8,32,768]{2,1,0:T(8,128)(2,1)S(1)}, bf16[8,32,768]{2,1,0:T(8,128)(2,1)}, u32[]{:S(2)}, u32[]{:S(2)}) collective-permute-start(bf16[8,32,768]{2,1,0:T(8,128)(2,1)S(1)} %get-tuple-element.32.act), channel_id=1, source_target_pairs={{0,256},{32,288},{64,320},{96,352},{128,384},{160,416},{192,448},{... | collective-permute-start | bytes 1179656 | tf_op jit(solution)/shard_map/ppermute | solution.py:51
  98.4 4.2 %all-to-all-start.3 = ((bf16[16,32,768]{2,1,0:T(8,128)(2,1)}), bf16[16,32,768]{2,1,0:T(8,128)(2,1)S(1)}, u32[]{:S(2)}, u32[]{:S(2)}) async-start(bf16[16,32,768]{2,1,0:T(8,128)(2,1)} %copy-done.3), calls=%async_computation.3 | async-start | bytes 1572864 | tf_op jit(solution)/shard_map/all_to_all | solution.py:61
  102.5 6.0 %collective-permute-done.3.act_far = bf16[8,32,768]{2,1,0:T(8,128)(2,1)} collective-permute-done((bf16[8,32,768]{2,1,0:T(8,128)(2,1)S(1)}, bf16[8,32,768]{2,1,0:T(8,128)(2,1)}, u32[]{:S(2)}, u32[]{:S(2)}) %collective-permute-start.3) | collective-permute-done | bytes 393248 | tf_op jit(solution)/shard_map/ppermute | solution.py:51
  108.5 0.0 copy-start.6
  108.6 1.3 copy-done.6
  109.8 2.2 %shard_map.81 = (f32[16,8,768]{2,1,0:T(8,128)S(1)}, bf16[16,8,768]{2,1,0:T(8,128)(2,1)S(1)}, bf16[16,16,768]{2,1,0:T(8,128)(2,1)S(1)}, bf16[16,16,768]{2,1,0:T(8,128)(2,1)S(1)}) custom-call(bf16[8,32,768]{2,1,0:T(8,128)(2,1)S(1)} %get-tuple-element.32.act, bf16[8,32,768]{2,1,0:T(8,128)(2,1)} %collective-permute-done.3.act_far, ...), custom_call_target="tpu_custom_call" | custom-call | flops 60000002048 | bytes 4521984 | tf_op jit(solution)/shard_map/pallas_call | solution.py:92
  112.0 0.0 copy-start.7
  112.0 0.7 copy-done.7
  112.8 0.0 copy-start.9
  112.8 0.7 copy-done.9
  113.5 3.1 %collective-permute-start.4 = (bf16[16,8,768]{2,1,0:T(8,128)(2,1)S(1)}, bf16[16,8,768]{2,1,0:T(8,128)(2,1)S(1)}, u32[]{:S(2)}, u32[]{:S(2)}) collective-permute-start(bf16[16,8,768]{2,1,0:T(8,128)(2,1)S(1)} %get-tuple-element.34), channel_id=1, source_target_pairs={{0,16},{1,17},{2,18},{3,19},{4,20},{5,21},{6,22},{7,23},{8,24},{9,... | collective-permute-start | bytes 589832 | tf_op jit(solution)/shard_map/ppermute | solution.py:51
  116.6 5.1 %collective-permute-done.4.came = bf16[16,8,768]{2,1,0:T(8,128)(2,1)S(1)} collective-permute-done((bf16[16,8,768]{2,1,0:T(8,128)(2,1)S(1)}, bf16[16,8,768]{2,1,0:T(8,128)(2,1)S(1)}, u32[]{:S(2)}, u32[]{:S(2)}) %collective-permute-start.4) | collective-permute-done | bytes 196640 | tf_op jit(solution)/shard_map/ppermute | solution.py:51
  121.7 1.9 %all-to-all-done.3.grad = bf16[16,32,768]{2,1,0:T(8,128)(2,1)S(1)} async-done(((bf16[16,32,768]{2,1,0:T(8,128)(2,1)}), bf16[16,32,768]{2,1,0:T(8,128)(2,1)S(1)}, u32[]{:S(2)}, u32[]{:S(2)}) %all-to-all-start.3) | async-done | bytes 786464 | tf_op jit(solution)/shard_map/all_to_all | solution.py:61
  123.7 1.6 %shard_map.83 = bf16[16,24,768]{2,1,0:T(8,128)(2,1)} custom-call(bf16[16,32,768]{2,1,0:T(8,128)(2,1)S(1)} %all-to-all-done.3.grad, bf16[16,8,768]{2,1,0:T(8,128)(2,1)S(1)} %shard_map.82.layer, bf16[768,768]{1,0:T(8,128)(2,1)S(1)} %copy-done, bf16[768,768]{1,0:T(8,128)(2,1)S(1)} %collective-permute-done.expand_far), custom_call_target="tpu_custom_call" | custom-call | bytes 3932160 | tf_op jit(solution)/shard_map/pallas_call | solution.py:92
  125.3 0.0 copy-start.2
  125.3 0.0 copy-start.10
  125.3 7.9 %all-to-all-start.4 = ((bf16[16,24,768]{2,1,0:T(8,128)(2,1)}), bf16[16,24,768]{2,1,0:T(8,128)(2,1)S(1)}, u32[]{:S(2)}, u32[]{:S(2)}) async-start(bf16[16,24,768]{2,1,0:T(8,128)(2,1)} %shard_map.83), calls=%async_computation.4 | async-start | bytes 1179648 | tf_op jit(solution)/shard_map/all_to_all | solution.py:61
  133.2 0.0 copy-done.2
  133.2 1.9 %collective-permute-start.5 = (bf16[16,32,768]{2,1,0:T(8,128)(2,1)S(1)}, bf16[16,32,768]{2,1,0:T(8,128)(2,1)S(1)}, u32[]{:S(2)}, u32[]{:S(2)}) collective-permute-start(bf16[16,32,768]{2,1,0:T(8,128)(2,1)S(1)} %copy-done.2), channel_id=1, source_target_pairs={{0,1},{1,0},{2,3},{3,2},{4,5},{5,4},{6,7},{7,6},{8,9},{9,8},{10,11... | collective-permute-start | bytes 2359304 | tf_op jit(solution)/shard_map/ppermute | solution.py:41
  135.2 0.0 copy-done.10
  135.2 0.0 copy-start.8
  135.2 0.1 shard_map.84
  135.3 2.5 %collective-permute-start.6 = (bf16[2,16,16,768]{3,2,1,0:T(8,128)(2,1)S(1)}, bf16[2,16,16,768]{3,2,1,0:T(8,128)(2,1)S(1)}, u32[]{:S(2)}, u32[]{:S(2)}) collective-permute-start(bf16[2,16,16,768]{3,2,1,0:T(8,128)(2,1)S(1)} %get-tuple-element.40), channel_id=1, source_target_pairs={{0,1},{1,0},{2,3},{3,2},{4,5},{5,4},{6,7},{7,6},{8,9},{9,8},{10,11... | collective-permute-start | bytes 2359304 | tf_op jit(solution)/shard_map/ppermute | solution.py:41
  137.8 0.0 collective-permute-done.5.panels_far
  137.8 1.9 %collective-permute-done.6.got = bf16[2,16,16,768]{3,2,1,0:T(8,128)(2,1)S(1)} collective-permute-done((bf16[2,16,16,768]{3,2,1,0:T(8,128)(2,1)S(1)}, bf16[2,16,16,768]{3,2,1,0:T(8,128)(2,1)S(1)}, u32[]{:S(2)}, u32[]{:S(2)}) %collective-permute-start.6) | collective-permute-done | bytes 786464 | tf_op jit(solution)/shard_map/ppermute | solution.py:41
  139.7 0.0 copy-done.8
  139.7 2.4 %shard_map.85 = (bf16[768,768]{1,0:T(8,128)(2,1)}, bf16[768,768]{1,0:T(8,128)(2,1)}) custom-call(bf16[16,32,768]{2,1,0:T(8,128)(2,1)S(1)} %copy-done.2, bf16[16,32,768]{2,1,0:T(8,128)(2,1)S(1)} %collective-permute-done.5.panels_far, bf16[16,16,768]{2,1,0:T(8,128)(2,1)S(1)} %copy-done.8, bf16[16,16,768]{2,1,0:T(8,128)(2,1)S(1)} %get-tuple-element.39.grad, ...), custom_call_target="tpu_custom_call" | custom-call | flops 1200000000 | bytes 5505024 | tf_op jit(solution)/shard_map/pallas_call | solution.py:92
  142.1 3.5 %all-to-all-done.4.sums = bf16[16,24,768]{2,1,0:T(8,128)(2,1)S(1)} async-done(((bf16[16,24,768]{2,1,0:T(8,128)(2,1)}), bf16[16,24,768]{2,1,0:T(8,128)(2,1)S(1)}, u32[]{:S(2)}, u32[]{:S(2)}) %all-to-all-start.4) | async-done | bytes 589856 | tf_op jit(solution)/shard_map/all_to_all | solution.py:61
  145.7 0.7 shard_map.86
  (1 shorter events, 0.0 us)
Async XLA Ops:
  1.4 10.2 %copy-start = (bf16[768,768]{1,0:T(8,128)(2,1)S(1)}, bf16[768,768]{1,0:T(8,128)(2,1)}, u32[]{:S(2)}) copy-start(bf16[768,768]{1,0:T(8,128)(2,1)} %expand.3) | copy-start | bytes 3538948
  2.4 29.1 %all-to-all-start = ((bf16[16,32,768]{2,1,0:T(8,128)(2,1)}), bf16[16,32,768]{2,1,0:T(8,128)(2,1)S(1)}, u32[]{:S(2)}, u32[]{:S(2)}) async-start(bf16[16,32,768]{2,1,0:T(8,128)(2,1)} %broadcast_in_dim.2), calls=%async_computation | async-start | bytes 1572864 | tf_op jit(solution)/shard_map/all_to_all | solution.py:61
  11.6 4.7 %collective-permute-start = (bf16[768,768]{1,0:T(8,128)(2,1)S(1)}, bf16[768,768]{1,0:T(8,128)(2,1)S(1)}, u32[]{:S(2)}, u32[]{:S(2)}) collective-permute-start(bf16[768,768]{1,0:T(8,128)(2,1)S(1)} %copy-done), channel_id=1, source_target_pairs={{0,1},{1,0},{2,3},{3,2},{4,5},{5,4},{6,7},{7,6},{8,9},{9,8},{10,11... | collective-permute-start | bytes 3538952 | tf_op jit(solution)/shard_map/ppermute | solution.py:41
  13.5 31.6 %collective-permute-start.1 = (bf16[768,768]{1,0:T(8,128)(2,1)}, bf16[768,768]{1,0:T(8,128)(2,1)}, u32[]{:S(2)}, u32[]{:S(2)}) collective-permute-start(bf16[768,768]{1,0:T(8,128)(2,1)} %project.5), channel_id=1, source_target_pairs={{0,1},{1,0},{2,3},{3,2},{4,5},{5,4},{6,7},{7,6},{8,9},{9,8},{10,11... | collective-permute-start | bytes 3538952 | tf_op jit(solution)/shard_map/ppermute | solution.py:41
  31.4 0.9 copy-start.1
  32.3 0.9 copy-start.4
  33.2 32.9 %all-to-all-start.1 = ((bf16[16,32,768]{2,1,0:T(8,128)(2,1)}), bf16[16,32,768]{2,1,0:T(8,128)(2,1)S(1)}, u32[]{:S(2)}, u32[]{:S(2)}) async-start(bf16[16,32,768]{2,1,0:T(8,128)(2,1)} %copy-done.4), calls=%async_computation.1 | async-start | bytes 1572864 | tf_op jit(solution)/shard_map/all_to_all | solution.py:61
  48.0 18.4 %collective-permute-start.2 = (bf16[8,32,768]{2,1,0:T(8,128)(2,1)}, bf16[8,32,768]{2,1,0:T(8,128)(2,1)S(1)}, u32[]{:S(2)}, u32[]{:S(2)}) collective-permute-start(bf16[8,32,768]{2,1,0:T(8,128)(2,1)} %shard_map.76), channel_id=1, source_target_pairs={{0,256},{32,288},{64,320},{96,352},{128,384},{160,416},{192,448},{... | collective-permute-start | bytes 1179656 | tf_op jit(solution)/shard_map/ppermute | solution.py:51
  66.1 1.1 copy-start.5
  94.8 0.9 copy-start.3
  95.7 12.8 %collective-permute-start.3 = (bf16[8,32,768]{2,1,0:T(8,128)(2,1)S(1)}, bf16[8,32,768]{2,1,0:T(8,128)(2,1)}, u32[]{:S(2)}, u32[]{:S(2)}) collective-permute-start(bf16[8,32,768]{2,1,0:T(8,128)(2,1)S(1)} %get-tuple-element.32.act), channel_id=1, source_target_pairs={{0,256},{32,288},{64,320},{96,352},{128,384},{160,416},{192,448},{... | collective-permute-start | bytes 1179656 | tf_op jit(solution)/shard_map/ppermute | solution.py:51
  98.4 25.3 %all-to-all-start.3 = ((bf16[16,32,768]{2,1,0:T(8,128)(2,1)}), bf16[16,32,768]{2,1,0:T(8,128)(2,1)S(1)}, u32[]{:S(2)}, u32[]{:S(2)}) async-start(bf16[16,32,768]{2,1,0:T(8,128)(2,1)} %copy-done.3), calls=%async_computation.3 | async-start | bytes 1572864 | tf_op jit(solution)/shard_map/all_to_all | solution.py:61
  108.5 1.3 copy-start.6
  112.0 0.8 copy-start.7
  112.8 0.7 copy-start.9
  113.5 8.2 %collective-permute-start.4 = (bf16[16,8,768]{2,1,0:T(8,128)(2,1)S(1)}, bf16[16,8,768]{2,1,0:T(8,128)(2,1)S(1)}, u32[]{:S(2)}, u32[]{:S(2)}) collective-permute-start(bf16[16,8,768]{2,1,0:T(8,128)(2,1)S(1)} %get-tuple-element.34), channel_id=1, source_target_pairs={{0,16},{1,17},{2,18},{3,19},{4,20},{5,21},{6,22},{7,23},{8,24},{9,... | collective-permute-start | bytes 589832 | tf_op jit(solution)/shard_map/ppermute | solution.py:51
  125.3 7.9 %copy-start.2 = (bf16[16,32,768]{2,1,0:T(8,128)(2,1)S(1)}, bf16[16,32,768]{2,1,0:T(8,128)(2,1)}, u32[]{:S(2)}) copy-start(bf16[16,32,768]{2,1,0:T(8,128)(2,1)} %copy-done.1) | copy-start | bytes 2359300
  125.3 9.9 %copy-start.10 = (bf16[16,16,768]{2,1,0:T(8,128)(2,1)S(1)}, bf16[16,16,768]{2,1,0:T(8,128)(2,1)}, u32[]{:S(2)}) copy-start(bf16[16,16,768]{2,1,0:T(8,128)(2,1)} %copy-done.9) | copy-start | bytes 1179652
  125.3 20.3 %all-to-all-start.4 = ((bf16[16,24,768]{2,1,0:T(8,128)(2,1)}), bf16[16,24,768]{2,1,0:T(8,128)(2,1)S(1)}, u32[]{:S(2)}, u32[]{:S(2)}) async-start(bf16[16,24,768]{2,1,0:T(8,128)(2,1)} %shard_map.83), calls=%async_computation.4 | async-start | bytes 1179648 | tf_op jit(solution)/shard_map/all_to_all | solution.py:61
  133.2 4.6 %collective-permute-start.5 = (bf16[16,32,768]{2,1,0:T(8,128)(2,1)S(1)}, bf16[16,32,768]{2,1,0:T(8,128)(2,1)S(1)}, u32[]{:S(2)}, u32[]{:S(2)}) collective-permute-start(bf16[16,32,768]{2,1,0:T(8,128)(2,1)S(1)} %copy-done.2), channel_id=1, source_target_pairs={{0,1},{1,0},{2,3},{3,2},{4,5},{5,4},{6,7},{7,6},{8,9},{9,8},{10,11... | collective-permute-start | bytes 2359304 | tf_op jit(solution)/shard_map/ppermute | solution.py:41
  135.2 4.5 %copy-start.8 = (bf16[16,16,768]{2,1,0:T(8,128)(2,1)S(1)}, bf16[16,16,768]{2,1,0:T(8,128)(2,1)}, u32[]{:S(2)}) copy-start(bf16[16,16,768]{2,1,0:T(8,128)(2,1)} %copy-done.7) | copy-start | bytes 1179652
  135.3 4.4 %collective-permute-start.6 = (bf16[2,16,16,768]{3,2,1,0:T(8,128)(2,1)S(1)}, bf16[2,16,16,768]{3,2,1,0:T(8,128)(2,1)S(1)}, u32[]{:S(2)}, u32[]{:S(2)}) collective-permute-start(bf16[2,16,16,768]{3,2,1,0:T(8,128)(2,1)S(1)} %get-tuple-element.40), channel_id=1, source_target_pairs={{0,1},{1,0},{2,3},{3,2},{4,5},{5,4},{6,7},{7,6},{8,9},{9,8},{10,11... | collective-permute-start | bytes 2359304 | tf_op jit(solution)/shard_map/ppermute | solution.py:41
